TPU v7x, 32 devices: a whole 2x2x4 slice. The times are simulated.
32 devices in a mesh: box: 8 (over z, x), col: 4 (over y, core).
Axes of the slice: x: 2, y: 2, z: 4, core: 2. Of those that a mesh axis runs over, the one named last changes fastest.
Arguments:
- density: bfloat16 [1024, 16, 456], P('box'), may hold values from -6 to 6
- export_ids: int32 [8, 8, 4], P('box'), may hold values from -1 to 127, as said below
- list_slot: int32 [1024, 64], P('box'), may hold values from -1 to 31, as said below
- translations: bfloat16 [64, 456, 456], P('col'), may hold values from -0.046875 to 0.046875
- patch_points: int32 [64, 1024], P('box'), may hold values from 0 to 466943, as said below
- inverses: bfloat16 [64, 1024, 1024], P('box'), may hold values from -0.1875 to 0.1875
Outputs:
- field: bfloat16 [1024, 16, 456], P('box', 'col')
- corrected: bfloat16 [1024, 16, 456], P('box', 'col')
Inputs may be any that keep to these rules, and one draw needn't show every extreme that they name: export_ids[s, d, c] is one of device s's boxes (an index below 128 within s's boxes) or -1 for an empty slot; the boxes of one pair (s, d) are distinct; a device's slots from itself and from the devices just before and after it are all filled. list_slot[b, o] is -1 where box b has no translation o, else an import slot of b's device whose export entry is not -1. `patch_points`: a patch of device d's patches has distinct points within 8 consecutive boxes that begin no more than 2 boxes before d's first box and end no more than 2 boxes after its last.
All inputs are finite; a program needn't handle non-finite values.
Results may differ from a plain program's by a relative error of at most 0.0045.
Values may be sent and summed in bfloat16 or wider, within the bound.
No kernel may reach another device: no remote copies, remote signals or barrier semaphores. Data moves between devices by JAX's collectives and lax.ppermute only.
A program may use at most 128 MiB of HBM per device.

v0:
```python
import jax
import jax.numpy as jnp
from jax import lax
from jax.sharding import PartitionSpec as P

RIM = 2


def with_halo(block, sides, width):
    for axis, dim in sides:
        count = lax.axis_size(axis)
        forward = [(i, i + 1) for i in range(count - 1)]
        backward = [(target, source) for source, target in forward]
        low = lax.ppermute(
            lax.slice_in_dim(block, block.shape[dim] - width, None, axis=dim), axis, forward
        )
        high = lax.ppermute(lax.slice_in_dim(block, 0, width, axis=dim), axis, backward)
        block = jnp.concatenate([low, block, high], axis=dim)
    return block


def pick_boxes(columns_first, wanted):
    present = wanted >= 0
    chosen = jnp.take(columns_first, jnp.maximum(wanted, 0), axis=1)
    return jnp.where(present[None, :, None], chosen, jnp.zeros((), chosen.dtype))


def body(density, export_ids, list_slot, translations, patch_points, inverses):
    box_dev, total_cols, width = density.shape
    groups = lax.axis_size("col")
    share = total_cols // groups
    col_index = lax.axis_index("col")
    sources = export_ids.shape[1]
    capacity = export_ids.shape[2]
    wanted = export_ids[0].reshape(-1)
    columns_first = jnp.transpose(density, (1, 0, 2))
    own_group = lax.dynamic_slice_in_dim(columns_first, col_index * share, share, 0)
    outgoing = pick_boxes(own_group, wanted).reshape(share, sources, capacity, width)
    partial_import = lax.all_to_all(outgoing, "box", split_axis=1, concat_axis=1, tiled=True)
    imported = lax.all_gather(partial_import, "col", axis=0, tiled=True)
    imported = imported.reshape(total_cols, sources * capacity, width)
    local_ops = translations.shape[0]
    slot_columns = lax.dynamic_slice_in_dim(list_slot, col_index * local_ops, local_ops, 1).T
    column_block = imported

    def advance(totals, pieces):
        slot_row, operator = pieces
        live_rows = slot_row >= 0
        gathered = jnp.take(column_block, jnp.maximum(slot_row, 0), axis=1)
        gathered = jnp.where(live_rows[None, :, None], gathered, jnp.zeros((), gathered.dtype))
        term = jnp.dot(
            gathered.reshape(share * lax.axis_size("col") * box_dev, width),
            operator,
            preferred_element_type=jnp.float32,
        )
        return (totals + term.reshape(share * lax.axis_size("col"), box_dev, width), None)

    start_sum = jnp.zeros((share * lax.axis_size("col"), box_dev, width), jnp.float32)
    result, _ = lax.scan(advance, start_sum, (slot_columns, translations))
    field_sum = lax.psum_scatter(result, "col", scatter_dimension=0, tiled=True)
    field_cols = field_sum.astype(jnp.bfloat16)
    extended = with_halo(field_cols, (("box", 1),), RIM)
    flat_field = extended.reshape(share, -1)
    anchor = (lax.axis_index("box") * box_dev - RIM) * width
    local_points = (patch_points - anchor).reshape(-1)
    patch_count = patch_points.shape[0]
    patch_size = patch_points.shape[1]
    values = jnp.take(flat_field, local_points, axis=1).reshape(share, patch_count, patch_size)
    products = jnp.einsum(
        "cpi,pij->cpj", values, inverses, preferred_element_type=jnp.float32
    ).astype(jnp.bfloat16)
    spread = jnp.zeros((share, flat_field.shape[1]), jnp.float32)
    spread = spread.at[:, local_points].add(products.reshape(share, -1).astype(jnp.float32))
    spread = spread.reshape(share, box_dev + 2 * RIM, width)
    returned = with_halo(spread.astype(jnp.bfloat16), (("box", 1),), RIM).astype(spread.dtype)
    owned = spread[:, RIM : RIM + box_dev]
    owned = owned.at[:, :RIM].add(returned[:, :RIM])
    owned = owned.at[:, box_dev - RIM :].add(returned[:, returned.shape[1] - RIM :])
    corrected = (field_cols.astype(jnp.float32) + owned).astype(jnp.bfloat16)
    return (jnp.transpose(field_cols, (1, 0, 2)), jnp.transpose(corrected, (1, 0, 2)))


def solution(mesh):
    return jax.shard_map(
        body,
        mesh=mesh,
        in_specs=(
            P("box", None, None),
            P("box", None, None),
            P("box", None),
            P("col", None, None),
            P("box", None),
            P("box", None, None),
        ),
        out_specs=(P("box", "col", None), P("box", "col", None)),
        check_vma=False,
    )
```

profile of v0, /device:TPU:10, one launch (start us, length us, event | category | flops | bytes accessed | tf_op | source)
XLA Modules:
  0.0 436.9 jit_solution(2171252420765163630)
XLA Ops:
  30.0 159.8 %while.13 = (s32[]{:T(128)}, f32[16,128,456]{1,2,0:T(8,128)}, s32[16,128]{1,0:T(8,128)S(1)}, bf16[16,32,456]{2,0,1:T(8,128)(2,1)S(1)}, bf16[16,456,456]{2,1,0:T(8,128)(2,1)}, /*index=5*/s32[]{:T(128)}, s32[]{:T(128)}) while((s32[]{:T(128)}, f32[16,128,456]{1,2,0:T(8,128)}, s32[16,128]{1,0:T(8,128)S(1)}, ...), condition=%wide.region_1.2_spmd.clone, body=%wide.region_0.1_spmd.clone.sunk | while | flops 855442944 | bytes 17514080 | solution.py:59
  41.3 7.6 %select_add_fusion.2 = f32[16,128,456]{1,2,0:T(8,128)} fusion(f32[16,128,456]{1,2,0:T(8,128)} %get-tuple-element.153, bf16[16,128,456]{2,0,1:T(8,128)(2,1)} %select_bitcast_fusion.2, pred[]{:T(512)S(6)} %compare.14, bf16[16,456,456]{2,1,0:T(8,128)(2,1)} %get-tuple-element.163, s32[]{:T(128)} %get-tuple-element.152), kind=kOutput, calls=%fused_computation.4.clone.1 | convolution fusion | flops 853573632 | bytes 10035713 | tf_op jit(solution)/shard_map/while/body/eval_jaxpr/dot_general | solution.py:51
  51.4 7.6 %select_add_fusion.2 = f32[16,128,456]{1,2,0:T(8,128)} fusion(f32[16,128,456]{1,2,0:T(8,128)} %get-tuple-element.153, bf16[16,128,456]{2,0,1:T(8,128)(2,1)} %select_bitcast_fusion.2, pred[]{:T(512)S(6)} %compare.14, bf16[16,456,456]{2,1,0:T(8,128)(2,1)} %get-tuple-element.163, s32[]{:T(128)} %get-tuple-element.152), kind=kOutput, calls=%fused_computation.4.clone.1 | convolution fusion | flops 853573632 | bytes 10035713 | tf_op jit(solution)/shard_map/while/body/eval_jaxpr/dot_general | solution.py:51
  61.4 7.6 %select_add_fusion.2 = f32[16,128,456]{1,2,0:T(8,128)} fusion(f32[16,128,456]{1,2,0:T(8,128)} %get-tuple-element.153, bf16[16,128,456]{2,0,1:T(8,128)(2,1)} %select_bitcast_fusion.2, pred[]{:T(512)S(6)} %compare.14, bf16[16,456,456]{2,1,0:T(8,128)(2,1)} %get-tuple-element.163, s32[]{:T(128)} %get-tuple-element.152), kind=kOutput, calls=%fused_computation.4.clone.1 | convolution fusion | flops 853573632 | bytes 10035713 | tf_op jit(solution)/shard_map/while/body/eval_jaxpr/dot_general | solution.py:51
  71.5 7.6 %select_add_fusion.2 = f32[16,128,456]{1,2,0:T(8,128)} fusion(f32[16,128,456]{1,2,0:T(8,128)} %get-tuple-element.153, bf16[16,128,456]{2,0,1:T(8,128)(2,1)} %select_bitcast_fusion.2, pred[]{:T(512)S(6)} %compare.14, bf16[16,456,456]{2,1,0:T(8,128)(2,1)} %get-tuple-element.163, s32[]{:T(128)} %get-tuple-element.152), kind=kOutput, calls=%fused_computation.4.clone.1 | convolution fusion | flops 853573632 | bytes 10035713 | tf_op jit(solution)/shard_map/while/body/eval_jaxpr/dot_general | solution.py:51
  81.6 7.6 %select_add_fusion.2 = f32[16,128,456]{1,2,0:T(8,128)} fusion(f32[16,128,456]{1,2,0:T(8,128)} %get-tuple-element.153, bf16[16,128,456]{2,0,1:T(8,128)(2,1)} %select_bitcast_fusion.2, pred[]{:T(512)S(6)} %compare.14, bf16[16,456,456]{2,1,0:T(8,128)(2,1)} %get-tuple-element.163, s32[]{:T(128)} %get-tuple-element.152), kind=kOutput, calls=%fused_computation.4.clone.1 | convolution fusion | flops 853573632 | bytes 10035713 | tf_op jit(solution)/shard_map/while/body/eval_jaxpr/dot_general | solution.py:51
  91.6 7.6 %select_add_fusion.2 = f32[16,128,456]{1,2,0:T(8,128)} fusion(f32[16,128,456]{1,2,0:T(8,128)} %get-tuple-element.153, bf16[16,128,456]{2,0,1:T(8,128)(2,1)} %select_bitcast_fusion.2, pred[]{:T(512)S(6)} %compare.14, bf16[16,456,456]{2,1,0:T(8,128)(2,1)} %get-tuple-element.163, s32[]{:T(128)} %get-tuple-element.152), kind=kOutput, calls=%fused_computation.4.clone.1 | convolution fusion | flops 853573632 | bytes 10035713 | tf_op jit(solution)/shard_map/while/body/eval_jaxpr/dot_general | solution.py:51
  101.7 7.6 %select_add_fusion.2 = f32[16,128,456]{1,2,0:T(8,128)} fusion(f32[16,128,456]{1,2,0:T(8,128)} %get-tuple-element.153, bf16[16,128,456]{2,0,1:T(8,128)(2,1)} %select_bitcast_fusion.2, pred[]{:T(512)S(6)} %compare.14, bf16[16,456,456]{2,1,0:T(8,128)(2,1)} %get-tuple-element.163, s32[]{:T(128)} %get-tuple-element.152), kind=kOutput, calls=%fused_computation.4.clone.1 | convolution fusion | flops 853573632 | bytes 10035713 | tf_op jit(solution)/shard_map/while/body/eval_jaxpr/dot_general | solution.py:51
  111.7 7.6 %select_add_fusion.2 = f32[16,128,456]{1,2,0:T(8,128)} fusion(f32[16,128,456]{1,2,0:T(8,128)} %get-tuple-element.153, bf16[16,128,456]{2,0,1:T(8,128)(2,1)} %select_bitcast_fusion.2, pred[]{:T(512)S(6)} %compare.14, bf16[16,456,456]{2,1,0:T(8,128)(2,1)} %get-tuple-element.163, s32[]{:T(128)} %get-tuple-element.152), kind=kOutput, calls=%fused_computation.4.clone.1 | convolution fusion | flops 853573632 | bytes 10035713 | tf_op jit(solution)/shard_map/while/body/eval_jaxpr/dot_general | solution.py:51
  121.8 7.6 %select_add_fusion.2 = f32[16,128,456]{1,2,0:T(8,128)} fusion(f32[16,128,456]{1,2,0:T(8,128)} %get-tuple-element.153, bf16[16,128,456]{2,0,1:T(8,128)(2,1)} %select_bitcast_fusion.2, pred[]{:T(512)S(6)} %compare.14, bf16[16,456,456]{2,1,0:T(8,128)(2,1)} %get-tuple-element.163, s32[]{:T(128)} %get-tuple-element.152), kind=kOutput, calls=%fused_computation.4.clone.1 | convolution fusion | flops 853573632 | bytes 10035713 | tf_op jit(solution)/shard_map/while/body/eval_jaxpr/dot_general | solution.py:51
  131.9 7.6 %select_add_fusion.2 = f32[16,128,456]{1,2,0:T(8,128)} fusion(f32[16,128,456]{1,2,0:T(8,128)} %get-tuple-element.153, bf16[16,128,456]{2,0,1:T(8,128)(2,1)} %select_bitcast_fusion.2, pred[]{:T(512)S(6)} %compare.14, bf16[16,456,456]{2,1,0:T(8,128)(2,1)} %get-tuple-element.163, s32[]{:T(128)} %get-tuple-element.152), kind=kOutput, calls=%fused_computation.4.clone.1 | convolution fusion | flops 853573632 | bytes 10035713 | tf_op jit(solution)/shard_map/while/body/eval_jaxpr/dot_general | solution.py:51
  141.9 7.6 %select_add_fusion.2 = f32[16,128,456]{1,2,0:T(8,128)} fusion(f32[16,128,456]{1,2,0:T(8,128)} %get-tuple-element.153, bf16[16,128,456]{2,0,1:T(8,128)(2,1)} %select_bitcast_fusion.2, pred[]{:T(512)S(6)} %compare.14, bf16[16,456,456]{2,1,0:T(8,128)(2,1)} %get-tuple-element.163, s32[]{:T(128)} %get-tuple-element.152), kind=kOutput, calls=%fused_computation.4.clone.1 | convolution fusion | flops 853573632 | bytes 10035713 | tf_op jit(solution)/shard_map/while/body/eval_jaxpr/dot_general | solution.py:51
  152.0 7.6 %select_add_fusion.2 = f32[16,128,456]{1,2,0:T(8,128)} fusion(f32[16,128,456]{1,2,0:T(8,128)} %get-tuple-element.153, bf16[16,128,456]{2,0,1:T(8,128)(2,1)} %select_bitcast_fusion.2, pred[]{:T(512)S(6)} %compare.14, bf16[16,456,456]{2,1,0:T(8,128)(2,1)} %get-tuple-element.163, s32[]{:T(128)} %get-tuple-element.152), kind=kOutput, calls=%fused_computation.4.clone.1 | convolution fusion | flops 853573632 | bytes 10035713 | tf_op jit(solution)/shard_map/while/body/eval_jaxpr/dot_general | solution.py:51
  162.0 7.6 %select_add_fusion.2 = f32[16,128,456]{1,2,0:T(8,128)} fusion(f32[16,128,456]{1,2,0:T(8,128)} %get-tuple-element.153, bf16[16,128,456]{2,0,1:T(8,128)(2,1)} %select_bitcast_fusion.2, pred[]{:T(512)S(6)} %compare.14, bf16[16,456,456]{2,1,0:T(8,128)(2,1)} %get-tuple-element.163, s32[]{:T(128)} %get-tuple-element.152), kind=kOutput, calls=%fused_computation.4.clone.1 | convolution fusion | flops 853573632 | bytes 10035713 | tf_op jit(solution)/shard_map/while/body/eval_jaxpr/dot_general | solution.py:51
  172.1 7.6 %select_add_fusion.2 = f32[16,128,456]{1,2,0:T(8,128)} fusion(f32[16,128,456]{1,2,0:T(8,128)} %get-tuple-element.153, bf16[16,128,456]{2,0,1:T(8,128)(2,1)} %select_bitcast_fusion.2, pred[]{:T(512)S(6)} %compare.14, bf16[16,456,456]{2,1,0:T(8,128)(2,1)} %get-tuple-element.163, s32[]{:T(128)} %get-tuple-element.152), kind=kOutput, calls=%fused_computation.4.clone.1 | convolution fusion | flops 853573632 | bytes 10035713 | tf_op jit(solution)/shard_map/while/body/eval_jaxpr/dot_general | solution.py:51
  182.2 7.6 %select_add_fusion.2 = f32[16,128,456]{1,2,0:T(8,128)} fusion(f32[16,128,456]{1,2,0:T(8,128)} %get-tuple-element.153, bf16[16,128,456]{2,0,1:T(8,128)(2,1)} %select_bitcast_fusion.2, pred[]{:T(512)S(6)} %compare.14, bf16[16,456,456]{2,1,0:T(8,128)(2,1)} %get-tuple-element.163, s32[]{:T(128)} %get-tuple-element.152), kind=kOutput, calls=%fused_computation.4.clone.1 | convolution fusion | flops 853573632 | bytes 10035713 | tf_op jit(solution)/shard_map/while/body/eval_jaxpr/dot_general | solution.py:51
  190.6 39.8 %reduce-scatter.2.cloned.1.call-done = f32[4,128,456]{1,2,0:T(8,128)} async-done(((f32[16,128,456]{1,2,0:T(8,128)}), f32[4,128,456]{1,2,0:T(8,128)}) %reduce-scatter.2.cloned.1.call-update) | async-done | bytes 933904 | tf_op jit(solution)/shard_map/reduce_scatter | solution.py:60
  237.9 18.3 %collective-permute-done = bf16[4,2,456]{1,2,0:T(8,128)(2,1)S(1)} collective-permute-done((bf16[4,2,456]{1,2,0:T(8,128)(2,1)S(1)}, bf16[4,2,456]{1,2,0:T(8,128)(2,1)S(1)}, u32[]{:S(2)}, u32[]{:S(2)}) %collective-permute-start) | collective-permute-done | bytes 7328 | tf_op jit(solution)/shard_map/ppermute | solution.py:14
  256.8 13.8 %copy.52 = bf16[4,132,456]{0,2,1:T(8,128)(2,1)} copy(bf16[4,132,456]{1,2,0:T(8,128)(2,1)S(1)} %pad_maximum_fusion) | data formatting | bytes 963072 | tf_op jit(solution)/shard_map/concatenate | solution.py:18
  270.5 29.3 %gather_fusion.2 = bf16[8192,4]{1,0:T(8,128)(2,1)S(1)} fusion(bf16[4,60192]{0,1:T(8,128)(2,1)} %bitcast.55, s32[8192]{0:T(1024)S(1)} %broadcast_clamp_fusion), kind=kCustom, calls=%fused_computation.2 | custom fusion | bytes 163840 | tf_op jit(solution)/shard_map/jit(_take)/gather | solution.py:68
  300.7 8.0 %fusion.9 = f32[8,4,1024]{2,1,0:T(4,128)S(1)} fusion(bf16[8,1024,1024]{2,1,0:T(8,128)(2,1)} %param.17, bf16[4,8,1024]{2,0,1:T(4,128)(2,1)S(1)} %copy.53, pred[8,1024]{1,0:T(8,128)(4,1)S(1)} %compare_and_fusion), kind=kOutput, calls=%fused_computation.19 | convolution fusion | flops 67207168 | bytes 16982016 | tf_op jit(solution)/shard_map/cpi,pij->cpj/dot_general | solution.py:69
  311.4 56.4 %scatter_custom_fusion = f32[4,60192]{0,1:T(8,128)} fusion(s32[8192]{0:T(1024)S(1)} %bitcast.61, f32[8192,4]{1,0:T(8,128)} %copy.54, f32[]{:T(128)} %constant.128.clone.1), kind=kCustom, calls=%fused_computation.16 | custom fusion | flops 32768 | bytes 963584 | tf_op jit(solution)/shard_map/scatter-add | solution.py:73
  367.8 21.7 %copy.55 = f32[4,132,456]{1,2,0:T(8,128)S(1)} copy(f32[4,132,456]{0,2,1:T(8,128)} %bitcast.54) | data formatting | bytes 1926144 | tf_op jit(solution)/shard_map/reshape | solution.py:74
  398.1 15.9 %collective-permute-done.2 = bf16[4,2,456]{1,2,0:T(8,128)(2,1)S(1)} collective-permute-done((bf16[4,2,456]{1,2,0:T(8,128)(2,1)S(1)}, bf16[4,2,456]{1,2,0:T(8,128)(2,1)S(1)}, u32[]{:S(2)}, u32[]{:S(2)}) %collective-permute-start.2) | collective-permute-done | bytes 7328 | tf_op jit(solution)/shard_map/ppermute | solution.py:14
  (137 shorter events, 105.4 us)
Async XLA Ops:
  7.2 1.5 copy-start
  11.0 11.4 %all-to-all-start = ((bf16[4,8,4,456]{3,0,2,1:T(4,128)(2,1)}), bf16[4,8,4,456]{3,0,2,1:T(4,128)(2,1)S(1)}, u32[]{:S(2)}, u32[]{:S(2)}) async-start(bf16[4,8,4,456]{3,0,2,1:T(4,128)(2,1)} %select_select_fusion), calls=%async_computation | async-start | bytes 262144 | tf_op jit(solution)/shard_map/all_to_all | solution.py:39
  17.2 213.2 %reduce-scatter.2.cloned.1.call-start = ((), (), s32[]{:S(2)}) async-start(), calls=%async_computation.2 | async-start | bytes 4669440 | tf_op jit(solution)/shard_map/reduce_scatter | solution.py:60
  189.7 0.8 copy-start.4
  231.9 24.3 %collective-permute-start = (bf16[4,2,456]{1,2,0:T(8,128)(2,1)S(1)}, bf16[4,2,456]{1,2,0:T(8,128)(2,1)S(1)}, u32[]{:S(2)}, u32[]{:S(2)}) collective-permute-start(bf16[4,2,456]{1,2,0:T(8,128)(2,1)S(1)} %get-tuple-element.106), channel_id=1, source_target_pairs={{0,4},{4,8},{8,12},{12,16},{16,20},{20,24},{24,28},{1,5},{5,9},{9,... | collective-permute-start | bytes 21896 | tf_op jit(solution)/shard_map/ppermute | solution.py:14
  235.2 20.9 %collective-permute-start.1 = (bf16[4,2,456]{1,2,0:T(8,128)(2,1)S(1)}, bf16[4,2,456]{1,2,0:T(8,128)(2,1)S(1)}, u32[]{:S(2)}, u32[]{:S(2)}) collective-permute-start(bf16[4,2,456]{1,2,0:T(8,128)(2,1)S(1)} %get-tuple-element.107), channel_id=1, source_target_pairs={{4,0},{8,4},{12,8},{16,12},{20,16},{24,20},{28,24},{5,1},{9,5},{13... | collective-permute-start | bytes 21896 | tf_op jit(solution)/shard_map/ppermute | solution.py:17
  389.4 6.5 %copy-start.2 = (f32[4,128,456]{1,2,0:T(8,128)S(1)}, f32[4,128,456]{1,2,0:T(8,128)}, u32[]{:S(2)}) copy-start(f32[4,128,456]{1,2,0:T(8,128)} %reduce-scatter.2.cloned.1.call-done) | copy-start | bytes 2801668
  389.8 24.2 %collective-permute-start.2 = (bf16[4,2,456]{1,2,0:T(8,128)(2,1)S(1)}, bf16[4,2,456]{1,2,0:T(8,128)(2,1)S(1)}, u32[]{:S(2)}, u32[]{:S(2)}) collective-permute-start(bf16[4,2,456]{1,2,0:T(8,128)(2,1)S(1)} %get-tuple-element.104), channel_id=1, source_target_pairs={{0,4},{4,8},{8,12},{12,16},{16,20},{20,24},{24,28},{1,5},{5,9},{9,... | collective-permute-start | bytes 21896 | tf_op jit(solution)/shard_map/ppermute | solution.py:14
  394.1 20.1 %collective-permute-start.3 = (bf16[4,2,456]{1,2,0:T(8,128)(2,1)S(1)}, bf16[4,2,456]{1,2,0:T(8,128)(2,1)S(1)}, u32[]{:S(2)}, u32[]{:S(2)}) collective-permute-start(bf16[4,2,456]{1,2,0:T(8,128)(2,1)S(1)} %get-tuple-element.105), channel_id=1, source_target_pairs={{4,0},{8,4},{12,8},{16,12},{20,16},{24,20},{28,24},{5,1},{9,5},{13... | collective-permute-start | bytes 21896 | tf_op jit(solution)/shard_map/ppermute | solution.py:17
  414.8 1.3 copy-start.3
  420.7 9.3 %copy-start.1 = (bf16[128,16,456]{0,2,1:T(8,128)(2,1)S(1)}, bf16[128,16,456]{0,2,1:T(8,128)(2,1)}, u32[]{:S(2)}) copy-start(bf16[128,16,456]{0,2,1:T(8,128)(2,1)} %param.12) | copy-start | bytes 5603332
Sparse Core Ops, SparseCore 0:
  189.9 40.4 reduce-scatter.1
where the time goes:
time: 440 us; the launch traced here: 437 us
  matrix products  128 us (29%)
  other arithmetic  96.9 us (22%)
  local copies, waits for them, and re-layouts  92.9 us (21%)
  waiting for transfers between devices  78.6 us (18%)
  starting transfers between devices  18.4 us (4%)
  between operations  14.2 us (3%)
  blocking collectives  7.2 us (2%)
    dot_general x16, matrix products, advance(): jnp.dot(gathered.reshape(share * lax.axis_size('col') * box_dev, width),...  120 us
    scatter-add x1, other arithmetic, body(): spread.at[:, local_points]  56.4 us
    reduce_scatter x1, waiting for transfers between devices, body(): field_sum = lax.psum_scatter(result, 'col', scatter_dimension=0, tiled=True)  39.8 us
    ppermute x2, waiting for transfers between devices, with_halo(): lax.ppermute(lax.slice_in_dim(block, block.shape[dim] - width, None, axis...  34.2 us
    gather x2, local copies, waits for them, and re-layouts, body(): jnp.take(flat_field, local_points, axis=1)  30.2 us
    select_n x16, other arithmetic, advance(): jnp.where(live_rows[None, :, None], gathered, jnp.zeros((), gathered.dtype))  27.9 us
    reshape x1, local copies, waits for them, and re-layouts, body(): spread = spread.reshape(share, box_dev + 2 * RIM, width)  21.7 us
    concatenate x1, local copies, waits for them, and re-layouts, with_halo(): block = jnp.concatenate([low, block, high], axis=dim)  13.8 us
  transfers between devices with their start and end apart: 6, of which 5 were waited for; matrix products, arithmetic and copies ran while one was open for 1% of the time, Pallas kernels for 0%

commit v1 on v0

v1 whole, which is shorter than its diff:
```python
import functools

import jax
import jax.numpy as jnp
from jax import lax
from jax.experimental import pallas as pl
from jax.experimental.pallas import tpu as pltpu
from jax.sharding import PartitionSpec as P

RIM = 2
SPAN = 8
LANES = 128
NT = (((1,), (1,)), ((), ()))
ANY = pl.BlockSpec(memory_space=pl.ANY)
VMEM = pl.BlockSpec(memory_space=pltpu.VMEM)
SMEM = pl.BlockSpec(memory_space=pltpu.SMEM)


def round_up(n, m):
    return -(-n // m) * m


def params(limit):
    return pltpu.CompilerParams(vmem_limit_bytes=limit << 20)


def iota(shape, dim):
    return lax.broadcasted_iota(jnp.int32, shape, dim)


def div(x, n):
    if n & (n - 1) == 0:
        return x >> (n.bit_length() - 1)
    return lax.div(x, jnp.int32(n))


def mod(x, n):
    if n & (n - 1) == 0:
        return x & (n - 1)
    return lax.rem(x, jnp.int32(n))


def pick_kernel(share, groups_ref, ids_ref, density_ref, out_ref, block, sems):
    capacity, dests = ids_ref.shape
    cols, width, boxes = block.shape
    copies = []
    for j in range(cols // share):
        copy = pltpu.make_async_copy(
            density_ref.at[pl.ds(groups_ref[j] * share, share)],
            block.at[pl.ds(j * share, share)],
            sems.at[j],
        )
        copy.start()
        copies.append(copy)
    rows = dests * cols * capacity
    row = iota((rows, boxes), 0)
    pair = div(row, cols * capacity) * capacity + mod(row, capacity)
    column = mod(div(row, capacity), cols)

    def place(k, wanted):
        return jnp.where(pair == k, ids_ref[mod(k, capacity), div(k, capacity)], wanted)

    wanted = jnp.full((rows, boxes), -1, jnp.int32)
    if dests * capacity <= 64:
        for k in range(dests * capacity):
            wanted = place(jnp.int32(k), wanted)
    else:
        wanted = lax.fori_loop(0, dests * capacity, place, wanted)
    hit = wanted == iota((rows, boxes), 1)
    for copy in copies:
        copy.wait()
    total = jnp.zeros((rows, width), jnp.float32)
    for c in range(cols):
        chosen = jnp.where(hit & (column == c), 1.0, 0.0).astype(jnp.bfloat16)
        total = total + lax.dot_general(
            chosen, block[c], NT, preferred_element_type=jnp.float32
        )
    out_ref[...] = total.astype(out_ref.dtype).reshape(out_ref.shape)


def field_kernel(
    share, capacity, group, ops_at_ref, imported_ref, slots_ref, *rest
):
    operator_refs, (out_ref, edge_ref, weights, terms, hot, sems) = rest[:-6], rest[-6:]
    sources, per_source, width = imported_ref.shape
    local_ops = operator_refs[0].shape[0]
    boxes = slots_ref.shape[1]
    slots = sources * capacity
    stride = terms.shape[1] // share
    chunk = local_ops
    for size in (4, 2, 1):
        if local_ops % size == 0:
            chunk = size
            break
    copies = []
    for half, ref in enumerate(operator_refs):
        for at in range(0, local_ops, chunk):
            copy = pltpu.make_async_copy(
                ref.at[pl.ds(at, chunk)],
                weights.at[pl.ds(half * local_ops + at, chunk)],
                sems.at[len(copies)],
            )
            copy.start()
            copies.append(copy)
    arrived = sources * per_source
    shape = (share * slots, arrived)
    row = iota(shape, 0)
    slot = mod(row, slots)
    origin = (
        div(slot, capacity) * per_source
        + (group * share + div(row, slots)) * capacity
        + mod(slot, capacity)
    )
    order = jnp.where(origin == iota(shape, 1), 1.0, 0.0).astype(jnp.bfloat16)
    flat = imported_ref[...].reshape(arrived, width)
    ordered = jnp.dot(order, flat, preferred_element_type=jnp.float32).astype(jnp.bfloat16)
    for half in range(len(operator_refs)):
        wanted = slots_ref[pl.ds(ops_at_ref[half], local_ops), :]
        for o in range(local_ops):
            picked = iota((slots, boxes), 0) == wanted[o : o + 1, :]
            at = (half * local_ops + o) * slots
            hot[at : at + slots, :] = jnp.where(picked, 1.0, 0.0).astype(jnp.bfloat16)
    picks = hot[...].T
    for i, copy in enumerate(copies):
        copy.wait()
        for o in range(i * chunk, (i + 1) * chunk):
            term = jnp.dot(ordered, weights[o], preferred_element_type=jnp.float32)
            term = term.astype(jnp.bfloat16)
            for c in range(share):
                terms[o * slots : (o + 1) * slots, c * stride : c * stride + width] = term[
                    c * slots : (c + 1) * slots
                ]
    total = jnp.dot(picks, terms[...], preferred_element_type=jnp.float32)
    tiles = stride // LANES
    for c in range(share):
        out_ref[c] = total[:, c * stride : (c + 1) * stride].astype(out_ref.dtype)
    for c in range(share):
        for t in range(tiles):
            part = total[:, (c * tiles + t) * LANES : (c * tiles + t + 1) * LANES]
            for b in range(RIM):
                at = (b * share + c) * tiles + t
                edge_ref[0, at : at + 1, :] = part[b : b + 1]
                edge_ref[1, at : at + 1, :] = part[boxes - RIM + b : boxes - RIM + b + 1]


def field_call(imported, slots_t, operators, ops_at, share, capacity, group, dtype):
    sources = imported.shape[0]
    width = imported.shape[2]
    boxes = slots_t.shape[1]
    slots = sources * capacity
    all_ops = sum(o.shape[0] for o in operators)
    stride = round_up(width, LANES)
    return pl.pallas_call(
        functools.partial(field_kernel, share, capacity, group),
        out_shape=[
            jax.ShapeDtypeStruct((share, boxes, stride), dtype),
            jax.ShapeDtypeStruct((2, RIM * share * (stride // LANES), LANES), jnp.float32),
        ],
        in_specs=[SMEM, VMEM, VMEM] + [ANY] * len(operators),
        out_specs=[VMEM, VMEM],
        scratch_shapes=[
            pltpu.VMEM((all_ops, width, width), jnp.bfloat16),
            pltpu.VMEM((all_ops * slots, share * stride), jnp.bfloat16),
            pltpu.VMEM((all_ops * slots, boxes), jnp.bfloat16),
            pltpu.SemaphoreType.DMA((all_ops,)),
        ],
        compiler_params=params(56),
        cost_estimate=pl.CostEstimate(
            flops=2 * all_ops * share * slots * width * (width + boxes),
            bytes_accessed=all_ops * width * stride * 2,
            transcendentals=0,
        ),
    )(ops_at, imported, slots_t, *operators)


def patch_kernel(
    info_ref, starts_ref, code_ref, lane_ref, own_ref, received_ref, low_ref, high_ref,
    inverses_ref, field_ref, corrected_ref, side_ref, rows_ref, ext, spread, values, blocks, sems,
):
    share, boxes, stride = own_ref.shape
    width = field_ref.shape[1]
    patches, points = code_ref.shape
    tiles = stride // LANES
    per_box = share * tiles
    window = SPAN * per_box
    rim = RIM * per_box
    copies = []
    for p in range(patches):
        copy = pltpu.make_async_copy(inverses_ref.at[p], blocks.at[p], sems.at[p])
        copy.start()
        copies.append(copy)
    spread[...] = jnp.zeros_like(spread)
    ext[:rim, :] = low_ref[...]
    ext[rim + boxes * per_box :, :] = high_ref[...]
    for c in range(share):
        for t in range(tiles):
            part = own_ref[c, :, t * LANES : (t + 1) * LANES]
            for r in range(received_ref.shape[0]):
                part = part + received_ref[r, c, :, t * LANES : (t + 1) * LANES].astype(jnp.float32)
            part = part.astype(jnp.bfloat16).astype(jnp.float32)
            ext[pl.ds(rim + c * tiles + t, boxes, stride=per_box), :] = part
            last = min(width - t * LANES, LANES)
            field_ref[c, t * LANES : t * LANES + last, :] = part.T[:last].astype(field_ref.dtype)
    row = iota((window, LANES), 0)
    row_code = div(row, per_box) * tiles + mod(row, tiles)
    for p in range(patches):
        held = ext[pl.ds(pl.multiple_of(starts_ref[p] * per_box, 8), window), :]
        for at in range(0, points, LANES):
            code = code_ref[p : p + 1, at : at + LANES]
            lane = jnp.broadcast_to(lane_ref[p : p + 1, at : at + LANES], (window, LANES))
            found = jnp.take_along_axis(held, lane, axis=1)
            found = jnp.where(row_code == code, found, 0.0)
            found = jnp.sum(found.reshape(SPAN, per_box, LANES), axis=0)
            values[p, :, at : at + LANES] = jnp.sum(found.reshape(share, tiles, LANES), axis=1)
    row = iota((window, points), 0)
    row_code = div(row, per_box) * tiles + mod(row, tiles)
    for p in range(patches):
        copies[p].wait()
        product = jnp.dot(
            values[p].astype(jnp.bfloat16), blocks[p], preferred_element_type=jnp.float32
        )
        product = product.astype(jnp.bfloat16).astype(jnp.float32)
        product = jnp.concatenate(
            [jnp.broadcast_to(product[c : c + 1], (tiles, points)) for c in range(share)], axis=0
        )
        product = jnp.concatenate([product] * SPAN, axis=0)
        left = jnp.where(row_code == code_ref[p : p + 1, :], product, 0.0).astype(jnp.bfloat16)
        right = jnp.where(iota((LANES, points), 0) == lane_ref[p : p + 1, :], 1.0, 0.0)
        placed = lax.dot_general(
            left, right.astype(jnp.bfloat16), NT, preferred_element_type=jnp.float32
        )
        at = pl.ds(pl.multiple_of(starts_ref[p] * per_box, 8), window)
        spread[at, :] = spread[at, :] + placed
    for c in range(share):
        for t in range(tiles):
            at = pl.ds(rim + c * tiles + t, boxes, stride=per_box)
            total = ext[at, :] + spread[at, :]
            last = min(width - t * LANES, LANES)
            corrected_ref[c, t * LANES : t * LANES + last, :] = total.T[:last].astype(
                corrected_ref.dtype
            )
    end = rim + boxes * per_box
    rows_ref[0] = ext[rim : 2 * rim, :] + spread[rim : 2 * rim, :]
    rows_ref[1] = ext[end - rim : end, :] + spread[end - rim : end, :]
    even = info_ref[0] == 0
    low = spread[:rim, :]
    high = spread[end:, :]
    side_ref[0] = jnp.where(even, high, low)
    side_ref[1] = jnp.where(even, low, high)


def finish_kernel(info_ref, first_ref, second_ref, rows_ref, corrected_ref, out_ref, tall):
    share, width, boxes = corrected_ref.shape
    per_box = rows_ref.shape[1] // RIM
    tiles = per_box // share
    even = info_ref[0] == 0
    first = first_ref[...]
    second = second_ref[...]
    low = rows_ref[0] + jnp.where(even, second, first)
    high = rows_ref[1] + jnp.where(even, first, second)
    tall[...] = jnp.zeros_like(tall)
    for c in range(share):
        for t in range(tiles):
            for b in range(RIM):
                at = b * per_box + c * tiles + t
                tall[b : b + 1, :] = low[at : at + 1]
                tall[boxes - RIM + b : boxes - RIM + b + 1, :] = high[at : at + 1]
            turned = tall[...].T
            last = min(width - t * LANES, LANES)
            box = iota((last, boxes), 1)
            edge = (box < RIM) | (box >= boxes - RIM)
            kept = corrected_ref[c, t * LANES : t * LANES + last, :].astype(jnp.float32)
            out_ref[c, t * LANES : t * LANES + last, :] = jnp.where(
                edge, turned[:last], kept
            ).astype(out_ref.dtype)


def swap_sides(first, second, axis):
    count = lax.axis_size(axis)
    evens = [(i, i + 1) for i in range(0, count - 1, 2)]
    odds = [(i, i + 1) for i in range(1, count - 1, 2)]
    evens += [(b, a) for a, b in evens]
    odds += [(b, a) for a, b in odds]
    return lax.ppermute(first, axis, evens), lax.ppermute(second, axis, odds)


def body(density, export_ids, list_slot, translations, patch_points, inverses):
    boxes, total_cols, width = density.shape
    groups = lax.axis_size("col")
    share = total_cols // groups
    capacity = export_ids.shape[2]
    sources = export_ids.shape[1]
    local_ops = translations.shape[0]
    patches, points = patch_points.shape
    stride = round_up(width, LANES)
    tiles = stride // LANES
    inner = 2 if groups % 2 == 0 else 1
    outer = groups // inner
    col = lax.axis_index("col").astype(jnp.int32)
    box = lax.axis_index("box").astype(jnp.int32)
    core, half = col % inner, col // inner
    handled = jnp.stack([((half + j) % outer) * inner + core for j in range(outer)])
    ops_at = jnp.stack([(half * inner + (core + i) % inner) * local_ops for i in range(inner)])
    info = jnp.stack([box % 2])

    operators = [translations]
    for i in range(1, inner):
        moves = [(h * inner + (k + i) % inner, h * inner + k) for h in range(outer) for k in range(inner)]
        operators.append(lax.ppermute(translations, "col", moves))

    cols = outer * share
    outgoing = pl.pallas_call(
        functools.partial(pick_kernel, share),
        out_shape=jax.ShapeDtypeStruct((sources, cols * capacity, width), jnp.bfloat16),
        in_specs=[SMEM, SMEM, ANY],
        out_specs=VMEM,
        scratch_shapes=[
            pltpu.VMEM((cols, width, boxes), jnp.bfloat16),
            pltpu.SemaphoreType.DMA((outer,)),
        ],
        compiler_params=params(32),
    )(handled, export_ids[0].T, jnp.transpose(density, (1, 2, 0)))
    imported = lax.all_to_all(outgoing, "box", split_axis=0, concat_axis=0, tiled=True)

    slots_t = list_slot.T
    parts = []
    edge_parts = []
    for j in range(1, outer):
        part, edge = field_call(imported, slots_t, operators, ops_at, share, capacity, j, jnp.bfloat16)
        moves = [
            (h * inner + k, ((h + j) % outer) * inner + k) for h in range(outer) for k in range(inner)
        ]
        edge_parts.append(lax.ppermute(edge, "col", moves))
        parts.append(lax.ppermute(part, "col", moves))
    own, edges = field_call(imported, slots_t, operators, ops_at, share, capacity, 0, jnp.float32)
    received = jnp.stack(parts)
    for edge in edge_parts:
        edges = edges + edge
    edges = edges.astype(jnp.bfloat16).astype(jnp.float32)
    low, high = edges[0], edges[1]
    even = box % 2 == 0
    first, second = swap_sides(jnp.where(even, high, low), jnp.where(even, low, high), "box")
    low_in = jnp.where(even, second, first)
    high_in = jnp.where(even, first, second)

    local = patch_points - (box * boxes - RIM) * width
    at_box = local // width
    at_point = local - at_box * width
    start = jnp.minimum(jnp.min(at_box, axis=1), boxes + 2 * RIM - SPAN)
    code = (at_box - start[:, None]) * tiles + at_point // LANES
    lane = at_point % LANES

    per_box = share * tiles
    ext_rows = (boxes + 2 * RIM) * per_box
    field_t, corrected_t, sides, rows = pl.pallas_call(
        patch_kernel,
        out_shape=[
            jax.ShapeDtypeStruct((share, width, boxes), jnp.bfloat16),
            jax.ShapeDtypeStruct((share, width, boxes), jnp.bfloat16),
            jax.ShapeDtypeStruct((2, RIM * per_box, LANES), jnp.float32),
            jax.ShapeDtypeStruct((2, RIM * per_box, LANES), jnp.float32),
        ],
        in_specs=[SMEM, SMEM] + [VMEM] * 6 + [ANY],
        out_specs=[VMEM] * 4,
        scratch_shapes=[
            pltpu.VMEM((ext_rows, LANES), jnp.float32),
            pltpu.VMEM((ext_rows, LANES), jnp.float32),
            pltpu.VMEM((patches, share, points), jnp.float32),
            pltpu.VMEM((patches, points, points), jnp.bfloat16),
            pltpu.SemaphoreType.DMA((patches,)),
        ],
        compiler_params=params(48),
    )(info, start, code, lane, own, received, low_in, high_in, inverses)

    back_first, back_second = swap_sides(sides[0], sides[1], "box")
    corrected_t = pl.pallas_call(
        finish_kernel,
        out_shape=jax.ShapeDtypeStruct(corrected_t.shape, corrected_t.dtype),
        in_specs=[SMEM] + [VMEM] * 4,
        out_specs=VMEM,
        scratch_shapes=[pltpu.VMEM((boxes, LANES), jnp.float32)],
        input_output_aliases={4: 0},
        compiler_params=params(32),
    )(info, back_first, back_second, rows, corrected_t)
    return jnp.transpose(field_t, (2, 0, 1)), jnp.transpose(corrected_t, (2, 0, 1))


def solution(mesh):
    return jax.shard_map(
        body,
        mesh=mesh,
        in_specs=(
            P("box", None, None),
            P("box", None, None),
            P("box", None),
            P("col", None, None),
            P("box", None),
            P("box", None, None),
        ),
        out_specs=(P("box", "col", None), P("box", "col", None)),
        check_vma=False,
    )
```

time: 440 us -> 70.2 us (0.16)
  matrix products: 128 us -> 0 us
  other arithmetic: 96.9 us -> 2.51 us
  local copies, waits for them, and re-layouts: 92.9 us -> 4.12 us
  waiting for transfers between devices: 78.6 us -> 11.9 us
  Pallas kernels: 0 us -> 32.1 us
  between operations: 14.2 us -> 0.79 us
  blocking collectives: 7.2 us -> 0 us
    dot_general x17 -> x0, matrix products: 128 us -> none  [the longest x16 120 us: advance(): jnp.dot(gathered.reshape(share * lax.axis_size('col') * box_dev, width),...]
    scatter-add x1 -> x0, other arithmetic: 56.4 us -> none  [body(): spread.at[:, local_points]]
    gather x19 -> x0, local copies, waits for them, and re-layouts: 41.7 us -> none  [the longest x2 30.2 us: body(): jnp.take(flat_field, local_points, axis=1)]
    reduce_scatter x1 -> x0, waiting for transfers between devices: 39.8 us -> none  [body(): field_sum = lax.psum_scatter(result, 'col', scatter_dimension=0, tiled=True)]
    pallas_call x0 -> x5, Pallas kernels: none -> 32.1 us  [the longest x2 17.1 us: field_call(): pl.pallas_call(functools.partial(field_kernel, share, capacity, group), o...]
    ppermute x4 -> x7, waiting for transfers between devices: 34.3 us -> 5.98 us  [the longest x4 5.97 us: swap_sides(): return (lax.ppermute(first, axis, evens), lax.ppermute(second, axis, odds))]
    select_n x18 -> x3, other arithmetic: 28.7 us -> 0.93 us  [the longest x1 0.92 us: body(): lane = at_point % LANES]
    reshape x1 -> x0, local copies, waits for them, and re-layouts: 21.7 us -> none  [body(): spread = spread.reshape(share, box_dev + 2 * RIM, width)]
  transfers between devices with their start and end apart: 6 -> 8, of which waited for: 5 -> 4; matrix products, arithmetic and copies ran while one was open for 1% -> 4% of each run, Pallas kernels for 0% -> 17%
where the time goes in v1:
time: 70.2 us; the launch traced here: 69.7 us
  Pallas kernels  32.1 us (46%)
  starting transfers between devices  18.2 us (26%)
  waiting for transfers between devices  11.9 us (17%)
  local copies, waits for them, and re-layouts  4.12 us (6%)
  other arithmetic  2.51 us (4%)
  between operations  0.79 us (1%)
    pallas_call x2, Pallas kernels, field_call(): pl.pallas_call(functools.partial(field_kernel, share, capacity, group), o...  17.1 us
    pallas_call x1, Pallas kernels, body(): pl.pallas_call(patch_kernel, out_shape=[jax.ShapeDtypeStruct((share, widt...  10.1 us
    ppermute x4, starting transfers between devices, swap_sides(): return (lax.ppermute(first, axis, evens), lax.ppermute(second, axis, odds))  9.83 us
    all_to_all x1, starting transfers between devices, body(): lax.all_to_all(outgoing, 'box', split_axis=0, concat_axis=0, tiled=True)  6.24 us
    ppermute x4, waiting for transfers between devices, swap_sides(): return (lax.ppermute(first, axis, evens), lax.ppermute(second, axis, odds))  5.97 us
    all_to_all x1, waiting for transfers between devices, body(): lax.all_to_all(outgoing, 'box', split_axis=0, concat_axis=0, tiled=True)  5.93 us
    unnamed x10, local copies, waits for them, and re-layouts  4.11 us
    pallas_call x1, Pallas kernels, body(): pl.pallas_call(functools.partial(pick_kernel, share), out_shape=jax.Shape...  2.88 us
  transfers between devices with their start and end apart: 8, of which 4 were waited for; matrix products, arithmetic and copies ran while one was open for 4% of the time, Pallas kernels for 17%

profile of v1, /device:TPU:10, one launch (start us, length us, event | category | flops | bytes accessed | tf_op | source)
XLA Modules:
  0.0 69.7 jit_solution(10109617453259131181)
XLA Ops:
  0.8 0.1 pad_add_fusion.1.groups_ref
  0.8 1.5 %copy-done = bf16[128,16,456]{0,2,1:T(8,128)(2,1)S(1)} copy-done((bf16[128,16,456]{0,2,1:T(8,128)(2,1)S(1)}, bf16[128,16,456]{0,2,1:T(8,128)(2,1)}, u32[]{:S(2)}) %copy-start) | copy-done | bytes 1867800
  2.4 0.7 copy-done.2
  3.0 2.9 %shard_map.77 = bf16[8,32,456]{2,1,0:T(8,128)(2,1)} custom-call(s32[2]{0:T(128)S(1)} %pad_add_fusion.1.groups_ref, s32[4,8]{1,0:T(4,128)S(1)} %bitcast.23, bf16[16,456,128]{2,1,0:T(8,128)(2,1)S(1)} %bitcast.21), custom_call_target="tpu_custom_call" | custom-call | tf_op jit(solution)/shard_map/pallas_call | solution.py:312
  5.9 6.2 %all-to-all-start = ((bf16[8,32,456]{2,1,0:T(8,128)(2,1)}), bf16[8,32,456]{2,1,0:T(8,128)(2,1)S(1)}, u32[]{:S(2)}, u32[]{:S(2)}) async-start(bf16[8,32,456]{2,1,0:T(8,128)(2,1)} %shard_map.77), calls=%async_computation | async-start | bytes 524288 | tf_op jit(solution)/shard_map/all_to_all | solution.py:323
  12.2 0.7 pad_add_fusion.ops_at_ref
  12.8 0.9 %add_select_fusion = (s32[8,1024]{1,0:T(8,128)S(1)}, s32[8]{0:T(128)S(1)}) fusion(s32[8,1024]{1,0:T(8,128)} %param.10, s32[]{:T(128)S(6)} %mul.33), kind=kLoop, calls=%fused_computation | loop fusion | flops 188408 | bytes 65572 | tf_op jit(solution)/shard_map/jit(remainder)/select_n | solution.py:351
  13.7 5.9 %all-to-all-done.imported_ref = bf16[8,32,456]{2,1,0:T(8,128)(2,1)S(1)} async-done(((bf16[8,32,456]{2,1,0:T(8,128)(2,1)}), bf16[8,32,456]{2,1,0:T(8,128)(2,1)S(1)}, u32[]{:S(2)}, u32[]{:S(2)}) %all-to-all-start) | async-done | bytes 233504 | tf_op jit(solution)/shard_map/all_to_all | solution.py:323
  19.7 0.7 %copy-done.3 = bf16[8,32,456]{2,1,0:T(8,128)(2,1)} copy-done((bf16[8,32,456]{2,1,0:T(8,128)(2,1)}, bf16[8,32,456]{2,1,0:T(8,128)(2,1)S(1)}, u32[]{:S(2)}) %copy-start.3) | copy-done | bytes 233496
  20.4 8.5 %shard_map.79 = (bf16[4,128,512]{2,1,0:T(8,128)(2,1)}, f32[2,32,128]{2,1,0:T(8,128)}) custom-call(s32[2]{0:T(128)} %pad_add_fusion.ops_at_ref, bf16[8,32,456]{2,1,0:T(8,128)(2,1)} %copy-done.3, s32[64,128]{1,0:T(8,128)} %bitcast.25, bf16[16,456,456]{2,1,0:T(8,128)(2,1)} %rest_0_.3, bf16[16,456,456]{2,1,0:T(8,128)(2,1)} %collective-permute-done.rest_1_), custom_call_target="tpu_custom_call" | custom-call | flops 2181562368 | bytes 14942208 | tf_op jit(solution)/shard_map/pallas_call | solution.py:153
  28.8 1.6 %collective-permute-start.2 = (f32[2,32,128]{2,1,0:T(8,128)}, f32[2,32,128]{2,1,0:T(8,128)S(1)}, u32[]{:S(2)}, u32[]{:S(2)}) collective-permute-start(f32[2,32,128]{2,1,0:T(8,128)} %get-tuple-element.13), channel_id=1, source_target_pairs={{0,2},{1,3},{2,0},{3,1},{4,6},{5,7},{6,4},{7,5},{8,10},{9,11},{10,... | collective-permute-start | bytes 98312 | tf_op jit(solution)/shard_map/ppermute | solution.py:333
  30.4 0.5 collective-permute-start.1
  30.9 8.6 %shard_map.78 = (f32[4,128,512]{2,1,0:T(8,128)}, f32[2,32,128]{2,1,0:T(8,128)}) custom-call(s32[2]{0:T(128)} %pad_add_fusion.ops_at_ref, bf16[8,32,456]{2,1,0:T(8,128)(2,1)} %copy-done.3, s32[64,128]{1,0:T(8,128)} %bitcast.26, bf16[16,456,456]{2,1,0:T(8,128)(2,1)} %rest_0_.3, bf16[16,456,456]{2,1,0:T(8,128)(2,1)} %collective-permute-done.rest_1_), custom_call_target="tpu_custom_call" | custom-call | flops 2181562368 | bytes 14942208 | tf_op jit(solution)/shard_map/pallas_call | solution.py:153
  39.6 0.8 %fusion.3 = f32[2,32,128]{2,1,0:T(8,128)S(1)} fusion(f32[2,32,128]{2,1,0:T(8,128)} %get-tuple-element.12, f32[2,32,128]{2,1,0:T(8,128)S(1)} %collective-permute-done.2), kind=kLoop, calls=%fused_computation.14 | loop fusion | flops 24576 | bytes 98304 | tf_op jit(solution)/shard_map/convert_element_type | solution.py:339
  40.4 3.4 %collective-permute-start.3 = (f32[32,128]{1,0:T(8,128)S(1)}, f32[32,128]{1,0:T(8,128)S(1)}, u32[]{:S(2)}, u32[]{:S(2)}) collective-permute-start(f32[32,128]{1,0:T(8,128)S(1)} %get-tuple-element.23), channel_id=1, source_target_pairs={{4,8},{12,16},{20,24},{8,4},{16,12},{24,20},{5,9},{13,17},{21,25},... | collective-permute-start | bytes 49160 | tf_op jit(solution)/shard_map/ppermute | solution.py:284
  43.8 2.1 %collective-permute-start.4 = (f32[32,128]{1,0:T(8,128)S(1)}, f32[32,128]{1,0:T(8,128)S(1)}, u32[]{:S(2)}, u32[]{:S(2)}) collective-permute-start(f32[32,128]{1,0:T(8,128)S(1)} %get-tuple-element.22), channel_id=1, source_target_pairs={{0,4},{8,12},{16,20},{24,28},{4,0},{12,8},{20,16},{28,24},{1,5},{9... | collective-permute-start | bytes 49160 | tf_op jit(solution)/shard_map/ppermute | solution.py:284
  46.0 0.9 %collective-permute-done.3 = f32[32,128]{1,0:T(8,128)S(1)} collective-permute-done((f32[32,128]{1,0:T(8,128)S(1)}, f32[32,128]{1,0:T(8,128)S(1)}, u32[]{:S(2)}, u32[]{:S(2)}) %collective-permute-start.3) | collective-permute-done | bytes 16416 | tf_op jit(solution)/shard_map/ppermute | solution.py:284
  46.9 0.8 %collective-permute-done.4 = f32[32,128]{1,0:T(8,128)S(1)} collective-permute-done((f32[32,128]{1,0:T(8,128)S(1)}, f32[32,128]{1,0:T(8,128)S(1)}, u32[]{:S(2)}, u32[]{:S(2)}) %collective-permute-start.4) | collective-permute-done | bytes 16416 | tf_op jit(solution)/shard_map/ppermute | solution.py:284
  47.7 1.2 %copy-done.1 = f32[4,128,512]{2,1,0:T(8,128)S(1)} copy-done((f32[4,128,512]{2,1,0:T(8,128)S(1)}, f32[4,128,512]{2,1,0:T(8,128)}, u32[]{:S(2)}) %copy-start.1) | copy-done | bytes 1048600
  48.9 10.1 %shard_map.80 = (bf16[4,456,128]{2,1,0:T(8,128)(2,1)}, bf16[4,456,128]{2,1,0:T(8,128)(2,1)}, f32[2,32,128]{2,1,0:T(8,128)S(1)}, f32[2,32,128]{2,1,0:T(8,128)S(1)}) custom-call(s32[1]{0:T(128)} %bitcast.info_ref, s32[8]{0:T(128)S(1)} %broadcast_minimum_fusion.starts_ref, s32[8,1024]{1,0:T(8,128)S(1)} %fusion.code_ref, ...), custom_call_target="tpu_custom_call" | custom-call | tf_op jit(solution)/shard_map/pallas_call | solution.py:355
  59.0 2.1 %collective-permute-start.5 = (f32[32,128]{1,0:T(8,128)S(1)}, f32[32,128]{1,0:T(8,128)S(1)}, u32[]{:S(2)}, u32[]{:S(2)}) collective-permute-start(f32[32,128]{1,0:T(8,128)S(1)} %get-tuple-element.19), channel_id=1, source_target_pairs={{0,4},{8,12},{16,20},{24,28},{4,0},{12,8},{20,16},{28,24},{1,5},{9... | collective-permute-start | bytes 49160 | tf_op jit(solution)/shard_map/ppermute | solution.py:284
  61.1 2.2 %collective-permute-start.6 = (f32[32,128]{1,0:T(8,128)S(1)}, f32[32,128]{1,0:T(8,128)S(1)}, u32[]{:S(2)}, u32[]{:S(2)}) collective-permute-start(f32[32,128]{1,0:T(8,128)S(1)} %get-tuple-element.18), channel_id=1, source_target_pairs={{4,8},{12,16},{20,24},{8,4},{16,12},{24,20},{5,9},{13,17},{21,25},... | collective-permute-start | bytes 49160 | tf_op jit(solution)/shard_map/ppermute | solution.py:284
  63.3 4.3 %collective-permute-done.6.second_ref = f32[32,128]{1,0:T(8,128)S(1)} collective-permute-done((f32[32,128]{1,0:T(8,128)S(1)}, f32[32,128]{1,0:T(8,128)S(1)}, u32[]{:S(2)}, u32[]{:S(2)}) %collective-permute-start.6) | collective-permute-done | bytes 16416 | tf_op jit(solution)/shard_map/ppermute | solution.py:284
  67.6 2.0 %shard_map.81 = bf16[4,456,128]{2,1,0:T(8,128)(2,1)} custom-call(s32[1]{0:T(128)} %bitcast.info_ref, f32[32,128]{1,0:T(8,128)S(1)} %collective-permute-done.5.first_ref, f32[32,128]{1,0:T(8,128)S(1)} %collective-permute-done.6.second_ref, f32[2,32,128]{2,1,0:T(8,128)S(1)} %get-tuple-element.16.rows_ref, ...), custom_call_target="tpu_custom_call", output_to_operand_aliasing={{}: (4, {})} | custom-call | tf_op jit(solution)/shard_map/pallas_call | solution.py:376
  (16 shorter events, 0.2 us)
Async XLA Ops:
  0.6 19.1 %collective-permute-start = (bf16[16,456,456]{2,1,0:T(8,128)(2,1)}, bf16[16,456,456]{2,1,0:T(8,128)(2,1)}, u32[]{:S(2)}, u32[]{:S(2)}) collective-permute-start(bf16[16,456,456]{2,1,0:T(8,128)(2,1)} %rest_0_.3), channel_id=1, source_target_pairs={{1,0},{0,1},{3,2},{2,3},{5,4},{4,5},{7,6},{6,7},{9,8},{8,9},{11,10... | collective-permute-start | bytes 19961864 | tf_op jit(solution)/shard_map/ppermute | solution.py:309
  0.8 1.5 %copy-start = (bf16[128,16,456]{0,2,1:T(8,128)(2,1)S(1)}, bf16[128,16,456]{0,2,1:T(8,128)(2,1)}, u32[]{:S(2)}) copy-start(bf16[128,16,456]{0,2,1:T(8,128)(2,1)} %param.6) | copy-start | bytes 5603332
  2.4 0.7 copy-start.2
  5.9 13.8 %all-to-all-start = ((bf16[8,32,456]{2,1,0:T(8,128)(2,1)}), bf16[8,32,456]{2,1,0:T(8,128)(2,1)S(1)}, u32[]{:S(2)}, u32[]{:S(2)}) async-start(bf16[8,32,456]{2,1,0:T(8,128)(2,1)} %shard_map.77), calls=%async_computation | async-start | bytes 524288 | tf_op jit(solution)/shard_map/all_to_all | solution.py:323
  19.7 0.7 %copy-start.3 = (bf16[8,32,456]{2,1,0:T(8,128)(2,1)}, bf16[8,32,456]{2,1,0:T(8,128)(2,1)S(1)}, u32[]{:S(2)}) copy-start(bf16[8,32,456]{2,1,0:T(8,128)(2,1)S(1)} %all-to-all-done.imported_ref) | copy-start | bytes 700420
  28.8 10.8 %collective-permute-start.2 = (f32[2,32,128]{2,1,0:T(8,128)}, f32[2,32,128]{2,1,0:T(8,128)S(1)}, u32[]{:S(2)}, u32[]{:S(2)}) collective-permute-start(f32[2,32,128]{2,1,0:T(8,128)} %get-tuple-element.13), channel_id=1, source_target_pairs={{0,2},{1,3},{2,0},{3,1},{4,6},{5,7},{6,4},{7,5},{8,10},{9,11},{10,... | collective-permute-start | bytes 98312 | tf_op jit(solution)/shard_map/ppermute | solution.py:333
  30.4 15.5 %copy-start.4 = (s32[8,1024]{1,0:T(8,128)S(1)}, s32[8,1024]{1,0:T(8,128)}, u32[]{:S(2)}) copy-start(s32[8,1024]{1,0:T(8,128)} %param.10) | copy-start | bytes 98308
  30.4 17.3 %collective-permute-start.1 = (bf16[4,128,512]{2,1,0:T(8,128)(2,1)}, bf16[4,128,512]{2,1,0:T(8,128)(2,1)S(1)}, u32[]{:S(2)}, u32[]{:S(2)}) collective-permute-start(bf16[4,128,512]{2,1,0:T(8,128)(2,1)} %get-tuple-element.11), channel_id=1, source_target_pairs={{0,2},{1,3},{2,0},{3,1},{4,6},{5,7},{6,4},{7,5},{8,10},{9,11},{10,... | collective-permute-start | bytes 1572872 | tf_op jit(solution)/shard_map/ppermute | solution.py:334
  40.4 6.5 %collective-permute-start.3 = (f32[32,128]{1,0:T(8,128)S(1)}, f32[32,128]{1,0:T(8,128)S(1)}, u32[]{:S(2)}, u32[]{:S(2)}) collective-permute-start(f32[32,128]{1,0:T(8,128)S(1)} %get-tuple-element.23), channel_id=1, source_target_pairs={{4,8},{12,16},{20,24},{8,4},{16,12},{24,20},{5,9},{13,17},{21,25},... | collective-permute-start | bytes 49160 | tf_op jit(solution)/shard_map/ppermute | solution.py:284
  43.8 3.8 %collective-permute-start.4 = (f32[32,128]{1,0:T(8,128)S(1)}, f32[32,128]{1,0:T(8,128)S(1)}, u32[]{:S(2)}, u32[]{:S(2)}) collective-permute-start(f32[32,128]{1,0:T(8,128)S(1)} %get-tuple-element.22), channel_id=1, source_target_pairs={{0,4},{8,12},{16,20},{24,28},{4,0},{12,8},{20,16},{28,24},{1,5},{9... | collective-permute-start | bytes 49160 | tf_op jit(solution)/shard_map/ppermute | solution.py:284
  47.7 1.2 %copy-start.1 = (f32[4,128,512]{2,1,0:T(8,128)S(1)}, f32[4,128,512]{2,1,0:T(8,128)}, u32[]{:S(2)}) copy-start(f32[4,128,512]{2,1,0:T(8,128)} %get-tuple-element.10.own_ref) | copy-start | bytes 3145732
  59.0 4.3 %collective-permute-start.5 = (f32[32,128]{1,0:T(8,128)S(1)}, f32[32,128]{1,0:T(8,128)S(1)}, u32[]{:S(2)}, u32[]{:S(2)}) collective-permute-start(f32[32,128]{1,0:T(8,128)S(1)} %get-tuple-element.19), channel_id=1, source_target_pairs={{0,4},{8,12},{16,20},{24,28},{4,0},{12,8},{20,16},{28,24},{1,5},{9... | collective-permute-start | bytes 49160 | tf_op jit(solution)/shard_map/ppermute | solution.py:284
  61.1 6.5 %collective-permute-start.6 = (f32[32,128]{1,0:T(8,128)S(1)}, f32[32,128]{1,0:T(8,128)S(1)}, u32[]{:S(2)}, u32[]{:S(2)}) collective-permute-start(f32[32,128]{1,0:T(8,128)S(1)} %get-tuple-element.18), channel_id=1, source_target_pairs={{4,8},{12,16},{20,24},{8,4},{16,12},{24,20},{5,9},{13,17},{21,25},... | collective-permute-start | bytes 49160 | tf_op jit(solution)/shard_map/ppermute | solution.py:284

commit v2 on v0

v2 whole, which is shorter than its diff:
```python
import functools

import jax
import jax.numpy as jnp
from jax import lax
from jax.experimental import pallas as pl
from jax.experimental.pallas import tpu as pltpu
from jax.sharding import PartitionSpec as P

RIM = 2
SPAN = 8
LANES = 128
NT = (((1,), (1,)), ((), ()))
ANY = pl.BlockSpec(memory_space=pl.ANY)
VMEM = pl.BlockSpec(memory_space=pltpu.VMEM)
SMEM = pl.BlockSpec(memory_space=pltpu.SMEM)


def round_up(n, m):
    return -(-n // m) * m


def params(limit):
    return pltpu.CompilerParams(vmem_limit_bytes=limit << 20)


def iota(shape, dim):
    return lax.broadcasted_iota(jnp.int32, shape, dim)


def div(x, n):
    if n & (n - 1) == 0:
        return x >> (n.bit_length() - 1)
    return lax.div(x, jnp.int32(n))


def mod(x, n):
    if n & (n - 1) == 0:
        return x & (n - 1)
    return lax.rem(x, jnp.int32(n))


def handled_groups():
    groups = lax.axis_size("col")
    inner = 2 if groups % 2 == 0 else 1
    return inner, groups // inner


def pick_kernel(share, ids_hbm, density_ref, out_ref, ids_ref, block, sems):
    capacity, dests = ids_ref.shape
    cols, width, boxes = block.shape
    inner, outer = handled_groups()
    col = lax.axis_index("col")
    ids_copy = pltpu.make_async_copy(ids_hbm, ids_ref, sems.at[outer])
    ids_copy.start()
    copies = []
    for j in range(outer):
        group = mod(div(col, inner) + j, outer) * inner + mod(col, inner)
        copy = pltpu.make_async_copy(
            density_ref.at[pl.ds(group * share, share)],
            block.at[pl.ds(j * share, share)],
            sems.at[j],
        )
        copy.start()
        copies.append(copy)
    ids_copy.wait()
    rows = dests * cols * capacity
    row = iota((rows, boxes), 0)
    pair = div(row, cols * capacity) * capacity + mod(row, capacity)
    column = mod(div(row, capacity), cols)

    def place(k, wanted):
        return jnp.where(pair == k, ids_ref[mod(k, capacity), div(k, capacity)], wanted)

    wanted = jnp.full((rows, boxes), -1, jnp.int32)
    if dests * capacity <= 64:
        for k in range(dests * capacity):
            wanted = place(jnp.int32(k), wanted)
    else:
        wanted = lax.fori_loop(0, dests * capacity, place, wanted)
    hit = wanted == iota((rows, boxes), 1)
    for copy in copies:
        copy.wait()
    total = jnp.zeros((rows, width), jnp.float32)
    for c in range(cols):
        chosen = jnp.where(hit & (column == c), 1.0, 0.0).astype(jnp.bfloat16)
        total = total + lax.dot_general(
            chosen, block[c], NT, preferred_element_type=jnp.float32
        )
    out_ref[...] = total.astype(out_ref.dtype).reshape(out_ref.shape)


def prepare_kernel(
    slots, tiles, width, local_ops, slots_ref, points_ref, picks_ref, code_ref, lane_ref, spans_ref, hot
):
    boxes = slots_ref.shape[1]
    patches = code_ref.shape[0]
    inner, outer = handled_groups()
    col = lax.axis_index("col")
    for half in range(inner):
        first = (div(col, inner) * inner + mod(col + half, inner)) * local_ops
        wanted = slots_ref[pl.ds(first, local_ops), :]
        for o in range(local_ops):
            picked = iota((slots, boxes), 0) == wanted[o : o + 1, :]
            at = (half * local_ops + o) * slots
            hot[at : at + slots, :] = jnp.where(picked, 1.0, 0.0).astype(jnp.bfloat16)
    picks_ref[...] = hot[...].T
    local = points_ref[...] - (lax.axis_index("box") * boxes - RIM) * width
    at_box = ((local.astype(jnp.float32) + 0.5) * (1.0 / width)).astype(jnp.int32)
    at_point = local - at_box * width
    lowest = jnp.min(at_box, axis=1, keepdims=True)
    highest = jnp.max(at_box, axis=1, keepdims=True)
    start = jnp.minimum(lowest, boxes + 2 * RIM - SPAN)
    code = (at_box - start) * tiles + div(at_point, LANES)
    lane = mod(at_point, LANES)
    for p in range(patches):
        code_ref[p] = code[p : p + 1]
        lane_ref[p] = lane[p : p + 1]
        spans_ref[p] = jnp.min(lowest[p : p + 1])
        spans_ref[patches + p] = jnp.min(highest[p : p + 1])


def prepare_call(slots_t, patch_points, slots, tiles, width, local_ops):
    inner, _ = handled_groups()
    boxes = slots_t.shape[1]
    patches, points = patch_points.shape
    all_slots = inner * local_ops * slots
    return pl.pallas_call(
        functools.partial(prepare_kernel, slots, tiles, width, local_ops),
        out_shape=[
            jax.ShapeDtypeStruct((boxes, all_slots), jnp.bfloat16),
            jax.ShapeDtypeStruct((patches, 1, points), jnp.int32),
            jax.ShapeDtypeStruct((patches, 1, points), jnp.int32),
            jax.ShapeDtypeStruct((2 * patches,), jnp.int32),
        ],
        in_specs=[VMEM] * 2,
        out_specs=[VMEM] * 3 + [SMEM],
        scratch_shapes=[pltpu.VMEM((all_slots, boxes), jnp.bfloat16)],
        compiler_params=params(8),
    )(
        pltpu.with_memory_space_constraint(slots_t, pltpu.HBM),
        pltpu.with_memory_space_constraint(patch_points, pltpu.HBM),
    )


def field_kernel(share, capacity, group, fetch, imported_ref, picks_ref, *rest):
    if fetch:
        sources_refs, (out_ref, edge_ref, operators_ref, terms, sems) = rest[:-5], rest[-5:]
    else:
        sources_refs, (operators_ref, out_ref, edge_ref, terms) = (), rest
    sources, per_source, width = imported_ref.shape
    all_ops = operators_ref.shape[0]
    boxes = picks_ref.shape[0]
    slots = sources * capacity
    stride = terms.shape[1] // share
    tiles = stride // LANES
    copies, chunk = {}, 1
    for ref in sources_refs:
        local_ops = ref.shape[0]
        chunk = 4 if local_ops % 4 == 0 else 1
        for at in range(0, local_ops, chunk):
            to = len(copies) * chunk
            copy = pltpu.make_async_copy(
                ref.at[pl.ds(at, chunk)], operators_ref.at[pl.ds(to, chunk)], sems.at[len(copies)]
            )
            copy.start()
            copies[to] = copy
    arrived = sources * per_source
    shape = (share * slots, arrived)
    row = iota(shape, 0)
    slot = mod(row, slots)
    origin = (
        div(slot, capacity) * per_source
        + (group * share + div(row, slots)) * capacity
        + mod(slot, capacity)
    )
    order = jnp.where(origin == iota(shape, 1), 1.0, 0.0).astype(jnp.bfloat16)
    flat = imported_ref[...].reshape(arrived, width)
    ordered = jnp.dot(order, flat, preferred_element_type=jnp.float32).astype(jnp.bfloat16)
    for o in range(all_ops):
        if o in copies:
            copies[o].wait()
        term = jnp.dot(ordered, operators_ref[o], preferred_element_type=jnp.float32)
        term = term.astype(jnp.bfloat16)
        for c in range(share):
            terms[o * slots : (o + 1) * slots, c * stride : c * stride + width] = term[
                c * slots : (c + 1) * slots
            ]
    total = jnp.dot(picks_ref[...], terms[...], preferred_element_type=jnp.float32)
    total = total.astype(out_ref.dtype)
    for c in range(share):
        out_ref[c] = total[:, c * stride : (c + 1) * stride]
        for t in range(tiles):
            at = (c * tiles + t) * LANES
            to = pl.ds(c * tiles + t, RIM, stride=share * tiles)
            edge_ref[0, to, :] = total[:RIM, at : at + LANES].astype(jnp.float32)
            edge_ref[1, to, :] = total[boxes - RIM :, at : at + LANES].astype(jnp.float32)


def field_call(imported, picks, operators, share, capacity, group, dtype):
    sources, _, width = imported.shape
    boxes, all_slots = picks.shape
    all_ops = all_slots // (sources * capacity)
    stride = round_up(width, LANES)
    fetch = isinstance(operators, tuple)
    out_shape = [
        jax.ShapeDtypeStruct((share, boxes, stride), dtype),
        jax.ShapeDtypeStruct((2, RIM * share * (stride // LANES), LANES), jnp.float32),
    ]
    scratch = [pltpu.VMEM((all_slots, share * stride), jnp.bfloat16)]
    if fetch:
        out_shape.append(pltpu.VMEM((all_ops, width, width), operators[0].dtype))
        scratch.append(pltpu.SemaphoreType.DMA((all_ops,)))
        operators = [pltpu.with_memory_space_constraint(o, pltpu.HBM) for o in operators]
    else:
        operators = [pltpu.with_memory_space_constraint(operators, pltpu.VMEM)]
    return pl.pallas_call(
        functools.partial(field_kernel, share, capacity, group, fetch),
        out_shape=out_shape,
        in_specs=[VMEM] * 2 + [ANY if fetch else VMEM] * len(operators),
        out_specs=[VMEM] * len(out_shape),
        scratch_shapes=scratch,
        compiler_params=params(8 + all_slots * share * stride * 2 // (1 << 20)),
        cost_estimate=pl.CostEstimate(
            flops=2 * all_slots * share * width * (width + boxes),
            bytes_accessed=2 * all_ops * width * width,
            transcendentals=0,
        ),
    )(imported, picks, *operators)


def edge_kernel(*refs):
    edge_refs, (first_ref, second_ref) = refs[:-2], refs[-2:]
    total = edge_refs[0][...]
    for ref in edge_refs[1:]:
        total = total + ref[...]
    total = total.astype(jnp.bfloat16).astype(jnp.float32)
    even = mod(lax.axis_index("box"), 2) == 0
    first_ref[...] = jnp.where(even, total[1], total[0])
    second_ref[...] = jnp.where(even, total[0], total[1])


def edge_call(*edges):
    side = jax.ShapeDtypeStruct(edges[0].shape[1:], jnp.float32)
    return pl.pallas_call(
        edge_kernel,
        out_shape=[side, side],
        in_specs=[VMEM] * len(edges),
        out_specs=[VMEM, VMEM],
        compiler_params=params(2),
        cost_estimate=pl.CostEstimate(flops=10**10, bytes_accessed=0, transcendentals=0),
    )(*edges)


def order_patches(spans_ref, order_ref, boxes):
    patches = spans_ref.shape[0] // 2
    count = jnp.int32(0)
    for wanted in (True, False):
        for p in range(patches):
            reaches = (spans_ref[p] < RIM) | (spans_ref[patches + p] >= boxes + RIM)
            order_ref[count] = p
            count = count + jnp.where(reaches == wanted, 1, 0)
        if wanted:
            first = count
    return first


def patch_batch(chosen, spans_ref, code_ref, lane_ref, ext, inverses_ref, spread, share, boxes):
    points = code_ref.shape[2]
    per_box = ext.shape[0] // (boxes + 2 * RIM)
    tiles = per_box // share
    window = SPAN * per_box
    places, products = [], []
    row = iota((window, LANES), 0)
    row_code = div(row, per_box) * tiles + mod(row, tiles)
    for p in chosen:
        start = jnp.minimum(spans_ref[p], boxes + 2 * RIM - SPAN) * per_box
        places.append(pl.ds(pl.multiple_of(start, 8), window))
        held = ext[places[-1], :]
        values = []
        for at in range(0, points, LANES):
            code = code_ref[p, :, at : at + LANES]
            lane = jnp.broadcast_to(lane_ref[p, :, at : at + LANES], (window, LANES))
            found = jnp.take_along_axis(held, lane, axis=1)
            found = jnp.where(row_code == code, found, 0.0)
            found = jnp.sum(found.reshape(SPAN, per_box, LANES), axis=0)
            values.append(jnp.sum(found.reshape(share, tiles, LANES), axis=1))
        values = jnp.concatenate(values, axis=1).astype(jnp.bfloat16)
        product = jnp.dot(values, inverses_ref[p], preferred_element_type=jnp.float32)
        products.append(product.astype(jnp.bfloat16).astype(jnp.float32))
    row = iota((window, points), 0)
    row_code = div(row, per_box) * tiles + mod(row, tiles)
    for p, place, product in zip(chosen, places, products):
        product = jnp.concatenate(
            [jnp.broadcast_to(product[c : c + 1], (tiles, points)) for c in range(share)], axis=0
        )
        product = jnp.concatenate([product] * SPAN, axis=0)
        left = jnp.where(row_code == code_ref[p], product, 0.0).astype(jnp.bfloat16)
        right = jnp.where(iota((LANES, points), 0) == lane_ref[p], 1.0, 0.0)
        placed = lax.dot_general(
            left, right.astype(jnp.bfloat16), NT, preferred_element_type=jnp.float32
        )
        spread[place, :] = spread[place, :] + placed


def batch_size(patches):
    return 2 if patches % 2 == 0 else 1


def early_kernel(
    spans_ref, code_ref, lane_ref, own_ref, received_ref, inverses_ref, first_ref, second_ref,
    ext, spread, first_out, second_out, order_ref,
):
    share, boxes, stride = own_ref.shape
    tiles = stride // LANES
    per_box = share * tiles
    rim = RIM * per_box
    end = rim + boxes * per_box
    patches = code_ref.shape[0]
    even = mod(lax.axis_index("box"), 2) == 0
    first = first_ref[...]
    second = second_ref[...]
    spread[...] = jnp.zeros_like(spread)
    ext[:rim, :] = jnp.where(even, second, first)
    ext[end:, :] = jnp.where(even, first, second)
    for c in range(share):
        for t in range(tiles):
            part = own_ref[c, :, t * LANES : (t + 1) * LANES]
            for r in range(received_ref.shape[0]):
                part = part + received_ref[r, c, :, t * LANES : (t + 1) * LANES].astype(jnp.float32)
            part = part.astype(jnp.bfloat16).astype(jnp.float32)
            ext[pl.ds(rim + c * tiles + t, boxes, stride=per_box), :] = part
    batch = batch_size(patches)
    reaching = order_patches(spans_ref, order_ref, boxes)

    def step(i, carry):
        chosen = [order_ref[i * batch + k] for k in range(batch)]
        patch_batch(chosen, spans_ref, code_ref, lane_ref, ext, inverses_ref, spread, share, boxes)
        return carry

    lax.fori_loop(0, div(reaching + batch - 1, batch), step, 0)
    low = spread[:rim, :]
    high = spread[end:, :]
    first_out[...] = jnp.where(even, high, low)
    second_out[...] = jnp.where(even, low, high)


def late_kernel(
    spans_ref, code_ref, lane_ref, ext, early_ref, inverses_ref,
    field_ref, corrected_ref, rows_ref, spread, order_ref,
):
    share, width, boxes = field_ref.shape
    per_box = ext.shape[0] // (boxes + 2 * RIM)
    tiles = per_box // share
    rim = RIM * per_box
    end = rim + boxes * per_box
    patches = code_ref.shape[0]
    spread[...] = early_ref[...]
    batch = batch_size(patches)
    reaching = order_patches(spans_ref, order_ref, boxes)

    def step(i, carry):
        chosen = [order_ref[i * batch + k] for k in range(batch)]
        patch_batch(chosen, spans_ref, code_ref, lane_ref, ext, inverses_ref, spread, share, boxes)
        return carry

    lax.fori_loop(div(reaching + batch - 1, batch), patches // batch, step, 0)
    for c in range(share):
        for t in range(tiles):
            at = pl.ds(rim + c * tiles + t, boxes, stride=per_box)
            last = min(width - t * LANES, LANES)
            own = ext[at, :]
            total = own + spread[at, :]
            to = slice(t * LANES, t * LANES + last)
            field_ref[c, to, :] = own.T[:last].astype(field_ref.dtype)
            corrected_ref[c, to, :] = total.T[:last].astype(corrected_ref.dtype)
    rows_ref[:rim] = ext[rim : 2 * rim, :] + spread[rim : 2 * rim, :]
    rows_ref[rim:] = ext[end - rim : end, :] + spread[end - rim : end, :]


def finish_kernel(first_ref, second_ref, rows_ref, corrected_ref, out_ref):
    share, width, boxes = corrected_ref.shape
    rim = rows_ref.shape[0] // 2
    per_box = rim // RIM
    tiles = per_box // share
    even = mod(lax.axis_index("box"), 2) == 0
    first = first_ref[...]
    second = second_ref[...]
    low = rows_ref[:rim] + jnp.where(even, second, first)
    high = rows_ref[rim:] + jnp.where(even, first, second)
    rows = jnp.concatenate([low, high], axis=0)
    point = mod(iota(rows.shape, 0), tiles) * LANES + iota(rows.shape, 1)
    rows = jnp.where(point < width, rows, 0.0).T.astype(jnp.bfloat16)
    shape = (2 * rim, per_box * boxes)
    row = iota(shape, 0)
    box = div(mod(row, rim), per_box) + jnp.where(row < rim, 0, boxes - RIM)
    target = mod(row, per_box) * boxes + box
    place = jnp.where(target == iota(shape, 1), 1.0, 0.0).astype(jnp.bfloat16)
    placed = jnp.dot(rows, place, preferred_element_type=jnp.float32)
    box = iota((LANES, boxes), 1)
    edge = (box < RIM) | (box >= boxes - RIM)
    for c in range(share):
        for t in range(tiles):
            last = min(width - t * LANES, LANES)
            at = (c * tiles + t) * boxes
            to = slice(t * LANES, t * LANES + last)
            kept = corrected_ref[c, to, :].astype(jnp.float32)
            out_ref[c, to, :] = jnp.where(
                edge[:last], placed[:last, at : at + boxes], kept
            ).astype(out_ref.dtype)


def swap_sides(first, second):
    count = lax.axis_size("box")

    def moves(start):
        pairs = [(i, i + 1) for i in range(start, count - 1, 2)]
        return pairs + [(b, a) for a, b in pairs]

    return lax.ppermute(first, "box", moves(0)), lax.ppermute(second, "box", moves(1))


def body(density, export_ids, list_slot, translations, patch_points, inverses):
    boxes, total_cols, width = density.shape
    inner, outer = handled_groups()
    share = total_cols // (inner * outer)
    capacity = export_ids.shape[2]
    sources = export_ids.shape[1]
    patches, points = patch_points.shape
    stride = round_up(width, LANES)
    tiles = stride // LANES
    per_box = share * tiles
    places = [(h, k) for h in range(outer) for k in range(inner)]

    others = []
    for i in range(1, inner):
        moves = [(h * inner + (k + i) % inner, h * inner + k) for h, k in places]
        others.append(lax.ppermute(translations, "col", moves))

    cols = outer * share
    outgoing = pl.pallas_call(
        functools.partial(pick_kernel, share),
        out_shape=jax.ShapeDtypeStruct((sources, cols * capacity, width), jnp.bfloat16),
        in_specs=[ANY, ANY],
        out_specs=VMEM,
        scratch_shapes=[
            pltpu.SMEM((capacity, sources), jnp.int32),
            pltpu.VMEM((cols, width, boxes), jnp.bfloat16),
            pltpu.SemaphoreType.DMA((outer + 1,)),
        ],
        compiler_params=params(8),
    )(
        pltpu.with_memory_space_constraint(export_ids[0].T, pltpu.HBM),
        pltpu.with_memory_space_constraint(jnp.transpose(density, (1, 2, 0)), pltpu.HBM),
    )
    imported = lax.all_to_all(outgoing, "box", split_axis=0, concat_axis=0, tiled=True)

    _, *prepared = lax.optimization_barrier((outgoing, list_slot.T, patch_points))
    picks, code, lane, spans = prepare_call(
        *prepared, sources * capacity, tiles, width, translations.shape[0]
    )
    operators = (translations, *others)
    parts, edges = [], []
    for j in range(1, outer):
        part, edge, *loaded = field_call(
            imported, picks, operators, share, capacity, j, jnp.bfloat16
        )
        operators = loaded[0] if loaded else operators
        moves = [(h * inner + k, ((h + j) % outer) * inner + k) for h, k in places]
        edges.append(lax.ppermute(edge, "col", moves))
        parts.append(lax.ppermute(part, "col", moves))
    own, edge = field_call(imported, picks, operators, share, capacity, 0, jnp.float32)[:2]
    first, second = swap_sides(*edge_call(edge, *edges))
    received = jnp.stack(parts)

    ext_rows = (boxes + 2 * RIM) * per_box
    rim = RIM * per_box
    side = jax.ShapeDtypeStruct((rim, LANES), jnp.float32)
    ext, early, first, second = pl.pallas_call(
        early_kernel,
        out_shape=[
            pltpu.VMEM((ext_rows, LANES), jnp.float32),
            pltpu.VMEM((ext_rows, LANES), jnp.float32),
            side,
            side,
        ],
        in_specs=[SMEM] + [VMEM] * 7,
        out_specs=[VMEM] * 4,
        scratch_shapes=[pltpu.SMEM((patches + 1,), jnp.int32)],
        compiler_params=params(10),
    )(spans, code, lane, own, received, inverses, first, second)
    first, second = swap_sides(first, second)

    field_t, corrected_t, rows = pl.pallas_call(
        late_kernel,
        out_shape=[
            jax.ShapeDtypeStruct((share, width, boxes), jnp.bfloat16),
            pltpu.VMEM((share, width, boxes), jnp.bfloat16),
            pltpu.VMEM((2 * rim, LANES), jnp.float32),
        ],
        in_specs=[SMEM] + [VMEM] * 5,
        out_specs=[VMEM] * 3,
        scratch_shapes=[
            pltpu.VMEM((ext_rows, LANES), jnp.float32),
            pltpu.SMEM((patches + 1,), jnp.int32),
        ],
        compiler_params=params(10),
        cost_estimate=pl.CostEstimate(
            flops=2 * patches * share * points * points,
            bytes_accessed=patches * points * points * 2,
            transcendentals=0,
        ),
    )(spans, code, lane, ext, early, inverses)

    corrected_t = pl.pallas_call(
        finish_kernel,
        out_shape=jax.ShapeDtypeStruct(corrected_t.shape, corrected_t.dtype),
        in_specs=[VMEM] * 4,
        out_specs=VMEM,
        compiler_params=params(8),
    )(first, second, rows, corrected_t)
    return jnp.transpose(field_t, (2, 0, 1)), jnp.transpose(corrected_t, (2, 0, 1))


def solution(mesh):
    return jax.shard_map(
        body,
        mesh=mesh,
        in_specs=(
            P("box", None, None),
            P("box", None, None),
            P("box", None),
            P("col", None, None),
            P("box", None),
            P("box", None, None),
        ),
        out_specs=(P("box", "col", None), P("box", "col", None)),
        check_vma=False,
    )
```

time: 440 us -> 53.4 us (0.12)
  the two profiles are of different devices: /device:TPU:10 before, /device:TPU:2 now
where the time goes in v2:
time: 53.4 us; the launch traced here: 52.4 us
  Pallas kernels  22.6 us (42%)
  starting transfers between devices  16.8 us (31%)
  waiting for transfers between devices  12.2 us (23%)
  between operations  0.77 us (1%)
    pallas_call x2, Pallas kernels, field_call(): pl.pallas_call(functools.partial(field_kernel, share, capacity, group, fe...  9.62 us
    all_to_all x1, waiting for transfers between devices, body(): lax.all_to_all(outgoing, 'box', split_axis=0, concat_axis=0, tiled=True)  7.35 us
    ppermute x2, starting transfers between devices, swap_sides(): lax.ppermute(second, 'box', moves(1))  6.56 us
    all_to_all x1, starting transfers between devices, body(): lax.all_to_all(outgoing, 'box', split_axis=0, concat_axis=0, tiled=True)  6.35 us
    pallas_call x1, Pallas kernels, body(): pl.pallas_call(late_kernel, out_shape=[jax.ShapeDtypeStruct((share, width...  5.39 us
    ppermute x2, waiting for transfers between devices, swap_sides(): lax.ppermute(second, 'box', moves(1))  3.69 us
    pallas_call x1, Pallas kernels, body(): pl.pallas_call(functools.partial(pick_kernel, share), out_shape=jax.Shape...  2.61 us
    pallas_call x1, Pallas kernels, body(): pl.pallas_call(early_kernel, out_shape=[pltpu.VMEM((ext_rows, LANES), jnp...  2.28 us
  transfers between devices with their start and end apart: 8, of which 3 were waited for; matrix products, arithmetic and copies ran while one was open for 0% of the time, Pallas kernels for 24%

profile of v2, /device:TPU:2, one launch (start us, length us, event | category | flops | bytes accessed | tf_op | source)
XLA Modules:
  0.0 52.4 jit_solution(7658342041456595800)
XLA Ops:
  0.6 0.1 collective-permute-start
  0.7 2.6 %shard_map.77 = bf16[8,32,456]{2,1,0:T(8,128)(2,1)} custom-call(s32[4,8]{1,0:T(4,128)} %bitcast.14, bf16[16,456,128]{2,1,0:T(8,128)(2,1)} %bitcast.11), custom_call_target="tpu_custom_call" | custom-call | tf_op jit(solution)/shard_map/pallas_call | solution.py:441
  3.3 6.3 %all-to-all-start = ((bf16[8,32,456]{2,1,0:T(8,128)(2,1)}), bf16[8,32,456]{2,1,0:T(8,128)(2,1)S(1)}, u32[]{:S(2)}, u32[]{:S(2)}) async-start(bf16[8,32,456]{2,1,0:T(8,128)(2,1)} %shard_map.77), calls=%async_computation | async-start | bytes 524288 | tf_op jit(solution)/shard_map/all_to_all | solution.py:456
  9.7 1.6 %shard_map.78 = (bf16[128,1024]{1,0:T(8,128)(2,1)S(1)}, s32[8,1,1024]{2,1,0:T(1,128)S(1)}, s32[8,1,1024]{2,1,0:T(1,128)S(1)}, s32[16]{0:T(128)S(1)}) custom-call(s32[64,128]{1,0:T(8,128)} %bitcast.13, s32[8,1024]{1,0:T(8,128)} %points_ref), custom_call_target="tpu_custom_call" | custom-call | tf_op jit(solution)/shard_map/pallas_call | solution.py:128
  11.3 7.3 %all-to-all-done.imported_ref = bf16[8,32,456]{2,1,0:T(8,128)(2,1)S(1)} async-done(((bf16[8,32,456]{2,1,0:T(8,128)(2,1)}), bf16[8,32,456]{2,1,0:T(8,128)(2,1)S(1)}, u32[]{:S(2)}, u32[]{:S(2)}) %all-to-all-start) | async-done | bytes 233504 | tf_op jit(solution)/shard_map/all_to_all | solution.py:456
  18.6 0.0 collective-permute-done.rest_1_
  18.6 6.6 %shard_map.79 = (bf16[4,128,512]{2,1,0:T(8,128)(2,1)S(1)}, f32[2,32,128]{2,1,0:T(8,128)S(1)}, bf16[32,456,456]{2,1,0:T(8,128)(2,1)S(1)}) custom-call(bf16[8,32,456]{2,1,0:T(8,128)(2,1)S(1)} %all-to-all-done.imported_ref, bf16[128,1024]{1,0:T(8,128)(2,1)S(1)} %get-tuple-element.27.picks_ref, bf16[16,456,456]{2,1,0:T(8,128)(2,1)} %rest_0_.1, ...), custom_call_target="tpu_custom_call" | custom-call | flops 2181562368 | bytes 13307904 | tf_op jit(solution)/shard_map/pallas_call | solution.py:217
  25.3 1.6 %collective-permute-start.2 = (f32[2,32,128]{2,1,0:T(8,128)S(1)}, f32[2,32,128]{2,1,0:T(8,128)S(1)}, u32[]{:S(2)}, u32[]{:S(2)}) collective-permute-start(f32[2,32,128]{2,1,0:T(8,128)S(1)} %get-tuple-element.32), channel_id=1, source_target_pairs={{0,2},{1,3},{2,0},{3,1},{4,6},{5,7},{6,4},{7,5},{8,10},{9,11},{10,... | collective-permute-start | bytes 98312 | tf_op jit(solution)/shard_map/ppermute | solution.py:470
  26.8 0.5 collective-permute-start.1
  27.4 3.0 %shard_map.80 = (f32[4,128,512]{2,1,0:T(8,128)S(1)}, f32[2,32,128]{2,1,0:T(8,128)S(1)}) custom-call(bf16[8,32,456]{2,1,0:T(8,128)(2,1)S(1)} %all-to-all-done.imported_ref, bf16[128,1024]{1,0:T(8,128)(2,1)S(1)} %get-tuple-element.27.picks_ref, bf16[32,456,456]{2,1,0:T(8,128)(2,1)S(1)} %get-tuple-element.28.rest_0_), custom_call_target="tpu_custom_call" | custom-call | flops 2181562368 | bytes 13307904 | tf_op jit(solution)/shard_map/pallas_call | solution.py:217
  30.4 0.0 collective-permute-done.2.refs_1_
  30.4 0.0 slice-start
  30.4 0.0 slice-start.1
  30.4 0.0 slice-start.2
  30.4 0.7 %collective-permute-start.3 = (f32[32,128]{1,0:T(8,128)S(1)}, f32[32,128]{1,0:T(8,128)S(1)}, u32[]{:S(2)}, u32[]{:S(2)}) collective-permute-start(f32[32,128]{1,0:T(8,128)S(1)} %get-tuple-element.33), channel_id=1, source_target_pairs={{0,4},{8,12},{16,20},{24,28},{4,0},{12,8},{20,16},{28,24},{1,5},{9... | collective-permute-start | bytes 49160 | tf_op jit(solution)/shard_map/ppermute | solution.py:420
  31.1 3.2 %collective-permute-start.4 = (f32[32,128]{1,0:T(8,128)S(1)}, f32[32,128]{1,0:T(8,128)S(1)}, u32[]{:S(2)}, u32[]{:S(2)}) collective-permute-start(f32[32,128]{1,0:T(8,128)S(1)} %get-tuple-element.34), channel_id=1, source_target_pairs={{4,8},{12,16},{20,24},{8,4},{16,12},{24,20},{5,9},{13,17},{21,25},... | collective-permute-start | bytes 49160 | tf_op jit(solution)/shard_map/ppermute | solution.py:420
  34.3 0.0 collective-permute-done.3.first_ref
  34.3 3.7 %collective-permute-done.4.second_ref = f32[32,128]{1,0:T(8,128)S(1)} collective-permute-done((f32[32,128]{1,0:T(8,128)S(1)}, f32[32,128]{1,0:T(8,128)S(1)}, u32[]{:S(2)}, u32[]{:S(2)}) %collective-permute-start.4) | collective-permute-done | bytes 16416 | tf_op jit(solution)/shard_map/ppermute | solution.py:420
  38.0 1.2 %collective-permute-done.1 = bf16[4,128,512]{2,1,0:T(8,128)(2,1)S(1)} collective-permute-done((bf16[4,128,512]{2,1,0:T(8,128)(2,1)S(1)}, bf16[4,128,512]{2,1,0:T(8,128)(2,1)S(1)}, u32[]{:S(2)}, u32[]{:S(2)}) %collective-permute-start.1) | collective-permute-done | bytes 524320 | tf_op jit(solution)/shard_map/ppermute | solution.py:471
  39.2 2.3 %shard_map.82 = (f32[2112,128]{1,0:T(8,128)S(1)}, f32[2112,128]{1,0:T(8,128)S(1)}, f32[32,128]{1,0:T(8,128)S(1)}, f32[32,128]{1,0:T(8,128)S(1)}) custom-call(s32[16]{0:T(128)S(1)} %get-tuple-element.24.spans_ref, s32[8,1,1024]{2,1,0:T(1,128)S(1)} %get-tuple-element.25.code_ref, s32[8,1,1024]{2,1,0:T(1,128)S(1)} %get-tuple-element.26.lane_ref, ...), custom_call_target="tpu_custom_call" | custom-call | tf_op jit(solution)/shard_map/pallas_call | solution.py:479
  41.5 1.0 %collective-permute-start.5 = (f32[32,128]{1,0:T(8,128)S(1)}, f32[32,128]{1,0:T(8,128)S(1)}, u32[]{:S(2)}, u32[]{:S(2)}) collective-permute-start(f32[32,128]{1,0:T(8,128)S(1)} %get-tuple-element.38), channel_id=1, source_target_pairs={{0,4},{8,12},{16,20},{24,28},{4,0},{12,8},{20,16},{28,24},{1,5},{9... | collective-permute-start | bytes 49160 | tf_op jit(solution)/shard_map/ppermute | solution.py:420
  42.6 3.4 %collective-permute-start.6 = (f32[32,128]{1,0:T(8,128)S(1)}, f32[32,128]{1,0:T(8,128)S(1)}, u32[]{:S(2)}, u32[]{:S(2)}) collective-permute-start(f32[32,128]{1,0:T(8,128)S(1)} %get-tuple-element.39), channel_id=1, source_target_pairs={{4,8},{12,16},{20,24},{8,4},{16,12},{24,20},{5,9},{13,17},{21,25},... | collective-permute-start | bytes 49160 | tf_op jit(solution)/shard_map/ppermute | solution.py:420
  45.9 5.4 %shard_map.83 = (bf16[4,456,128]{2,1,0:T(8,128)(2,1)}, bf16[4,456,128]{2,1,0:T(8,128)(2,1)S(1)}, f32[64,128]{1,0:T(8,128)S(1)}) custom-call(s32[16]{0:T(128)S(1)} %get-tuple-element.24.spans_ref, s32[8,1,1024]{2,1,0:T(1,128)S(1)} %get-tuple-element.25.code_ref, s32[8,1,1024]{2,1,0:T(1,128)S(1)} %get-tuple-element.26.lane_ref, ...), custom_call_target="tpu_custom_call" | custom-call | flops 67108864 | bytes 16777216 | tf_op jit(solution)/shard_map/pallas_call | solution.py:494
  51.3 1.1 %shard_map.84 = bf16[4,456,128]{2,1,0:T(8,128)(2,1)} custom-call(f32[32,128]{1,0:T(8,128)S(1)} %collective-permute-done.5.first_ref, f32[32,128]{1,0:T(8,128)S(1)} %collective-permute-done.6.second_ref, f32[64,128]{1,0:T(8,128)S(1)} %get-tuple-element.40.rows_ref, bf16[4,456,128]{2,1,0:T(8,128)(2,1)S(1)} %get-tuple-element.41.corrected_ref), custom_call_target="tpu_custom_call" | custom-call | tf_op jit(solution)/shard_map/pallas_call | solution.py:515
  (9 shorter events, 0.0 us)
Async XLA Ops:
  0.6 18.0 %collective-permute-start = (bf16[16,456,456]{2,1,0:T(8,128)(2,1)}, bf16[16,456,456]{2,1,0:T(8,128)(2,1)}, u32[]{:S(2)}, u32[]{:S(2)}) collective-permute-start(bf16[16,456,456]{2,1,0:T(8,128)(2,1)} %rest_0_.1), channel_id=1, source_target_pairs={{1,0},{0,1},{3,2},{2,3},{5,4},{4,5},{7,6},{6,7},{9,8},{8,9},{11,10... | collective-permute-start | bytes 19961864 | tf_op jit(solution)/shard_map/ppermute | solution.py:438
  3.3 15.3 %all-to-all-start = ((bf16[8,32,456]{2,1,0:T(8,128)(2,1)}), bf16[8,32,456]{2,1,0:T(8,128)(2,1)S(1)}, u32[]{:S(2)}, u32[]{:S(2)}) async-start(bf16[8,32,456]{2,1,0:T(8,128)(2,1)} %shard_map.77), calls=%async_computation | async-start | bytes 524288 | tf_op jit(solution)/shard_map/all_to_all | solution.py:456
  25.3 5.1 %collective-permute-start.2 = (f32[2,32,128]{2,1,0:T(8,128)S(1)}, f32[2,32,128]{2,1,0:T(8,128)S(1)}, u32[]{:S(2)}, u32[]{:S(2)}) collective-permute-start(f32[2,32,128]{2,1,0:T(8,128)S(1)} %get-tuple-element.32), channel_id=1, source_target_pairs={{0,2},{1,3},{2,0},{3,1},{4,6},{5,7},{6,4},{7,5},{8,10},{9,11},{10,... | collective-permute-start | bytes 98312 | tf_op jit(solution)/shard_map/ppermute | solution.py:470
  26.8 12.4 %collective-permute-start.1 = (bf16[4,128,512]{2,1,0:T(8,128)(2,1)S(1)}, bf16[4,128,512]{2,1,0:T(8,128)(2,1)S(1)}, u32[]{:S(2)}, u32[]{:S(2)}) collective-permute-start(bf16[4,128,512]{2,1,0:T(8,128)(2,1)S(1)} %get-tuple-element.30), channel_id=1, source_target_pairs={{0,2},{1,3},{2,0},{3,1},{4,6},{5,7},{6,4},{7,5},{8,10},{9,11},{10,... | collective-permute-start | bytes 1572872 | tf_op jit(solution)/shard_map/ppermute | solution.py:471
  30.4 8.8 %slice-start = ((s8[16777216]{0:T(1024)(128)(4,1)}), s8[4194304]{0:T(1024)(128)(4,1)S(1)}, s32[]{:S(2)}) async-start(s8[16777216]{0:T(1024)(128)(4,1)} %bitcast.8), calls=%async_computation.1 | async-start | bytes 8388608
  30.4 8.8 %slice-start.1 = ((s8[16777216]{0:T(1024)(128)(4,1)}), s8[4194304]{0:T(1024)(128)(4,1)S(1)}, s32[]{:S(2)}) async-start(s8[16777216]{0:T(1024)(128)(4,1)} %bitcast.8), calls=%async_computation.2 | async-start | bytes 8388608
  30.4 8.8 %slice-start.2 = ((s8[16777216]{0:T(1024)(128)(4,1)}), s8[4194304]{0:T(1024)(128)(4,1)S(1)}, s32[]{:S(2)}) async-start(s8[16777216]{0:T(1024)(128)(4,1)} %bitcast.8), calls=%async_computation.3 | async-start | bytes 8388608
  30.4 8.8 %slice-start.3 = ((s8[16777216]{0:T(1024)(128)(4,1)}), s8[4194304]{0:T(1024)(128)(4,1)S(1)}, s32[]{:S(2)}) async-start(s8[16777216]{0:T(1024)(128)(4,1)} %bitcast.8), calls=%async_computation.4 | async-start | bytes 8388608
  30.4 3.9 %collective-permute-start.3 = (f32[32,128]{1,0:T(8,128)S(1)}, f32[32,128]{1,0:T(8,128)S(1)}, u32[]{:S(2)}, u32[]{:S(2)}) collective-permute-start(f32[32,128]{1,0:T(8,128)S(1)} %get-tuple-element.33), channel_id=1, source_target_pairs={{0,4},{8,12},{16,20},{24,28},{4,0},{12,8},{20,16},{28,24},{1,5},{9... | collective-permute-start | bytes 49160 | tf_op jit(solution)/shard_map/ppermute | solution.py:420
  31.1 6.9 %collective-permute-start.4 = (f32[32,128]{1,0:T(8,128)S(1)}, f32[32,128]{1,0:T(8,128)S(1)}, u32[]{:S(2)}, u32[]{:S(2)}) collective-permute-start(f32[32,128]{1,0:T(8,128)S(1)} %get-tuple-element.34), channel_id=1, source_target_pairs={{4,8},{12,16},{20,24},{8,4},{16,12},{24,20},{5,9},{13,17},{21,25},... | collective-permute-start | bytes 49160 | tf_op jit(solution)/shard_map/ppermute | solution.py:420
  41.5 9.8 %collective-permute-start.5 = (f32[32,128]{1,0:T(8,128)S(1)}, f32[32,128]{1,0:T(8,128)S(1)}, u32[]{:S(2)}, u32[]{:S(2)}) collective-permute-start(f32[32,128]{1,0:T(8,128)S(1)} %get-tuple-element.38), channel_id=1, source_target_pairs={{0,4},{8,12},{16,20},{24,28},{4,0},{12,8},{20,16},{28,24},{1,5},{9... | collective-permute-start | bytes 49160 | tf_op jit(solution)/shard_map/ppermute | solution.py:420
  42.6 8.8 %collective-permute-start.6 = (f32[32,128]{1,0:T(8,128)S(1)}, f32[32,128]{1,0:T(8,128)S(1)}, u32[]{:S(2)}, u32[]{:S(2)}) collective-permute-start(f32[32,128]{1,0:T(8,128)S(1)} %get-tuple-element.39), channel_id=1, source_target_pairs={{4,8},{12,16},{20,24},{8,4},{16,12},{24,20},{5,9},{13,17},{21,25},... | collective-permute-start | bytes 49160 | tf_op jit(solution)/shard_map/ppermute | solution.py:420

commit v3 on v2

--- a/solution.py
+++ b/solution.py
@@ -9,6 +9,7 @@
 
 RIM = 2
 SPAN = 8
+EARLY_OPS = 4
 LANES = 128
 NT = (((1,), (1,)), ((), ()))
 ANY = pl.BlockSpec(memory_space=pl.ANY)
@@ -46,7 +47,10 @@
     return inner, groups // inner
 
 
-def pick_kernel(share, ids_hbm, density_ref, out_ref, ids_ref, block, sems):
+def pick_kernel(share, swaps, load, ids_hbm, density_ref, operators_hbm, *rest):
+    out_refs, (ids_ref, block, sems) = rest[:-3], rest[-3:]
+    if load:
+        *out_refs, operators_ref = out_refs
     capacity, dests = ids_ref.shape
     cols, width, boxes = block.shape
     inner, outer = handled_groups()
@@ -63,10 +67,18 @@
         )
         copy.start()
         copies.append(copy)
+    if load:
+        operators_copy = pltpu.make_async_copy(
+            operators_hbm.at[pl.ds(0, load)], operators_ref, sems.at[outer + 1]
+        )
+        operators_copy.start()
     ids_copy.wait()
     rows = dests * cols * capacity
     row = iota((rows, boxes), 0)
-    pair = div(row, cols * capacity) * capacity + mod(row, capacity)
+    dest = div(row, cols * capacity)
+    if swaps:
+        dest = dest ^ lax.axis_index("box")
+    pair = dest * capacity + mod(row, capacity)
     column = mod(div(row, capacity), cols)
 
     def place(k, wanted):
@@ -87,12 +99,74 @@
         total = total + lax.dot_general(
             chosen, block[c], NT, preferred_element_type=jnp.float32
         )
-    out_ref[...] = total.astype(out_ref.dtype).reshape(out_ref.shape)
+    total = total.astype(out_refs[0].dtype).reshape(dests, cols * capacity, width)
+    if not swaps:
+        out_refs[0][...] = total
+        return
+    for k, ref in enumerate(out_refs[:-1]):
+        ref[...] = total[2 * k]
+        out_refs[-1][k] = total[2 * k + 1]
+    if load:
+        operators_copy.wait()
+
+
+def pick_call(export_ids, density, translations, share, swaps, load):
+    boxes, _, width = density.shape
+    _, sources, capacity = export_ids.shape
+    _, outer = handled_groups()
+    block = (outer * share * capacity, width)
+    if swaps:
+        shapes = [block] * (sources // 2) + [(sources // 2,) + block]
+    else:
+        shapes = [(sources,) + block]
+    return pl.pallas_call(
+        functools.partial(pick_kernel, share, swaps, load),
+        out_shape=[jax.ShapeDtypeStruct(shape, density.dtype) for shape in shapes]
+        + [pltpu.VMEM((load,) + translations.shape[1:], translations.dtype)] * (load > 0),
+        in_specs=[ANY] * 3,
+        out_specs=[VMEM] * (len(shapes) + (load > 0)),
+        scratch_shapes=[
+            pltpu.SMEM((capacity, sources), jnp.int32),
+            pltpu.VMEM((outer * share, width, boxes), density.dtype),
+            pltpu.SemaphoreType.DMA((outer + 2,)),
+        ],
+        compiler_params=params(8),
+    )(
+        pltpu.with_memory_space_constraint(export_ids[0].T, pltpu.HBM),
+        pltpu.with_memory_space_constraint(jnp.transpose(density, (1, 2, 0)), pltpu.HBM),
+        pltpu.with_memory_space_constraint(translations, pltpu.HBM),
+    )
+
+
+def swap_blocks(outgoing):
+    *keeps, send = outgoing
+    count = lax.axis_size("box")
+
+    def swap(x, mask):
+        return lax.ppermute(x, "box", [(i, i ^ mask) for i in range(count)])
+
+    received = swap(send, 1)
+    blocks = [keeps[0], received]
+    for k in range(1, len(keeps)):
+        blocks += [swap(keeps[k], 2 * k), swap(received[k], 2 * k)]
+    return blocks
 
 
 def prepare_kernel(
-    slots, tiles, width, local_ops, slots_ref, points_ref, picks_ref, code_ref, lane_ref, spans_ref, hot
+    slots, tiles, width, local_ops, slots_hbm, points_hbm, operators_hbm,
+    picks_ref, code_ref, lane_ref, spans_ref, *rest
 ):
+    *operators_refs, slots_ref, points_ref, hot, sems = rest
+    copies = [
+        pltpu.make_async_copy(slots_hbm, slots_ref, sems.at[0]),
+        pltpu.make_async_copy(points_hbm, points_ref, sems.at[1]),
+    ]
+    for ref in operators_refs:
+        part = operators_hbm.at[pl.ds(local_ops - ref.shape[0], ref.shape[0])]
+        copies.append(pltpu.make_async_copy(part, ref, sems.at[2]))
+    for copy in copies:
+        copy.start()
+    copies[0].wait()
     boxes = slots_ref.shape[1]
     patches = code_ref.shape[0]
     inner, outer = handled_groups()
@@ -105,6 +179,7 @@
             at = (half * local_ops + o) * slots
             hot[at : at + slots, :] = jnp.where(picked, 1.0, 0.0).astype(jnp.bfloat16)
     picks_ref[...] = hot[...].T
+    copies[1].wait()
     local = points_ref[...] - (lax.axis_index("box") * boxes - RIM) * width
     at_box = ((local.astype(jnp.float32) + 0.5) * (1.0 / width)).astype(jnp.int32)
     at_point = local - at_box * width
@@ -118,69 +193,87 @@
         lane_ref[p] = lane[p : p + 1]
         spans_ref[p] = jnp.min(lowest[p : p + 1])
         spans_ref[patches + p] = jnp.min(highest[p : p + 1])
-
-
-def prepare_call(slots_t, patch_points, slots, tiles, width, local_ops):
+    for copy in copies[2:]:
+        copy.wait()
+
+
+def prepare_call(slots_t, patch_points, translations, load, slots, tiles):
+    local_ops, width, _ = translations.shape
     inner, _ = handled_groups()
     boxes = slots_t.shape[1]
     patches, points = patch_points.shape
     all_slots = inner * local_ops * slots
+    keep = pltpu.VMEM if load else jax.ShapeDtypeStruct
     return pl.pallas_call(
         functools.partial(prepare_kernel, slots, tiles, width, local_ops),
         out_shape=[
-            jax.ShapeDtypeStruct((boxes, all_slots), jnp.bfloat16),
-            jax.ShapeDtypeStruct((patches, 1, points), jnp.int32),
-            jax.ShapeDtypeStruct((patches, 1, points), jnp.int32),
+            keep((boxes, all_slots), jnp.bfloat16),
+            keep((patches, 1, points), jnp.int32),
+            keep((patches, 1, points), jnp.int32),
             jax.ShapeDtypeStruct((2 * patches,), jnp.int32),
+        ]
+        + [pltpu.VMEM((load, width, width), translations.dtype)] * (load > 0),
+        in_specs=[ANY] * 3,
+        out_specs=[VMEM] * 3 + [SMEM] + [VMEM] * (load > 0),
+        scratch_shapes=[
+            pltpu.VMEM(slots_t.shape, slots_t.dtype),
+            pltpu.VMEM(patch_points.shape, patch_points.dtype),
+            pltpu.VMEM((all_slots, boxes), jnp.bfloat16),
+            pltpu.SemaphoreType.DMA((3,)),
         ],
-        in_specs=[VMEM] * 2,
-        out_specs=[VMEM] * 3 + [SMEM],
-        scratch_shapes=[pltpu.VMEM((all_slots, boxes), jnp.bfloat16)],
         compiler_params=params(8),
     )(
         pltpu.with_memory_space_constraint(slots_t, pltpu.HBM),
         pltpu.with_memory_space_constraint(patch_points, pltpu.HBM),
+        pltpu.with_memory_space_constraint(translations, pltpu.HBM),
     )
 
 
-def field_kernel(share, capacity, group, fetch, imported_ref, picks_ref, *rest):
-    if fetch:
-        sources_refs, (out_ref, edge_ref, operators_ref, terms, sems) = rest[:-5], rest[-5:]
+def field_kernel(share, capacity, group, arrivals, ready, pending, *refs):
+    imported_refs, picks_ref, rest = refs[:arrivals], refs[arrivals], refs[arrivals + 1 :]
+    *operator_refs, out_ref, edge_ref, terms, fetched, sems = rest
+    ready_refs, pending_refs = operator_refs[: len(ready)], operator_refs[len(ready) :]
+    work = [(at + i, ref, i, None) for at, ref in zip(ready, ready_refs) for i in range(ref.shape[0])]
+    filled = 0
+    for (start, count, at), ref in zip(pending, pending_refs):
+        chunk = 4 if count % 4 == 0 else 1
+        for i in range(0, count, chunk):
+            copy = pltpu.make_async_copy(
+                ref.at[pl.ds(start + i, chunk)], fetched.at[pl.ds(filled, chunk)], sems.at[filled]
+            )
+            copy.start()
+            for k in range(chunk):
+                work.append((at + i + k, fetched, filled + k, None if k else copy))
+            filled += chunk
+    if arrivals == 1:
+        sources, per_source, width = imported_refs[0].shape
+        flat = imported_refs[0][...].reshape(sources * per_source, width)
+        swapped = 0
     else:
-        sources_refs, (operators_ref, out_ref, edge_ref, terms) = (), rest
-    sources, per_source, width = imported_ref.shape
-    all_ops = operators_ref.shape[0]
+        sources = arrivals
+        per_source, width = imported_refs[0].shape
+        pieces = [ref[0] if i == 1 else ref[...] for i, ref in enumerate(imported_refs)]
+        flat = jnp.concatenate(pieces, axis=0)
+        swapped = lax.axis_index("box")
     boxes = picks_ref.shape[0]
     slots = sources * capacity
     stride = terms.shape[1] // share
     tiles = stride // LANES
-    copies, chunk = {}, 1
-    for ref in sources_refs:
-        local_ops = ref.shape[0]
-        chunk = 4 if local_ops % 4 == 0 else 1
-        for at in range(0, local_ops, chunk):
-            to = len(copies) * chunk
-            copy = pltpu.make_async_copy(
-                ref.at[pl.ds(at, chunk)], operators_ref.at[pl.ds(to, chunk)], sems.at[len(copies)]
-            )
-            copy.start()
-            copies[to] = copy
     arrived = sources * per_source
     shape = (share * slots, arrived)
     row = iota(shape, 0)
     slot = mod(row, slots)
     origin = (
-        div(slot, capacity) * per_source
+        (div(slot, capacity) ^ swapped) * per_source
         + (group * share + div(row, slots)) * capacity
         + mod(slot, capacity)
     )
     order = jnp.where(origin == iota(shape, 1), 1.0, 0.0).astype(jnp.bfloat16)
-    flat = imported_ref[...].reshape(arrived, width)
     ordered = jnp.dot(order, flat, preferred_element_type=jnp.float32).astype(jnp.bfloat16)
-    for o in range(all_ops):
-        if o in copies:
-            copies[o].wait()
-        term = jnp.dot(ordered, operators_ref[o], preferred_element_type=jnp.float32)
+    for o, ref, i, copy in work:
+        if copy is not None:
+            copy.wait()
+        term = jnp.dot(ordered, ref[i], preferred_element_type=jnp.float32)
         term = term.astype(jnp.bfloat16)
         for c in range(share):
             terms[o * slots : (o + 1) * slots, c * stride : c * stride + width] = term[
@@ -197,36 +290,41 @@
             edge_ref[1, to, :] = total[boxes - RIM :, at : at + LANES].astype(jnp.float32)
 
 
-def field_call(imported, picks, operators, share, capacity, group, dtype):
-    sources, _, width = imported.shape
+def field_call(imported, picks, ready, pending, share, capacity, group, dtype):
+    width = imported[0].shape[-1]
     boxes, all_slots = picks.shape
-    all_ops = all_slots // (sources * capacity)
+    arrivals = len(imported)
     stride = round_up(width, LANES)
-    fetch = isinstance(operators, tuple)
-    out_shape = [
-        jax.ShapeDtypeStruct((share, boxes, stride), dtype),
-        jax.ShapeDtypeStruct((2, RIM * share * (stride // LANES), LANES), jnp.float32),
-    ]
-    scratch = [pltpu.VMEM((all_slots, share * stride), jnp.bfloat16)]
-    if fetch:
-        out_shape.append(pltpu.VMEM((all_ops, width, width), operators[0].dtype))
-        scratch.append(pltpu.SemaphoreType.DMA((all_ops,)))
-        operators = [pltpu.with_memory_space_constraint(o, pltpu.HBM) for o in operators]
-    else:
-        operators = [pltpu.with_memory_space_constraint(operators, pltpu.VMEM)]
+    fetched = sum(count for _, _, count, _ in pending)
+    held = all_slots * share * stride * 2 + fetched * width * stride * 2
     return pl.pallas_call(
-        functools.partial(field_kernel, share, capacity, group, fetch),
-        out_shape=out_shape,
-        in_specs=[VMEM] * 2 + [ANY if fetch else VMEM] * len(operators),
-        out_specs=[VMEM] * len(out_shape),
-        scratch_shapes=scratch,
-        compiler_params=params(8 + all_slots * share * stride * 2 // (1 << 20)),
+        functools.partial(
+            field_kernel, share, capacity, group, arrivals,
+            [at for _, at in ready], [entry[1:] for entry in pending],
+        ),
+        out_shape=[
+            jax.ShapeDtypeStruct((share, boxes, stride), dtype),
+            jax.ShapeDtypeStruct((2, RIM * share * (stride // LANES), LANES), jnp.float32),
+        ],
+        in_specs=[VMEM] * (arrivals + 1 + len(ready)) + [ANY] * len(pending),
+        out_specs=[VMEM, VMEM],
+        scratch_shapes=[
+            pltpu.VMEM((all_slots, share * stride), jnp.bfloat16),
+            pltpu.VMEM((max(fetched, 1), width, width), jnp.bfloat16),
+            pltpu.SemaphoreType.DMA((max(fetched, 1),)),
+        ],
+        compiler_params=params(8 + held // (1 << 20)),
         cost_estimate=pl.CostEstimate(
             flops=2 * all_slots * share * width * (width + boxes),
-            bytes_accessed=2 * all_ops * width * width,
+            bytes_accessed=all_slots * share * stride * 2,
             transcendentals=0,
         ),
-    )(imported, picks, *operators)
+    )(
+        *imported,
+        picks,
+        *[pltpu.with_memory_space_constraint(array, pltpu.VMEM) for array, _ in ready],
+        *[pltpu.with_memory_space_constraint(array, pltpu.HBM) for array, *_ in pending],
+    )
 
 
 def edge_kernel(*refs):
@@ -437,39 +535,39 @@
         moves = [(h * inner + (k + i) % inner, h * inner + k) for h, k in places]
         others.append(lax.ppermute(translations, "col", moves))
 
-    cols = outer * share
-    outgoing = pl.pallas_call(
-        functools.partial(pick_kernel, share),
-        out_shape=jax.ShapeDtypeStruct((sources, cols * capacity, width), jnp.bfloat16),
-        in_specs=[ANY, ANY],
-        out_specs=VMEM,
-        scratch_shapes=[
-            pltpu.SMEM((capacity, sources), jnp.int32),
-            pltpu.VMEM((cols, width, boxes), jnp.bfloat16),
-            pltpu.SemaphoreType.DMA((outer + 1,)),
-        ],
-        compiler_params=params(8),
-    )(
-        pltpu.with_memory_space_constraint(export_ids[0].T, pltpu.HBM),
-        pltpu.with_memory_space_constraint(jnp.transpose(density, (1, 2, 0)), pltpu.HBM),
+    swaps = sources <= 16 and sources & (sources - 1) == 0
+    local_ops = translations.shape[0]
+    early = EARLY_OPS if swaps else 0
+    load = local_ops - early if swaps else 0
+    outgoing = pick_call(export_ids, density, translations, share, swaps, early)
+    ready = []
+    if early:
+        *outgoing, first_ops = outgoing
+        ready.append((first_ops, 0))
+    if swaps:
+        imported = swap_blocks(outgoing)
+    else:
+        imported = [lax.all_to_all(outgoing[0], "box", split_axis=0, concat_axis=0, tiled=True)]
+
+    _, *later = lax.optimization_barrier(
+        (outgoing[-1], list_slot.T, patch_points, translations)
     )
-    imported = lax.all_to_all(outgoing, "box", split_axis=0, concat_axis=0, tiled=True)
-
-    _, *prepared = lax.optimization_barrier((outgoing, list_slot.T, patch_points))
-    picks, code, lane, spans = prepare_call(
-        *prepared, sources * capacity, tiles, width, translations.shape[0]
-    )
-    operators = (translations, *others)
+    picks, code, lane, spans, *loaded = prepare_call(*later, load, sources * capacity, tiles)
+    arrived = [(other, (i + 1) * local_ops) for i, other in enumerate(others)]
+    pending = []
+    if swaps:
+        ready += [(array, early) for array in loaded] + arrived
+    else:
+        pending = [(array, 0, local_ops, at) for array, at in [(translations, 0)] + arrived]
     parts, edges = [], []
     for j in range(1, outer):
-        part, edge, *loaded = field_call(
-            imported, picks, operators, share, capacity, j, jnp.bfloat16
+        part, edge = field_call(
+            imported, picks, ready, pending, share, capacity, j, jnp.bfloat16
         )
-        operators = loaded[0] if loaded else operators
         moves = [(h * inner + k, ((h + j) % outer) * inner + k) for h, k in places]
         edges.append(lax.ppermute(edge, "col", moves))
         parts.append(lax.ppermute(part, "col", moves))
-    own, edge = field_call(imported, picks, operators, share, capacity, 0, jnp.float32)[:2]
+    own, edge = field_call(imported, picks, ready, pending, share, capacity, 0, jnp.float32)
     first, second = swap_sides(*edge_call(edge, *edges))
     received = jnp.stack(parts)
 

time: 53.4 us -> 47.8 us (0.90)
  the two profiles are of different devices: /device:TPU:2 before, /device:TPU:10 now
where the time goes in v3:
time: 47.8 us; the launch traced here: 47.4 us
  starting transfers between devices  21 us (44%)
  Pallas kernels  20 us (42%)
  waiting for transfers between devices  5.6 us (12%)
  between operations  0.82 us (2%)
    ppermute x2, starting transfers between devices, swap_sides(): lax.ppermute(second, 'box', moves(1))  9.29 us
    ppermute x7, starting transfers between devices, swap(): return lax.ppermute(x, 'box', [(i, i ^ mask) for i in range(count)])  8.28 us
    pallas_call x2, Pallas kernels, field_call(): pl.pallas_call(functools.partial(field_kernel, share, capacity, group, ar...  6.05 us
    pallas_call x1, Pallas kernels, body(): pl.pallas_call(late_kernel, out_shape=[jax.ShapeDtypeStruct((share, width...  5.39 us
    pallas_call x1, Pallas kernels, prepare_call(): pl.pallas_call(functools.partial(prepare_kernel, slots, tiles, width, loc...  3.25 us
    pallas_call x1, Pallas kernels, body(): pl.pallas_call(early_kernel, out_shape=[pltpu.VMEM((ext_rows, LANES), jnp...  2.28 us
    pallas_call x1, Pallas kernels, pick_call(): pl.pallas_call(functools.partial(pick_kernel, share, swaps, load), out_sh...  1.92 us
    ppermute x1, waiting for transfers between devices, body(): parts.append(lax.ppermute(part, 'col', moves))  1.88 us
  transfers between devices with their start and end apart: 14, of which 3 were waited for; matrix products, arithmetic and copies ran while one was open for 0% of the time, Pallas kernels for 29%

profile of v3, /device:TPU:10, one launch (start us, length us, event | category | flops | bytes accessed | tf_op | source)
XLA Modules:
  0.0 47.4 jit_solution(14310624546152804310)
XLA Ops:
  0.6 0.1 collective-permute-start.7
  0.7 1.9 %shard_map.77 = (bf16[32,456]{1,0:T(8,128)(2,1)S(1)}, bf16[32,456]{1,0:T(8,128)(2,1)S(1)}, bf16[32,456]{1,0:T(8,128)(2,1)S(1)}, bf16[32,456]{1,0:T(8,128)(2,1)S(...) custom-call(s32[4,8]{1,0:T(4,128)} %bitcast.20, bf16[16,456,128]{2,1,0:T(8,128)(2,1)} %bitcast.17, ...), custom_call_target="tpu_custom_call" | custom-call | tf_op jit(solution)/shard_map/pallas_call | solution.py:122
  2.6 0.6 %collective-permute-start = (bf16[4,32,456]{2,1,0:T(8,128)(2,1)S(1)}, bf16[4,32,456]{2,1,0:T(8,128)(2,1)S(1)}, u32[]{:S(2)}, u32[]{:S(2)}) collective-permute-start(bf16[4,32,456]{2,1,0:T(8,128)(2,1)S(1)} %get-tuple-element.29), channel_id=1, source_target_pairs={{0,4},{4,0},{8,12},{12,8},{16,20},{20,16},{24,28},{28,24},{1,5},{5... | collective-permute-start | bytes 350216 | tf_op jit(solution)/shard_map/ppermute | solution.py:146
  3.2 3.0 %collective-permute-start.3 = (bf16[32,456]{1,0:T(8,128)(2,1)S(1)}, bf16[32,456]{1,0:T(8,128)(2,1)S(1)}, u32[]{:S(2)}, u32[]{:S(2)}) collective-permute-start(bf16[32,456]{1,0:T(8,128)(2,1)S(1)} %get-tuple-element.38), channel_id=1, source_target_pairs={{0,16},{4,20},{8,24},{12,28},{16,0},{20,4},{24,8},{28,12},{1,17},{... | collective-permute-start | bytes 87560 | tf_op jit(solution)/shard_map/ppermute | solution.py:146
  6.3 0.4 collective-permute-start.5
  6.7 1.9 %collective-permute-done.refs_1_ = bf16[4,32,456]{2,1,0:T(8,128)(2,1)S(1)} collective-permute-done((bf16[4,32,456]{2,1,0:T(8,128)(2,1)S(1)}, bf16[4,32,456]{2,1,0:T(8,128)(2,1)S(1)}, u32[]{:S(2)}, u32[]{:S(2)}) %collective-permute-start) | collective-permute-done | bytes 116768 | tf_op jit(solution)/shard_map/ppermute | solution.py:146
  8.6 1.6 %collective-permute-start.6 = (bf16[32,456]{1,0:T(8,128)(2,1)S(1)}, bf16[32,456]{1,0:T(8,128)(2,1)S(1)}, u32[]{:S(2)}, u32[]{:S(2)}) collective-permute-start(bf16[32,456]{1,0:T(8,128)(2,1)S(1)} %get-tuple-element.56), channel_id=1, source_target_pairs={{0,24},{4,28},{8,16},{12,20},{16,8},{20,12},{24,0},{28,4},{1,25},{... | collective-permute-start | bytes 87560 | tf_op jit(solution)/shard_map/ppermute | solution.py:146
  10.2 1.2 %collective-permute-start.4 = (bf16[32,456]{1,0:T(8,128)(2,1)S(1)}, bf16[32,456]{1,0:T(8,128)(2,1)S(1)}, u32[]{:S(2)}, u32[]{:S(2)}) collective-permute-start(bf16[32,456]{1,0:T(8,128)(2,1)S(1)} %get-tuple-element.57), channel_id=1, source_target_pairs={{0,16},{4,20},{8,24},{12,28},{16,0},{20,4},{24,8},{28,12},{1,17},{... | collective-permute-start | bytes 87560 | tf_op jit(solution)/shard_map/ppermute | solution.py:146
  11.5 1.3 %collective-permute-start.2 = (bf16[32,456]{1,0:T(8,128)(2,1)S(1)}, bf16[32,456]{1,0:T(8,128)(2,1)S(1)}, u32[]{:S(2)}, u32[]{:S(2)}) collective-permute-start(bf16[32,456]{1,0:T(8,128)(2,1)S(1)} %get-tuple-element.58), channel_id=1, source_target_pairs={{0,8},{4,12},{8,0},{12,4},{16,24},{20,28},{24,16},{28,20},{1,9},{5... | collective-permute-start | bytes 87560 | tf_op jit(solution)/shard_map/ppermute | solution.py:146
  12.8 3.2 %shard_map.78 = (bf16[128,1024]{1,0:T(8,128)(2,1)S(1)}, s32[8,1,1024]{2,1,0:T(1,128)S(1)}, s32[8,1,1024]{2,1,0:T(1,128)S(1)}, s32[16]{0:T(128)S(1)}, bf16[12,456,456]{2,1,0:T(8,128)(2,1)S(1)}) custom-call(s32[64,128]{1,0:T(8,128)} %bitcast.19, s32[8,1024]{1,0:T(8,128)} %points_hbm, bf16[16,456,456]{2,1,0:T(8,128)(2,1)} %operators_hbm.2), custom_call_target="tpu_custom_call" | custom-call | tf_op jit(solution)/shard_map/pallas_call | solution.py:207
  16.1 3.0 %shard_map.80 = (bf16[4,128,512]{2,1,0:T(8,128)(2,1)S(1)}, f32[2,32,128]{2,1,0:T(8,128)S(1)}) custom-call(bf16[32,456]{1,0:T(8,128)(2,1)S(1)} %get-tuple-element.36.refs_0_, bf16[4,32,456]{2,1,0:T(8,128)(2,1)S(1)} %collective-permute-done.refs_1_, bf16[32,456]{1,0:T(8,128)(2,1)S(1)} %collective-permute-done.1.refs_2_, ...), custom_call_target="tpu_custom_call" | custom-call | flops 2181562368 | bytes 4194304 | tf_op jit(solution)/shard_map/pallas_call | solution.py:300
  19.1 1.6 %collective-permute-start.9 = (f32[2,32,128]{2,1,0:T(8,128)S(1)}, f32[2,32,128]{2,1,0:T(8,128)S(1)}, u32[]{:S(2)}, u32[]{:S(2)}) collective-permute-start(f32[2,32,128]{2,1,0:T(8,128)S(1)} %get-tuple-element.46), channel_id=1, source_target_pairs={{0,2},{1,3},{2,0},{3,1},{4,6},{5,7},{6,4},{7,5},{8,10},{9,11},{10,... | collective-permute-start | bytes 98312 | tf_op jit(solution)/shard_map/ppermute | solution.py:568
  20.7 0.5 %collective-permute-start.8 = (bf16[4,128,512]{2,1,0:T(8,128)(2,1)S(1)}, bf16[4,128,512]{2,1,0:T(8,128)(2,1)S(1)}, u32[]{:S(2)}, u32[]{:S(2)}) collective-permute-start(bf16[4,128,512]{2,1,0:T(8,128)(2,1)S(1)} %get-tuple-element.44), channel_id=1, source_target_pairs={{0,2},{1,3},{2,0},{3,1},{4,6},{5,7},{6,4},{7,5},{8,10},{9,11},{10,... | collective-permute-start | bytes 1572872 | tf_op jit(solution)/shard_map/ppermute | solution.py:569
  21.2 3.0 %shard_map.79 = (f32[4,128,512]{2,1,0:T(8,128)S(1)}, f32[2,32,128]{2,1,0:T(8,128)S(1)}) custom-call(bf16[32,456]{1,0:T(8,128)(2,1)S(1)} %get-tuple-element.36.refs_0_, bf16[4,32,456]{2,1,0:T(8,128)(2,1)S(1)} %collective-permute-done.refs_1_, bf16[32,456]{1,0:T(8,128)(2,1)S(1)} %collective-permute-done.1.refs_2_, ...), custom_call_target="tpu_custom_call" | custom-call | flops 2181562368 | bytes 4194304 | tf_op jit(solution)/shard_map/pallas_call | solution.py:300
  24.3 0.0 slice-start
  24.4 0.6 %collective-permute-start.10 = (f32[32,128]{1,0:T(8,128)S(1)}, f32[32,128]{1,0:T(8,128)S(1)}, u32[]{:S(2)}, u32[]{:S(2)}) collective-permute-start(f32[32,128]{1,0:T(8,128)S(1)} %get-tuple-element.47), channel_id=1, source_target_pairs={{0,4},{8,12},{16,20},{24,28},{4,0},{12,8},{20,16},{28,24},{1,5},{9... | collective-permute-start | bytes 49160 | tf_op jit(solution)/shard_map/ppermute | solution.py:518
  25.0 5.1 %collective-permute-start.11 = (f32[32,128]{1,0:T(8,128)S(1)}, f32[32,128]{1,0:T(8,128)S(1)}, u32[]{:S(2)}, u32[]{:S(2)}) collective-permute-start(f32[32,128]{1,0:T(8,128)S(1)} %get-tuple-element.48), channel_id=1, source_target_pairs={{4,8},{12,16},{20,24},{8,4},{16,12},{24,20},{5,9},{13,17},{21,25},... | collective-permute-start | bytes 49160 | tf_op jit(solution)/shard_map/ppermute | solution.py:518
  30.0 1.8 %collective-permute-done.11.second_ref = f32[32,128]{1,0:T(8,128)S(1)} collective-permute-done((f32[32,128]{1,0:T(8,128)S(1)}, f32[32,128]{1,0:T(8,128)S(1)}, u32[]{:S(2)}, u32[]{:S(2)}) %collective-permute-start.11) | collective-permute-done | bytes 16416 | tf_op jit(solution)/shard_map/ppermute | solution.py:518
  31.9 1.9 %collective-permute-done.8 = bf16[4,128,512]{2,1,0:T(8,128)(2,1)S(1)} collective-permute-done((bf16[4,128,512]{2,1,0:T(8,128)(2,1)S(1)}, bf16[4,128,512]{2,1,0:T(8,128)(2,1)S(1)}, u32[]{:S(2)}, u32[]{:S(2)}) %collective-permute-start.8) | collective-permute-done | bytes 524320 | tf_op jit(solution)/shard_map/ppermute | solution.py:569
  33.8 2.3 %shard_map.82 = (f32[2112,128]{1,0:T(8,128)S(1)}, f32[2112,128]{1,0:T(8,128)S(1)}, f32[32,128]{1,0:T(8,128)S(1)}, f32[32,128]{1,0:T(8,128)S(1)}) custom-call(s32[16]{0:T(128)S(1)} %get-tuple-element.33.spans_ref, s32[8,1,1024]{2,1,0:T(1,128)S(1)} %get-tuple-element.34.code_ref, s32[8,1,1024]{2,1,0:T(1,128)S(1)} %get-tuple-element.35.lane_ref, ...), custom_call_target="tpu_custom_call" | custom-call | tf_op jit(solution)/shard_map/pallas_call | solution.py:577
  36.1 0.6 %collective-permute-start.12 = (f32[32,128]{1,0:T(8,128)S(1)}, f32[32,128]{1,0:T(8,128)S(1)}, u32[]{:S(2)}, u32[]{:S(2)}) collective-permute-start(f32[32,128]{1,0:T(8,128)S(1)} %get-tuple-element.52), channel_id=1, source_target_pairs={{0,4},{8,12},{16,20},{24,28},{4,0},{12,8},{20,16},{28,24},{1,5},{9... | collective-permute-start | bytes 49160 | tf_op jit(solution)/shard_map/ppermute | solution.py:518
  36.7 4.2 %collective-permute-start.13 = (f32[32,128]{1,0:T(8,128)S(1)}, f32[32,128]{1,0:T(8,128)S(1)}, u32[]{:S(2)}, u32[]{:S(2)}) collective-permute-start(f32[32,128]{1,0:T(8,128)S(1)} %get-tuple-element.53), channel_id=1, source_target_pairs={{4,8},{12,16},{20,24},{8,4},{16,12},{24,20},{5,9},{13,17},{21,25},... | collective-permute-start | bytes 49160 | tf_op jit(solution)/shard_map/ppermute | solution.py:518
  40.9 5.4 %shard_map.83 = (bf16[4,456,128]{2,1,0:T(8,128)(2,1)}, bf16[4,456,128]{2,1,0:T(8,128)(2,1)S(1)}, f32[64,128]{1,0:T(8,128)S(1)}) custom-call(s32[16]{0:T(128)S(1)} %get-tuple-element.33.spans_ref, s32[8,1,1024]{2,1,0:T(1,128)S(1)} %get-tuple-element.34.code_ref, s32[8,1,1024]{2,1,0:T(1,128)S(1)} %get-tuple-element.35.lane_ref, ...), custom_call_target="tpu_custom_call" | custom-call | flops 67108864 | bytes 16777216 | tf_op jit(solution)/shard_map/pallas_call | solution.py:592
  46.3 1.1 %shard_map.84 = bf16[4,456,128]{2,1,0:T(8,128)(2,1)} custom-call(f32[32,128]{1,0:T(8,128)S(1)} %collective-permute-done.12.first_ref, f32[32,128]{1,0:T(8,128)S(1)} %collective-permute-done.13.second_ref, f32[64,128]{1,0:T(8,128)S(1)} %get-tuple-element.54.rows_ref, bf16[4,456,128]{2,1,0:T(8,128)(2,1)S(1)} %get-tuple-element.55.corrected_ref), custom_call_target="tpu_custom_call" | custom-call | tf_op jit(solution)/shard_map/pallas_call | solution.py:613
  (22 shorter events, 0.1 us)
Async XLA Ops:
  0.6 15.5 %collective-permute-start.7 = (bf16[16,456,456]{2,1,0:T(8,128)(2,1)}, bf16[16,456,456]{2,1,0:T(8,128)(2,1)S(1)}, u32[]{:S(2)}, u32[]{:S(2)}) collective-permute-start(bf16[16,456,456]{2,1,0:T(8,128)(2,1)} %operators_hbm.2), channel_id=1, source_target_pairs={{1,0},{0,1},{3,2},{2,3},{5,4},{4,5},{7,6},{6,7},{9,8},{8,9},{11,10... | collective-permute-start | bytes 19961864 | tf_op jit(solution)/shard_map/ppermute | solution.py:536
  2.6 5.9 %collective-permute-start = (bf16[4,32,456]{2,1,0:T(8,128)(2,1)S(1)}, bf16[4,32,456]{2,1,0:T(8,128)(2,1)S(1)}, u32[]{:S(2)}, u32[]{:S(2)}) collective-permute-start(bf16[4,32,456]{2,1,0:T(8,128)(2,1)S(1)} %get-tuple-element.29), channel_id=1, source_target_pairs={{0,4},{4,0},{8,12},{12,8},{16,20},{20,16},{24,28},{28,24},{1,5},{5... | collective-permute-start | bytes 350216 | tf_op jit(solution)/shard_map/ppermute | solution.py:146
  3.2 7.0 %collective-permute-start.1 = (bf16[32,456]{1,0:T(8,128)(2,1)S(1)}, bf16[32,456]{1,0:T(8,128)(2,1)S(1)}, u32[]{:S(2)}, u32[]{:S(2)}) collective-permute-start(bf16[32,456]{1,0:T(8,128)(2,1)S(1)} %get-tuple-element.37), channel_id=1, source_target_pairs={{0,8},{4,12},{8,0},{12,4},{16,24},{20,28},{24,16},{28,20},{1,9},{5... | collective-permute-start | bytes 87560 | tf_op jit(solution)/shard_map/ppermute | solution.py:146
  3.2 8.2 %collective-permute-start.3 = (bf16[32,456]{1,0:T(8,128)(2,1)S(1)}, bf16[32,456]{1,0:T(8,128)(2,1)S(1)}, u32[]{:S(2)}, u32[]{:S(2)}) collective-permute-start(bf16[32,456]{1,0:T(8,128)(2,1)S(1)} %get-tuple-element.38), channel_id=1, source_target_pairs={{0,16},{4,20},{8,24},{12,28},{16,0},{20,4},{24,8},{28,12},{1,17},{... | collective-permute-start | bytes 87560 | tf_op jit(solution)/shard_map/ppermute | solution.py:146
  6.3 9.8 %collective-permute-start.5 = (bf16[32,456]{1,0:T(8,128)(2,1)S(1)}, bf16[32,456]{1,0:T(8,128)(2,1)S(1)}, u32[]{:S(2)}, u32[]{:S(2)}) collective-permute-start(bf16[32,456]{1,0:T(8,128)(2,1)S(1)} %get-tuple-element.39), channel_id=1, source_target_pairs={{0,24},{4,28},{8,16},{12,20},{16,8},{20,12},{24,0},{28,4},{1,25},{... | collective-permute-start | bytes 87560 | tf_op jit(solution)/shard_map/ppermute | solution.py:146
  8.6 7.5 %collective-permute-start.6 = (bf16[32,456]{1,0:T(8,128)(2,1)S(1)}, bf16[32,456]{1,0:T(8,128)(2,1)S(1)}, u32[]{:S(2)}, u32[]{:S(2)}) collective-permute-start(bf16[32,456]{1,0:T(8,128)(2,1)S(1)} %get-tuple-element.56), channel_id=1, source_target_pairs={{0,24},{4,28},{8,16},{12,20},{16,8},{20,12},{24,0},{28,4},{1,25},{... | collective-permute-start | bytes 87560 | tf_op jit(solution)/shard_map/ppermute | solution.py:146
  10.2 5.8 %collective-permute-start.4 = (bf16[32,456]{1,0:T(8,128)(2,1)S(1)}, bf16[32,456]{1,0:T(8,128)(2,1)S(1)}, u32[]{:S(2)}, u32[]{:S(2)}) collective-permute-start(bf16[32,456]{1,0:T(8,128)(2,1)S(1)} %get-tuple-element.57), channel_id=1, source_target_pairs={{0,16},{4,20},{8,24},{12,28},{16,0},{20,4},{24,8},{28,12},{1,17},{... | collective-permute-start | bytes 87560 | tf_op jit(solution)/shard_map/ppermute | solution.py:146
  11.5 4.6 %collective-permute-start.2 = (bf16[32,456]{1,0:T(8,128)(2,1)S(1)}, bf16[32,456]{1,0:T(8,128)(2,1)S(1)}, u32[]{:S(2)}, u32[]{:S(2)}) collective-permute-start(bf16[32,456]{1,0:T(8,128)(2,1)S(1)} %get-tuple-element.58), channel_id=1, source_target_pairs={{0,8},{4,12},{8,0},{12,4},{16,24},{20,28},{24,16},{28,20},{1,9},{5... | collective-permute-start | bytes 87560 | tf_op jit(solution)/shard_map/ppermute | solution.py:146
  19.1 5.1 %collective-permute-start.9 = (f32[2,32,128]{2,1,0:T(8,128)S(1)}, f32[2,32,128]{2,1,0:T(8,128)S(1)}, u32[]{:S(2)}, u32[]{:S(2)}) collective-permute-start(f32[2,32,128]{2,1,0:T(8,128)S(1)} %get-tuple-element.46), channel_id=1, source_target_pairs={{0,2},{1,3},{2,0},{3,1},{4,6},{5,7},{6,4},{7,5},{8,10},{9,11},{10,... | collective-permute-start | bytes 98312 | tf_op jit(solution)/shard_map/ppermute | solution.py:568
  20.7 13.0 %collective-permute-start.8 = (bf16[4,128,512]{2,1,0:T(8,128)(2,1)S(1)}, bf16[4,128,512]{2,1,0:T(8,128)(2,1)S(1)}, u32[]{:S(2)}, u32[]{:S(2)}) collective-permute-start(bf16[4,128,512]{2,1,0:T(8,128)(2,1)S(1)} %get-tuple-element.44), channel_id=1, source_target_pairs={{0,2},{1,3},{2,0},{3,1},{4,6},{5,7},{6,4},{7,5},{8,10},{9,11},{10,... | collective-permute-start | bytes 1572872 | tf_op jit(solution)/shard_map/ppermute | solution.py:569
  24.3 9.5 %slice-start = ((s8[16777216]{0:T(1024)(128)(4,1)}), s8[4194304]{0:T(1024)(128)(4,1)S(1)}, s32[]{:S(2)}) async-start(s8[16777216]{0:T(1024)(128)(4,1)} %bitcast.14), calls=%async_computation | async-start | bytes 8388608
  24.3 9.5 %slice-start.1 = ((s8[16777216]{0:T(1024)(128)(4,1)}), s8[4194304]{0:T(1024)(128)(4,1)S(1)}, s32[]{:S(2)}) async-start(s8[16777216]{0:T(1024)(128)(4,1)} %bitcast.14), calls=%async_computation.1 | async-start | bytes 8388608
  24.3 9.5 %slice-start.2 = ((s8[16777216]{0:T(1024)(128)(4,1)}), s8[4194304]{0:T(1024)(128)(4,1)S(1)}, s32[]{:S(2)}) async-start(s8[16777216]{0:T(1024)(128)(4,1)} %bitcast.14), calls=%async_computation.2 | async-start | bytes 8388608
  24.3 9.5 %slice-start.3 = ((s8[16777216]{0:T(1024)(128)(4,1)}), s8[4194304]{0:T(1024)(128)(4,1)S(1)}, s32[]{:S(2)}) async-start(s8[16777216]{0:T(1024)(128)(4,1)} %bitcast.14), calls=%async_computation.3 | async-start | bytes 8388608
  24.4 5.7 %collective-permute-start.10 = (f32[32,128]{1,0:T(8,128)S(1)}, f32[32,128]{1,0:T(8,128)S(1)}, u32[]{:S(2)}, u32[]{:S(2)}) collective-permute-start(f32[32,128]{1,0:T(8,128)S(1)} %get-tuple-element.47), channel_id=1, source_target_pairs={{0,4},{8,12},{16,20},{24,28},{4,0},{12,8},{20,16},{28,24},{1,5},{9... | collective-permute-start | bytes 49160 | tf_op jit(solution)/shard_map/ppermute | solution.py:518
  25.0 6.9 %collective-permute-start.11 = (f32[32,128]{1,0:T(8,128)S(1)}, f32[32,128]{1,0:T(8,128)S(1)}, u32[]{:S(2)}, u32[]{:S(2)}) collective-permute-start(f32[32,128]{1,0:T(8,128)S(1)} %get-tuple-element.48), channel_id=1, source_target_pairs={{4,8},{12,16},{20,24},{8,4},{16,12},{24,20},{5,9},{13,17},{21,25},... | collective-permute-start | bytes 49160 | tf_op jit(solution)/shard_map/ppermute | solution.py:518
  36.1 10.2 %collective-permute-start.12 = (f32[32,128]{1,0:T(8,128)S(1)}, f32[32,128]{1,0:T(8,128)S(1)}, u32[]{:S(2)}, u32[]{:S(2)}) collective-permute-start(f32[32,128]{1,0:T(8,128)S(1)} %get-tuple-element.52), channel_id=1, source_target_pairs={{0,4},{8,12},{16,20},{24,28},{4,0},{12,8},{20,16},{28,24},{1,5},{9... | collective-permute-start | bytes 49160 | tf_op jit(solution)/shard_map/ppermute | solution.py:518
  36.7 9.6 %collective-permute-start.13 = (f32[32,128]{1,0:T(8,128)S(1)}, f32[32,128]{1,0:T(8,128)S(1)}, u32[]{:S(2)}, u32[]{:S(2)}) collective-permute-start(f32[32,128]{1,0:T(8,128)S(1)} %get-tuple-element.53), channel_id=1, source_target_pairs={{4,8},{12,16},{20,24},{8,4},{16,12},{24,20},{5,9},{13,17},{21,25},... | collective-permute-start | bytes 49160 | tf_op jit(solution)/shard_map/ppermute | solution.py:518

commit v4 on v3

--- a/solution.py
+++ b/solution.py
@@ -327,27 +327,42 @@
     )
 
 
-def edge_kernel(*refs):
-    edge_refs, (first_ref, second_ref) = refs[:-2], refs[-2:]
+def edge_kernel(share, code_ref, lane_ref, *refs):
+    edge_refs, (first_ref, second_ref, rows_ref, lanes_ref) = refs[:-4], refs[-4:]
     total = edge_refs[0][...]
     for ref in edge_refs[1:]:
-        total = total + ref[...]
+        total = total + ref[...].astype(jnp.bfloat16).astype(jnp.float32)
     total = total.astype(jnp.bfloat16).astype(jnp.float32)
     even = mod(lax.axis_index("box"), 2) == 0
     first_ref[...] = jnp.where(even, total[1], total[0])
     second_ref[...] = jnp.where(even, total[0], total[1])
-
-
-def edge_call(*edges):
-    side = jax.ShapeDtypeStruct(edges[0].shape[1:], jnp.float32)
+    patches, _, points = code_ref.shape
+    per_box = total.shape[1] // RIM
+    tiles = per_box // share
+    row = iota((rows_ref.shape[1], points), 0)
+    row_code = div(row, per_box) * tiles + mod(row, tiles)
+    lane = iota((LANES, points), 0)
+    for p in range(patches):
+        rows_ref[p] = jnp.where(row_code == code_ref[p], 1.0, 0.0).astype(jnp.bfloat16)
+        lanes_ref[p] = jnp.where(lane == lane_ref[p], 1.0, 0.0).astype(jnp.bfloat16)
+
+
+def edge_call(code, lane, share, *edges):
+    patches, _, points = code.shape
+    side = edges[0].shape[1:]
     return pl.pallas_call(
-        edge_kernel,
-        out_shape=[side, side],
-        in_specs=[VMEM] * len(edges),
-        out_specs=[VMEM, VMEM],
-        compiler_params=params(2),
+        functools.partial(edge_kernel, share),
+        out_shape=[
+            jax.ShapeDtypeStruct(side, jnp.float32),
+            jax.ShapeDtypeStruct(side, jnp.float32),
+            pltpu.VMEM((patches, SPAN * side[0] // RIM, points), jnp.bfloat16),
+            pltpu.VMEM((patches, LANES, points), jnp.bfloat16),
+        ],
+        in_specs=[VMEM] * (2 + len(edges)),
+        out_specs=[VMEM] * 4,
+        compiler_params=params(4),
         cost_estimate=pl.CostEstimate(flops=10**10, bytes_accessed=0, transcendentals=0),
-    )(*edges)
+    )(code, lane, *edges)
 
 
 def order_patches(spans_ref, order_ref, boxes):
@@ -363,7 +378,9 @@
     return first
 
 
-def patch_batch(chosen, spans_ref, code_ref, lane_ref, ext, inverses_ref, spread, share, boxes):
+def patch_batch(
+    chosen, spans_ref, code_ref, lane_ref, rows_ref, lanes_ref, ext, inverses_ref, spread, share, boxes
+):
     points = code_ref.shape[2]
     per_box = ext.shape[0] // (boxes + 2 * RIM)
     tiles = per_box // share
@@ -385,19 +402,13 @@
             values.append(jnp.sum(found.reshape(share, tiles, LANES), axis=1))
         values = jnp.concatenate(values, axis=1).astype(jnp.bfloat16)
         product = jnp.dot(values, inverses_ref[p], preferred_element_type=jnp.float32)
-        products.append(product.astype(jnp.bfloat16).astype(jnp.float32))
-    row = iota((window, points), 0)
-    row_code = div(row, per_box) * tiles + mod(row, tiles)
+        products.append(product)
     for p, place, product in zip(chosen, places, products):
         product = jnp.concatenate(
             [jnp.broadcast_to(product[c : c + 1], (tiles, points)) for c in range(share)], axis=0
-        )
-        product = jnp.concatenate([product] * SPAN, axis=0)
-        left = jnp.where(row_code == code_ref[p], product, 0.0).astype(jnp.bfloat16)
-        right = jnp.where(iota((LANES, points), 0) == lane_ref[p], 1.0, 0.0)
-        placed = lax.dot_general(
-            left, right.astype(jnp.bfloat16), NT, preferred_element_type=jnp.float32
-        )
+        ).astype(jnp.bfloat16)
+        left = rows_ref[p] * jnp.concatenate([product] * SPAN, axis=0)
+        placed = lax.dot_general(left, lanes_ref[p], NT, preferred_element_type=jnp.float32)
         spread[place, :] = spread[place, :] + placed
 
 
@@ -407,6 +418,7 @@
 
 def early_kernel(
     spans_ref, code_ref, lane_ref, own_ref, received_ref, inverses_ref, first_ref, second_ref,
+    rows_in, lanes_in,
     ext, spread, first_out, second_out, order_ref,
 ):
     share, boxes, stride = own_ref.shape
@@ -433,7 +445,10 @@
 
     def step(i, carry):
         chosen = [order_ref[i * batch + k] for k in range(batch)]
-        patch_batch(chosen, spans_ref, code_ref, lane_ref, ext, inverses_ref, spread, share, boxes)
+        patch_batch(
+            chosen, spans_ref, code_ref, lane_ref, rows_in, lanes_in, ext, inverses_ref, spread,
+            share, boxes,
+        )
         return carry
 
     lax.fori_loop(0, div(reaching + batch - 1, batch), step, 0)
@@ -444,7 +459,7 @@
 
 
 def late_kernel(
-    spans_ref, code_ref, lane_ref, ext, early_ref, inverses_ref,
+    spans_ref, code_ref, lane_ref, ext, early_ref, inverses_ref, rows_in, lanes_in,
     field_ref, corrected_ref, rows_ref, spread, order_ref,
 ):
     share, width, boxes = field_ref.shape
@@ -457,12 +472,20 @@
     batch = batch_size(patches)
     reaching = order_patches(spans_ref, order_ref, boxes)
 
-    def step(i, carry):
-        chosen = [order_ref[i * batch + k] for k in range(batch)]
-        patch_batch(chosen, spans_ref, code_ref, lane_ref, ext, inverses_ref, spread, share, boxes)
-        return carry
-
-    lax.fori_loop(div(reaching + batch - 1, batch), patches // batch, step, 0)
+    begin = div(reaching + batch - 1, batch) * batch
+    for size in (2 * batch, batch):
+
+        def step(i, carry, size=size, begin=begin):
+            chosen = [order_ref[begin + i * size + k] for k in range(size)]
+            patch_batch(
+                chosen, spans_ref, code_ref, lane_ref, rows_in, lanes_in, ext, inverses_ref, spread,
+                share, boxes,
+            )
+            return carry
+
+        steps = div(patches - begin, size)
+        lax.fori_loop(0, steps, step, 0)
+        begin = begin + steps * size
     for c in range(share):
         for t in range(tiles):
             at = pl.ds(rim + c * tiles + t, boxes, stride=per_box)
@@ -568,7 +591,8 @@
         edges.append(lax.ppermute(edge, "col", moves))
         parts.append(lax.ppermute(part, "col", moves))
     own, edge = field_call(imported, picks, ready, pending, share, capacity, 0, jnp.float32)
-    first, second = swap_sides(*edge_call(edge, *edges))
+    first, second, *masks = edge_call(code, lane, share, edge, *edges)
+    first, second = swap_sides(first, second)
     received = jnp.stack(parts)
 
     ext_rows = (boxes + 2 * RIM) * per_box
@@ -582,11 +606,11 @@
             side,
             side,
         ],
-        in_specs=[SMEM] + [VMEM] * 7,
+        in_specs=[SMEM] + [VMEM] * 9,
         out_specs=[VMEM] * 4,
         scratch_shapes=[pltpu.SMEM((patches + 1,), jnp.int32)],
         compiler_params=params(10),
-    )(spans, code, lane, own, received, inverses, first, second)
+    )(spans, code, lane, own, received, inverses, first, second, *masks)
     first, second = swap_sides(first, second)
 
     field_t, corrected_t, rows = pl.pallas_call(
@@ -596,7 +620,7 @@
             pltpu.VMEM((share, width, boxes), jnp.bfloat16),
             pltpu.VMEM((2 * rim, LANES), jnp.float32),
         ],
-        in_specs=[SMEM] + [VMEM] * 5,
+        in_specs=[SMEM] + [VMEM] * 7,
         out_specs=[VMEM] * 3,
         scratch_shapes=[
             pltpu.VMEM((ext_rows, LANES), jnp.float32),
@@ -608,7 +632,7 @@
             bytes_accessed=patches * points * points * 2,
             transcendentals=0,
         ),
-    )(spans, code, lane, ext, early, inverses)
+    )(spans, code, lane, ext, early, inverses, *masks)
 
     corrected_t = pl.pallas_call(
         finish_kernel,

time: 47.8 us -> 47.4 us (level)
  waiting for transfers between devices: 5.6 us -> 4.92 us
    pallas_call x1, Pallas kernels: 0.02 us -> 0.7 us  [edge_call(): pl.pallas_call(functools.partial(edge_kernel, share), out_shape=[jax.Shap...]
    ppermute x1, waiting for transfers between devices: 1.88 us -> 1.21 us  [body(): parts.append(lax.ppermute(part, 'col', moves))]
where the time goes in v4:
time: 47.4 us; the launch traced here: 47.1 us
  starting transfers between devices  21 us (44%)
  Pallas kernels  20.3 us (43%)
  waiting for transfers between devices  4.92 us (10%)
  between operations  0.82 us (2%)
    ppermute x2, starting transfers between devices, swap_sides(): lax.ppermute(second, 'box', moves(1))  9.29 us
    ppermute x7, starting transfers between devices, swap(): return lax.ppermute(x, 'box', [(i, i ^ mask) for i in range(count)])  8.28 us
    pallas_call x2, Pallas kernels, field_call(): pl.pallas_call(functools.partial(field_kernel, share, capacity, group, ar...  6.05 us
    pallas_call x1, Pallas kernels, body(): pl.pallas_call(late_kernel, out_shape=[jax.ShapeDtypeStruct((share, width...  5.01 us
    pallas_call x1, Pallas kernels, prepare_call(): pl.pallas_call(functools.partial(prepare_kernel, slots, tiles, width, loc...  3.25 us
    pallas_call x1, Pallas kernels, body(): pl.pallas_call(early_kernel, out_shape=[pltpu.VMEM((ext_rows, LANES), jnp...  2.29 us
    pallas_call x1, Pallas kernels, pick_call(): pl.pallas_call(functools.partial(pick_kernel, share, swaps, load), out_sh...  1.92 us
    ppermute x7, waiting for transfers between devices, swap(): return lax.ppermute(x, 'box', [(i, i ^ mask) for i in range(count)])  1.87 us
  transfers between devices with their start and end apart: 14, of which 3 were waited for; matrix products, arithmetic and copies ran while one was open for 0% of the time, Pallas kernels for 29%

profile of v4, /device:TPU:10, one launch (start us, length us, event | category | flops | bytes accessed | tf_op | source)
XLA Modules:
  0.0 47.1 jit_solution(2386925184004415)
XLA Ops:
  0.6 0.1 collective-permute-start.7
  0.7 1.9 %shard_map.77 = (bf16[32,456]{1,0:T(8,128)(2,1)S(1)}, bf16[32,456]{1,0:T(8,128)(2,1)S(1)}, bf16[32,456]{1,0:T(8,128)(2,1)S(1)}, bf16[32,456]{1,0:T(8,128)(2,1)S(...) custom-call(s32[4,8]{1,0:T(4,128)} %bitcast.20, bf16[16,456,128]{2,1,0:T(8,128)(2,1)} %bitcast.17, ...), custom_call_target="tpu_custom_call" | custom-call | tf_op jit(solution)/shard_map/pallas_call | solution.py:122
  2.6 0.6 %collective-permute-start = (bf16[4,32,456]{2,1,0:T(8,128)(2,1)S(1)}, bf16[4,32,456]{2,1,0:T(8,128)(2,1)S(1)}, u32[]{:S(2)}, u32[]{:S(2)}) collective-permute-start(bf16[4,32,456]{2,1,0:T(8,128)(2,1)S(1)} %get-tuple-element.31), channel_id=1, source_target_pairs={{0,4},{4,0},{8,12},{12,8},{16,20},{20,16},{24,28},{28,24},{1,5},{5... | collective-permute-start | bytes 350216 | tf_op jit(solution)/shard_map/ppermute | solution.py:146
  3.2 3.0 %collective-permute-start.3 = (bf16[32,456]{1,0:T(8,128)(2,1)S(1)}, bf16[32,456]{1,0:T(8,128)(2,1)S(1)}, u32[]{:S(2)}, u32[]{:S(2)}) collective-permute-start(bf16[32,456]{1,0:T(8,128)(2,1)S(1)} %get-tuple-element.40), channel_id=1, source_target_pairs={{0,16},{4,20},{8,24},{12,28},{16,0},{20,4},{24,8},{28,12},{1,17},{... | collective-permute-start | bytes 87560 | tf_op jit(solution)/shard_map/ppermute | solution.py:146
  6.3 0.4 collective-permute-start.5
  6.7 1.9 %collective-permute-done.refs_1_ = bf16[4,32,456]{2,1,0:T(8,128)(2,1)S(1)} collective-permute-done((bf16[4,32,456]{2,1,0:T(8,128)(2,1)S(1)}, bf16[4,32,456]{2,1,0:T(8,128)(2,1)S(1)}, u32[]{:S(2)}, u32[]{:S(2)}) %collective-permute-start) | collective-permute-done | bytes 116768 | tf_op jit(solution)/shard_map/ppermute | solution.py:146
  8.6 1.6 %collective-permute-start.6 = (bf16[32,456]{1,0:T(8,128)(2,1)S(1)}, bf16[32,456]{1,0:T(8,128)(2,1)S(1)}, u32[]{:S(2)}, u32[]{:S(2)}) collective-permute-start(bf16[32,456]{1,0:T(8,128)(2,1)S(1)} %get-tuple-element.60), channel_id=1, source_target_pairs={{0,24},{4,28},{8,16},{12,20},{16,8},{20,12},{24,0},{28,4},{1,25},{... | collective-permute-start | bytes 87560 | tf_op jit(solution)/shard_map/ppermute | solution.py:146
  10.2 1.2 %collective-permute-start.4 = (bf16[32,456]{1,0:T(8,128)(2,1)S(1)}, bf16[32,456]{1,0:T(8,128)(2,1)S(1)}, u32[]{:S(2)}, u32[]{:S(2)}) collective-permute-start(bf16[32,456]{1,0:T(8,128)(2,1)S(1)} %get-tuple-element.61), channel_id=1, source_target_pairs={{0,16},{4,20},{8,24},{12,28},{16,0},{20,4},{24,8},{28,12},{1,17},{... | collective-permute-start | bytes 87560 | tf_op jit(solution)/shard_map/ppermute | solution.py:146
  11.5 1.3 %collective-permute-start.2 = (bf16[32,456]{1,0:T(8,128)(2,1)S(1)}, bf16[32,456]{1,0:T(8,128)(2,1)S(1)}, u32[]{:S(2)}, u32[]{:S(2)}) collective-permute-start(bf16[32,456]{1,0:T(8,128)(2,1)S(1)} %get-tuple-element.62), channel_id=1, source_target_pairs={{0,8},{4,12},{8,0},{12,4},{16,24},{20,28},{24,16},{28,20},{1,9},{5... | collective-permute-start | bytes 87560 | tf_op jit(solution)/shard_map/ppermute | solution.py:146
  12.8 3.2 %shard_map.78 = (bf16[128,1024]{1,0:T(8,128)(2,1)S(1)}, s32[8,1,1024]{2,1,0:T(1,128)S(1)}, s32[8,1,1024]{2,1,0:T(1,128)S(1)}, s32[16]{0:T(128)S(1)}, bf16[12,456,456]{2,1,0:T(8,128)(2,1)S(1)}) custom-call(s32[64,128]{1,0:T(8,128)} %bitcast.19, s32[8,1024]{1,0:T(8,128)} %points_hbm, bf16[16,456,456]{2,1,0:T(8,128)(2,1)} %operators_hbm.2), custom_call_target="tpu_custom_call" | custom-call | tf_op jit(solution)/shard_map/pallas_call | solution.py:207
  16.1 3.0 %shard_map.80 = (bf16[4,128,512]{2,1,0:T(8,128)(2,1)S(1)}, f32[2,32,128]{2,1,0:T(8,128)S(1)}) custom-call(bf16[32,456]{1,0:T(8,128)(2,1)S(1)} %get-tuple-element.38.refs_0_, bf16[4,32,456]{2,1,0:T(8,128)(2,1)S(1)} %collective-permute-done.refs_1_, bf16[32,456]{1,0:T(8,128)(2,1)S(1)} %collective-permute-done.1.refs_2_, ...), custom_call_target="tpu_custom_call" | custom-call | flops 2181562368 | bytes 4194304 | tf_op jit(solution)/shard_map/pallas_call | solution.py:300
  19.1 1.6 %collective-permute-start.9 = (f32[2,32,128]{2,1,0:T(8,128)S(1)}, f32[2,32,128]{2,1,0:T(8,128)S(1)}, u32[]{:S(2)}, u32[]{:S(2)}) collective-permute-start(f32[2,32,128]{2,1,0:T(8,128)S(1)} %get-tuple-element.48), channel_id=1, source_target_pairs={{0,2},{1,3},{2,0},{3,1},{4,6},{5,7},{6,4},{7,5},{8,10},{9,11},{10,... | collective-permute-start | bytes 98312 | tf_op jit(solution)/shard_map/ppermute | solution.py:591
  20.7 0.5 %collective-permute-start.8 = (bf16[4,128,512]{2,1,0:T(8,128)(2,1)S(1)}, bf16[4,128,512]{2,1,0:T(8,128)(2,1)S(1)}, u32[]{:S(2)}, u32[]{:S(2)}) collective-permute-start(bf16[4,128,512]{2,1,0:T(8,128)(2,1)S(1)} %get-tuple-element.46), channel_id=1, source_target_pairs={{0,2},{1,3},{2,0},{3,1},{4,6},{5,7},{6,4},{7,5},{8,10},{9,11},{10,... | collective-permute-start | bytes 1572872 | tf_op jit(solution)/shard_map/ppermute | solution.py:592
  21.2 3.0 %shard_map.79 = (f32[4,128,512]{2,1,0:T(8,128)S(1)}, f32[2,32,128]{2,1,0:T(8,128)S(1)}) custom-call(bf16[32,456]{1,0:T(8,128)(2,1)S(1)} %get-tuple-element.38.refs_0_, bf16[4,32,456]{2,1,0:T(8,128)(2,1)S(1)} %collective-permute-done.refs_1_, bf16[32,456]{1,0:T(8,128)(2,1)S(1)} %collective-permute-done.1.refs_2_, ...), custom_call_target="tpu_custom_call" | custom-call | flops 2181562368 | bytes 4194304 | tf_op jit(solution)/shard_map/pallas_call | solution.py:300
  24.3 0.7 %shard_map.81 = (f32[32,128]{1,0:T(8,128)S(1)}, f32[32,128]{1,0:T(8,128)S(1)}, bf16[8,128,1024]{2,1,0:T(8,128)(2,1)S(1)}, bf16[8,128,1024]{2,1,0:T(8,128)(2,1)S(1)}) custom-call(s32[8,1,1024]{2,1,0:T(1,128)S(1)} %get-tuple-element.36.code_ref, s32[8,1,1024]{2,1,0:T(1,128)S(1)} %get-tuple-element.37.lane_ref, f32[2,32,128]{2,1,0:T(8,128)S(1)} %get-tuple-element.47.refs_0_, ...), custom_call_target="tpu_custom_call" | custom-call | flops 10000000000 | tf_op jit(solution)/shard_map/pallas_call | solution.py:353
  25.0 0.6 %collective-permute-start.10 = (f32[32,128]{1,0:T(8,128)S(1)}, f32[32,128]{1,0:T(8,128)S(1)}, u32[]{:S(2)}, u32[]{:S(2)}) collective-permute-start(f32[32,128]{1,0:T(8,128)S(1)} %get-tuple-element.49), channel_id=1, source_target_pairs={{0,4},{8,12},{16,20},{24,28},{4,0},{12,8},{20,16},{28,24},{1,5},{9... | collective-permute-start | bytes 49160 | tf_op jit(solution)/shard_map/ppermute | solution.py:541
  25.6 5.1 %collective-permute-start.11 = (f32[32,128]{1,0:T(8,128)S(1)}, f32[32,128]{1,0:T(8,128)S(1)}, u32[]{:S(2)}, u32[]{:S(2)}) collective-permute-start(f32[32,128]{1,0:T(8,128)S(1)} %get-tuple-element.50), channel_id=1, source_target_pairs={{4,8},{12,16},{20,24},{8,4},{16,12},{24,20},{5,9},{13,17},{21,25},... | collective-permute-start | bytes 49160 | tf_op jit(solution)/shard_map/ppermute | solution.py:541
  30.7 1.8 %collective-permute-done.11.second_ref = f32[32,128]{1,0:T(8,128)S(1)} collective-permute-done((f32[32,128]{1,0:T(8,128)S(1)}, f32[32,128]{1,0:T(8,128)S(1)}, u32[]{:S(2)}, u32[]{:S(2)}) %collective-permute-start.11) | collective-permute-done | bytes 16416 | tf_op jit(solution)/shard_map/ppermute | solution.py:541
  32.6 1.2 %collective-permute-done.8 = bf16[4,128,512]{2,1,0:T(8,128)(2,1)S(1)} collective-permute-done((bf16[4,128,512]{2,1,0:T(8,128)(2,1)S(1)}, bf16[4,128,512]{2,1,0:T(8,128)(2,1)S(1)}, u32[]{:S(2)}, u32[]{:S(2)}) %collective-permute-start.8) | collective-permute-done | bytes 524320 | tf_op jit(solution)/shard_map/ppermute | solution.py:592
  33.8 2.3 %shard_map.82 = (f32[2112,128]{1,0:T(8,128)S(1)}, f32[2112,128]{1,0:T(8,128)S(1)}, f32[32,128]{1,0:T(8,128)S(1)}, f32[32,128]{1,0:T(8,128)S(1)}) custom-call(s32[16]{0:T(128)S(1)} %get-tuple-element.35.spans_ref, s32[8,1,1024]{2,1,0:T(1,128)S(1)} %get-tuple-element.36.code_ref, s32[8,1,1024]{2,1,0:T(1,128)S(1)} %get-tuple-element.37.lane_ref, ...), custom_call_target="tpu_custom_call" | custom-call | tf_op jit(solution)/shard_map/pallas_call | solution.py:601
  36.1 0.6 %collective-permute-start.12 = (f32[32,128]{1,0:T(8,128)S(1)}, f32[32,128]{1,0:T(8,128)S(1)}, u32[]{:S(2)}, u32[]{:S(2)}) collective-permute-start(f32[32,128]{1,0:T(8,128)S(1)} %get-tuple-element.56), channel_id=1, source_target_pairs={{0,4},{8,12},{16,20},{24,28},{4,0},{12,8},{20,16},{28,24},{1,5},{9... | collective-permute-start | bytes 49160 | tf_op jit(solution)/shard_map/ppermute | solution.py:541
  36.7 4.2 %collective-permute-start.13 = (f32[32,128]{1,0:T(8,128)S(1)}, f32[32,128]{1,0:T(8,128)S(1)}, u32[]{:S(2)}, u32[]{:S(2)}) collective-permute-start(f32[32,128]{1,0:T(8,128)S(1)} %get-tuple-element.57), channel_id=1, source_target_pairs={{4,8},{12,16},{20,24},{8,4},{16,12},{24,20},{5,9},{13,17},{21,25},... | collective-permute-start | bytes 49160 | tf_op jit(solution)/shard_map/ppermute | solution.py:541
  40.9 5.0 %shard_map.83 = (bf16[4,456,128]{2,1,0:T(8,128)(2,1)}, bf16[4,456,128]{2,1,0:T(8,128)(2,1)S(1)}, f32[64,128]{1,0:T(8,128)S(1)}) custom-call(s32[16]{0:T(128)S(1)} %get-tuple-element.35.spans_ref, s32[8,1,1024]{2,1,0:T(1,128)S(1)} %get-tuple-element.36.code_ref, s32[8,1,1024]{2,1,0:T(1,128)S(1)} %get-tuple-element.37.lane_ref, ...), custom_call_target="tpu_custom_call" | custom-call | flops 67108864 | bytes 16777216 | tf_op jit(solution)/shard_map/pallas_call | solution.py:616
  45.9 1.1 %shard_map.84 = bf16[4,456,128]{2,1,0:T(8,128)(2,1)} custom-call(f32[32,128]{1,0:T(8,128)S(1)} %collective-permute-done.12.first_ref, f32[32,128]{1,0:T(8,128)S(1)} %collective-permute-done.13.second_ref, f32[64,128]{1,0:T(8,128)S(1)} %get-tuple-element.58.rows_ref, bf16[4,456,128]{2,1,0:T(8,128)(2,1)S(1)} %get-tuple-element.59.corrected_ref), custom_call_target="tpu_custom_call" | custom-call | tf_op jit(solution)/shard_map/pallas_call | solution.py:637
  (22 shorter events, 0.1 us)
Async XLA Ops:
  0.6 15.5 %collective-permute-start.7 = (bf16[16,456,456]{2,1,0:T(8,128)(2,1)}, bf16[16,456,456]{2,1,0:T(8,128)(2,1)S(1)}, u32[]{:S(2)}, u32[]{:S(2)}) collective-permute-start(bf16[16,456,456]{2,1,0:T(8,128)(2,1)} %operators_hbm.2), channel_id=1, source_target_pairs={{1,0},{0,1},{3,2},{2,3},{5,4},{4,5},{7,6},{6,7},{9,8},{8,9},{11,10... | collective-permute-start | bytes 19961864 | tf_op jit(solution)/shard_map/ppermute | solution.py:559
  2.6 5.9 %collective-permute-start = (bf16[4,32,456]{2,1,0:T(8,128)(2,1)S(1)}, bf16[4,32,456]{2,1,0:T(8,128)(2,1)S(1)}, u32[]{:S(2)}, u32[]{:S(2)}) collective-permute-start(bf16[4,32,456]{2,1,0:T(8,128)(2,1)S(1)} %get-tuple-element.31), channel_id=1, source_target_pairs={{0,4},{4,0},{8,12},{12,8},{16,20},{20,16},{24,28},{28,24},{1,5},{5... | collective-permute-start | bytes 350216 | tf_op jit(solution)/shard_map/ppermute | solution.py:146
  3.2 7.0 %collective-permute-start.1 = (bf16[32,456]{1,0:T(8,128)(2,1)S(1)}, bf16[32,456]{1,0:T(8,128)(2,1)S(1)}, u32[]{:S(2)}, u32[]{:S(2)}) collective-permute-start(bf16[32,456]{1,0:T(8,128)(2,1)S(1)} %get-tuple-element.39), channel_id=1, source_target_pairs={{0,8},{4,12},{8,0},{12,4},{16,24},{20,28},{24,16},{28,20},{1,9},{5... | collective-permute-start | bytes 87560 | tf_op jit(solution)/shard_map/ppermute | solution.py:146
  3.2 8.2 %collective-permute-start.3 = (bf16[32,456]{1,0:T(8,128)(2,1)S(1)}, bf16[32,456]{1,0:T(8,128)(2,1)S(1)}, u32[]{:S(2)}, u32[]{:S(2)}) collective-permute-start(bf16[32,456]{1,0:T(8,128)(2,1)S(1)} %get-tuple-element.40), channel_id=1, source_target_pairs={{0,16},{4,20},{8,24},{12,28},{16,0},{20,4},{24,8},{28,12},{1,17},{... | collective-permute-start | bytes 87560 | tf_op jit(solution)/shard_map/ppermute | solution.py:146
  6.3 9.8 %collective-permute-start.5 = (bf16[32,456]{1,0:T(8,128)(2,1)S(1)}, bf16[32,456]{1,0:T(8,128)(2,1)S(1)}, u32[]{:S(2)}, u32[]{:S(2)}) collective-permute-start(bf16[32,456]{1,0:T(8,128)(2,1)S(1)} %get-tuple-element.41), channel_id=1, source_target_pairs={{0,24},{4,28},{8,16},{12,20},{16,8},{20,12},{24,0},{28,4},{1,25},{... | collective-permute-start | bytes 87560 | tf_op jit(solution)/shard_map/ppermute | solution.py:146
  8.6 7.5 %collective-permute-start.6 = (bf16[32,456]{1,0:T(8,128)(2,1)S(1)}, bf16[32,456]{1,0:T(8,128)(2,1)S(1)}, u32[]{:S(2)}, u32[]{:S(2)}) collective-permute-start(bf16[32,456]{1,0:T(8,128)(2,1)S(1)} %get-tuple-element.60), channel_id=1, source_target_pairs={{0,24},{4,28},{8,16},{12,20},{16,8},{20,12},{24,0},{28,4},{1,25},{... | collective-permute-start | bytes 87560 | tf_op jit(solution)/shard_map/ppermute | solution.py:146
  10.2 5.8 %collective-permute-start.4 = (bf16[32,456]{1,0:T(8,128)(2,1)S(1)}, bf16[32,456]{1,0:T(8,128)(2,1)S(1)}, u32[]{:S(2)}, u32[]{:S(2)}) collective-permute-start(bf16[32,456]{1,0:T(8,128)(2,1)S(1)} %get-tuple-element.61), channel_id=1, source_target_pairs={{0,16},{4,20},{8,24},{12,28},{16,0},{20,4},{24,8},{28,12},{1,17},{... | collective-permute-start | bytes 87560 | tf_op jit(solution)/shard_map/ppermute | solution.py:146
  11.5 4.6 %collective-permute-start.2 = (bf16[32,456]{1,0:T(8,128)(2,1)S(1)}, bf16[32,456]{1,0:T(8,128)(2,1)S(1)}, u32[]{:S(2)}, u32[]{:S(2)}) collective-permute-start(bf16[32,456]{1,0:T(8,128)(2,1)S(1)} %get-tuple-element.62), channel_id=1, source_target_pairs={{0,8},{4,12},{8,0},{12,4},{16,24},{20,28},{24,16},{28,20},{1,9},{5... | collective-permute-start | bytes 87560 | tf_op jit(solution)/shard_map/ppermute | solution.py:146
  19.1 5.1 %collective-permute-start.9 = (f32[2,32,128]{2,1,0:T(8,128)S(1)}, f32[2,32,128]{2,1,0:T(8,128)S(1)}, u32[]{:S(2)}, u32[]{:S(2)}) collective-permute-start(f32[2,32,128]{2,1,0:T(8,128)S(1)} %get-tuple-element.48), channel_id=1, source_target_pairs={{0,2},{1,3},{2,0},{3,1},{4,6},{5,7},{6,4},{7,5},{8,10},{9,11},{10,... | collective-permute-start | bytes 98312 | tf_op jit(solution)/shard_map/ppermute | solution.py:591
  20.7 13.0 %collective-permute-start.8 = (bf16[4,128,512]{2,1,0:T(8,128)(2,1)S(1)}, bf16[4,128,512]{2,1,0:T(8,128)(2,1)S(1)}, u32[]{:S(2)}, u32[]{:S(2)}) collective-permute-start(bf16[4,128,512]{2,1,0:T(8,128)(2,1)S(1)} %get-tuple-element.46), channel_id=1, source_target_pairs={{0,2},{1,3},{2,0},{3,1},{4,6},{5,7},{6,4},{7,5},{8,10},{9,11},{10,... | collective-permute-start | bytes 1572872 | tf_op jit(solution)/shard_map/ppermute | solution.py:592
  24.3 9.5 %slice-start = ((s8[16777216]{0:T(1024)(128)(4,1)}), s8[4194304]{0:T(1024)(128)(4,1)S(1)}, s32[]{:S(2)}) async-start(s8[16777216]{0:T(1024)(128)(4,1)} %bitcast.14), calls=%async_computation | async-start | bytes 8388608
  24.3 9.5 %slice-start.1 = ((s8[16777216]{0:T(1024)(128)(4,1)}), s8[4194304]{0:T(1024)(128)(4,1)S(1)}, s32[]{:S(2)}) async-start(s8[16777216]{0:T(1024)(128)(4,1)} %bitcast.14), calls=%async_computation.1 | async-start | bytes 8388608
  24.3 9.5 %slice-start.2 = ((s8[16777216]{0:T(1024)(128)(4,1)}), s8[4194304]{0:T(1024)(128)(4,1)S(1)}, s32[]{:S(2)}) async-start(s8[16777216]{0:T(1024)(128)(4,1)} %bitcast.14), calls=%async_computation.2 | async-start | bytes 8388608
  24.3 9.5 %slice-start.3 = ((s8[16777216]{0:T(1024)(128)(4,1)}), s8[4194304]{0:T(1024)(128)(4,1)S(1)}, s32[]{:S(2)}) async-start(s8[16777216]{0:T(1024)(128)(4,1)} %bitcast.14), calls=%async_computation.3 | async-start | bytes 8388608
  25.0 5.7 %collective-permute-start.10 = (f32[32,128]{1,0:T(8,128)S(1)}, f32[32,128]{1,0:T(8,128)S(1)}, u32[]{:S(2)}, u32[]{:S(2)}) collective-permute-start(f32[32,128]{1,0:T(8,128)S(1)} %get-tuple-element.49), channel_id=1, source_target_pairs={{0,4},{8,12},{16,20},{24,28},{4,0},{12,8},{20,16},{28,24},{1,5},{9... | collective-permute-start | bytes 49160 | tf_op jit(solution)/shard_map/ppermute | solution.py:541
  25.6 6.9 %collective-permute-start.11 = (f32[32,128]{1,0:T(8,128)S(1)}, f32[32,128]{1,0:T(8,128)S(1)}, u32[]{:S(2)}, u32[]{:S(2)}) collective-permute-start(f32[32,128]{1,0:T(8,128)S(1)} %get-tuple-element.50), channel_id=1, source_target_pairs={{4,8},{12,16},{20,24},{8,4},{16,12},{24,20},{5,9},{13,17},{21,25},... | collective-permute-start | bytes 49160 | tf_op jit(solution)/shard_map/ppermute | solution.py:541
  36.1 9.8 %collective-permute-start.12 = (f32[32,128]{1,0:T(8,128)S(1)}, f32[32,128]{1,0:T(8,128)S(1)}, u32[]{:S(2)}, u32[]{:S(2)}) collective-permute-start(f32[32,128]{1,0:T(8,128)S(1)} %get-tuple-element.56), channel_id=1, source_target_pairs={{0,4},{8,12},{16,20},{24,28},{4,0},{12,8},{20,16},{28,24},{1,5},{9... | collective-permute-start | bytes 49160 | tf_op jit(solution)/shard_map/ppermute | solution.py:541
  36.7 9.2 %collective-permute-start.13 = (f32[32,128]{1,0:T(8,128)S(1)}, f32[32,128]{1,0:T(8,128)S(1)}, u32[]{:S(2)}, u32[]{:S(2)}) collective-permute-start(f32[32,128]{1,0:T(8,128)S(1)} %get-tuple-element.57), channel_id=1, source_target_pairs={{4,8},{12,16},{20,24},{8,4},{16,12},{24,20},{5,9},{13,17},{21,25},... | collective-permute-start | bytes 49160 | tf_op jit(solution)/shard_map/ppermute | solution.py:541

commit v5 on v4

--- a/solution.py
+++ b/solution.py
@@ -460,7 +460,7 @@
 
 def late_kernel(
     spans_ref, code_ref, lane_ref, ext, early_ref, inverses_ref, rows_in, lanes_in,
-    field_ref, corrected_ref, rows_ref, spread, order_ref,
+    field_hbm, corrected_ref, rows_ref, spread, field_ref, order_ref, sem,
 ):
     share, width, boxes = field_ref.shape
     per_box = ext.shape[0] // (boxes + 2 * RIM)
@@ -468,6 +468,13 @@
     rim = RIM * per_box
     end = rim + boxes * per_box
     patches = code_ref.shape[0]
+    for c in range(share):
+        for t in range(tiles):
+            own = ext[pl.ds(rim + c * tiles + t, boxes, stride=per_box), :]
+            last = min(width - t * LANES, LANES)
+            field_ref[c, t * LANES : t * LANES + last, :] = own.T[:last].astype(field_ref.dtype)
+    field_copy = pltpu.make_async_copy(field_ref, field_hbm, sem)
+    field_copy.start()
     spread[...] = early_ref[...]
     batch = batch_size(patches)
     reaching = order_patches(spans_ref, order_ref, boxes)
@@ -490,16 +497,15 @@
         for t in range(tiles):
             at = pl.ds(rim + c * tiles + t, boxes, stride=per_box)
             last = min(width - t * LANES, LANES)
-            own = ext[at, :]
-            total = own + spread[at, :]
+            total = ext[at, :] + spread[at, :]
             to = slice(t * LANES, t * LANES + last)
-            field_ref[c, to, :] = own.T[:last].astype(field_ref.dtype)
             corrected_ref[c, to, :] = total.T[:last].astype(corrected_ref.dtype)
     rows_ref[:rim] = ext[rim : 2 * rim, :] + spread[rim : 2 * rim, :]
     rows_ref[rim:] = ext[end - rim : end, :] + spread[end - rim : end, :]
-
-
-def finish_kernel(first_ref, second_ref, rows_ref, corrected_ref, out_ref):
+    field_copy.wait()
+
+
+def finish_kernel(first_ref, second_ref, rows_ref, corrected_ref, out_hbm, out_ref, sems):
     share, width, boxes = corrected_ref.shape
     rim = rows_ref.shape[0] // 2
     per_box = rim // RIM
@@ -529,6 +535,9 @@
             out_ref[c, to, :] = jnp.where(
                 edge[:last], placed[:last, at : at + boxes], kept
             ).astype(out_ref.dtype)
+        pltpu.make_async_copy(out_ref.at[c], out_hbm.at[c], sems.at[c]).start()
+    for c in range(share):
+        pltpu.make_async_copy(out_ref.at[c], out_hbm.at[c], sems.at[c]).wait()
 
 
 def swap_sides(first, second):
@@ -621,10 +630,12 @@
             pltpu.VMEM((2 * rim, LANES), jnp.float32),
         ],
         in_specs=[SMEM] + [VMEM] * 7,
-        out_specs=[VMEM] * 3,
+        out_specs=[ANY, VMEM, VMEM],
         scratch_shapes=[
             pltpu.VMEM((ext_rows, LANES), jnp.float32),
+            pltpu.VMEM((share, width, boxes), jnp.bfloat16),
             pltpu.SMEM((patches + 1,), jnp.int32),
+            pltpu.SemaphoreType.DMA,
         ],
         compiler_params=params(10),
         cost_estimate=pl.CostEstimate(
@@ -638,7 +649,11 @@
         finish_kernel,
         out_shape=jax.ShapeDtypeStruct(corrected_t.shape, corrected_t.dtype),
         in_specs=[VMEM] * 4,
-        out_specs=VMEM,
+        out_specs=ANY,
+        scratch_shapes=[
+            pltpu.VMEM(corrected_t.shape, corrected_t.dtype),
+            pltpu.SemaphoreType.DMA((share,)),
+        ],
         compiler_params=params(8),
     )(first, second, rows, corrected_t)
     return jnp.transpose(field_t, (2, 0, 1)), jnp.transpose(corrected_t, (2, 0, 1))

time: 47.4 us -> 47.3 us (level); the launches traced: 47.1 us -> 47.6 us
  starting transfers between devices: 21 us -> 22.1 us
  Pallas kernels: 20.3 us -> 19.8 us
    ppermute x2, starting transfers between devices: 9.29 us -> 10.4 us  [swap_sides(): lax.ppermute(second, 'box', moves(1))]
    pallas_call x1, Pallas kernels: 5.01 us -> 4.5 us  [body(): pl.pallas_call(late_kernel, out_shape=[jax.ShapeDtypeStruct((share, width...]
  transfers between devices with their start and end apart: 14 -> 14, of which waited for: 3 -> 3; matrix products, arithmetic and copies ran while one was open for 0% -> 0% of each run, Pallas kernels for 29% -> 28%
where the time goes in v5:
time: 47.3 us; the launch traced here: 47.6 us
  starting transfers between devices  22.1 us (47%)
  Pallas kernels  19.8 us (42%)
  waiting for transfers between devices  4.92 us (10%)
  between operations  0.84 us (2%)
    ppermute x2, starting transfers between devices, swap_sides(): lax.ppermute(second, 'box', moves(1))  10.4 us
    ppermute x7, starting transfers between devices, swap(): return lax.ppermute(x, 'box', [(i, i ^ mask) for i in range(count)])  8.28 us
    pallas_call x2, Pallas kernels, field_call(): pl.pallas_call(functools.partial(field_kernel, share, capacity, group, ar...  6.05 us
    pallas_call x1, Pallas kernels, body(): pl.pallas_call(late_kernel, out_shape=[jax.ShapeDtypeStruct((share, width...  4.5 us
    pallas_call x1, Pallas kernels, prepare_call(): pl.pallas_call(functools.partial(prepare_kernel, slots, tiles, width, loc...  3.25 us
    pallas_call x1, Pallas kernels, body(): pl.pallas_call(early_kernel, out_shape=[pltpu.VMEM((ext_rows, LANES), jnp...  2.29 us
    pallas_call x1, Pallas kernels, pick_call(): pl.pallas_call(functools.partial(pick_kernel, share, swaps, load), out_sh...  1.92 us
    ppermute x7, waiting for transfers between devices, swap(): return lax.ppermute(x, 'box', [(i, i ^ mask) for i in range(count)])  1.87 us
  transfers between devices with their start and end apart: 14, of which 3 were waited for; matrix products, arithmetic and copies ran while one was open for 0% of the time, Pallas kernels for 28%

profile of v5, /device:TPU:10, one launch (start us, length us, event | category | flops | bytes accessed | tf_op | source)
XLA Modules:
  0.0 47.6 jit_solution(13511875006741276191)
XLA Ops:
  0.6 0.1 collective-permute-start.7
  0.7 1.9 %shard_map.77 = (bf16[32,456]{1,0:T(8,128)(2,1)S(1)}, bf16[32,456]{1,0:T(8,128)(2,1)S(1)}, bf16[32,456]{1,0:T(8,128)(2,1)S(1)}, bf16[32,456]{1,0:T(8,128)(2,1)S(...) custom-call(s32[4,8]{1,0:T(4,128)} %bitcast.20, bf16[16,456,128]{2,1,0:T(8,128)(2,1)} %bitcast.17, ...), custom_call_target="tpu_custom_call" | custom-call | tf_op jit(solution)/shard_map/pallas_call | solution.py:122
  2.6 0.6 %collective-permute-start = (bf16[4,32,456]{2,1,0:T(8,128)(2,1)S(1)}, bf16[4,32,456]{2,1,0:T(8,128)(2,1)S(1)}, u32[]{:S(2)}, u32[]{:S(2)}) collective-permute-start(bf16[4,32,456]{2,1,0:T(8,128)(2,1)S(1)} %get-tuple-element.31), channel_id=1, source_target_pairs={{0,4},{4,0},{8,12},{12,8},{16,20},{20,16},{24,28},{28,24},{1,5},{5... | collective-permute-start | bytes 350216 | tf_op jit(solution)/shard_map/ppermute | solution.py:146
  3.2 3.0 %collective-permute-start.3 = (bf16[32,456]{1,0:T(8,128)(2,1)S(1)}, bf16[32,456]{1,0:T(8,128)(2,1)S(1)}, u32[]{:S(2)}, u32[]{:S(2)}) collective-permute-start(bf16[32,456]{1,0:T(8,128)(2,1)S(1)} %get-tuple-element.40), channel_id=1, source_target_pairs={{0,16},{4,20},{8,24},{12,28},{16,0},{20,4},{24,8},{28,12},{1,17},{... | collective-permute-start | bytes 87560 | tf_op jit(solution)/shard_map/ppermute | solution.py:146
  6.3 0.4 collective-permute-start.5
  6.7 1.9 %collective-permute-done.refs_1_ = bf16[4,32,456]{2,1,0:T(8,128)(2,1)S(1)} collective-permute-done((bf16[4,32,456]{2,1,0:T(8,128)(2,1)S(1)}, bf16[4,32,456]{2,1,0:T(8,128)(2,1)S(1)}, u32[]{:S(2)}, u32[]{:S(2)}) %collective-permute-start) | collective-permute-done | bytes 116768 | tf_op jit(solution)/shard_map/ppermute | solution.py:146
  8.6 1.6 %collective-permute-start.6 = (bf16[32,456]{1,0:T(8,128)(2,1)S(1)}, bf16[32,456]{1,0:T(8,128)(2,1)S(1)}, u32[]{:S(2)}, u32[]{:S(2)}) collective-permute-start(bf16[32,456]{1,0:T(8,128)(2,1)S(1)} %get-tuple-element.60), channel_id=1, source_target_pairs={{0,24},{4,28},{8,16},{12,20},{16,8},{20,12},{24,0},{28,4},{1,25},{... | collective-permute-start | bytes 87560 | tf_op jit(solution)/shard_map/ppermute | solution.py:146
  10.2 1.2 %collective-permute-start.4 = (bf16[32,456]{1,0:T(8,128)(2,1)S(1)}, bf16[32,456]{1,0:T(8,128)(2,1)S(1)}, u32[]{:S(2)}, u32[]{:S(2)}) collective-permute-start(bf16[32,456]{1,0:T(8,128)(2,1)S(1)} %get-tuple-element.61), channel_id=1, source_target_pairs={{0,16},{4,20},{8,24},{12,28},{16,0},{20,4},{24,8},{28,12},{1,17},{... | collective-permute-start | bytes 87560 | tf_op jit(solution)/shard_map/ppermute | solution.py:146
  11.5 1.3 %collective-permute-start.2 = (bf16[32,456]{1,0:T(8,128)(2,1)S(1)}, bf16[32,456]{1,0:T(8,128)(2,1)S(1)}, u32[]{:S(2)}, u32[]{:S(2)}) collective-permute-start(bf16[32,456]{1,0:T(8,128)(2,1)S(1)} %get-tuple-element.62), channel_id=1, source_target_pairs={{0,8},{4,12},{8,0},{12,4},{16,24},{20,28},{24,16},{28,20},{1,9},{5... | collective-permute-start | bytes 87560 | tf_op jit(solution)/shard_map/ppermute | solution.py:146
  12.8 3.2 %shard_map.78 = (bf16[128,1024]{1,0:T(8,128)(2,1)S(1)}, s32[8,1,1024]{2,1,0:T(1,128)S(1)}, s32[8,1,1024]{2,1,0:T(1,128)S(1)}, s32[16]{0:T(128)S(1)}, bf16[12,456,456]{2,1,0:T(8,128)(2,1)S(1)}) custom-call(s32[64,128]{1,0:T(8,128)} %bitcast.19, s32[8,1024]{1,0:T(8,128)} %points_hbm, bf16[16,456,456]{2,1,0:T(8,128)(2,1)} %operators_hbm.2), custom_call_target="tpu_custom_call" | custom-call | tf_op jit(solution)/shard_map/pallas_call | solution.py:207
  16.1 3.0 %shard_map.80 = (bf16[4,128,512]{2,1,0:T(8,128)(2,1)S(1)}, f32[2,32,128]{2,1,0:T(8,128)S(1)}) custom-call(bf16[32,456]{1,0:T(8,128)(2,1)S(1)} %get-tuple-element.38.refs_0_, bf16[4,32,456]{2,1,0:T(8,128)(2,1)S(1)} %collective-permute-done.refs_1_, bf16[32,456]{1,0:T(8,128)(2,1)S(1)} %collective-permute-done.1.refs_2_, ...), custom_call_target="tpu_custom_call" | custom-call | flops 2181562368 | bytes 4194304 | tf_op jit(solution)/shard_map/pallas_call | solution.py:300
  19.1 1.6 %collective-permute-start.9 = (f32[2,32,128]{2,1,0:T(8,128)S(1)}, f32[2,32,128]{2,1,0:T(8,128)S(1)}, u32[]{:S(2)}, u32[]{:S(2)}) collective-permute-start(f32[2,32,128]{2,1,0:T(8,128)S(1)} %get-tuple-element.48), channel_id=1, source_target_pairs={{0,2},{1,3},{2,0},{3,1},{4,6},{5,7},{6,4},{7,5},{8,10},{9,11},{10,... | collective-permute-start | bytes 98312 | tf_op jit(solution)/shard_map/ppermute | solution.py:600
  20.7 0.5 %collective-permute-start.8 = (bf16[4,128,512]{2,1,0:T(8,128)(2,1)S(1)}, bf16[4,128,512]{2,1,0:T(8,128)(2,1)S(1)}, u32[]{:S(2)}, u32[]{:S(2)}) collective-permute-start(bf16[4,128,512]{2,1,0:T(8,128)(2,1)S(1)} %get-tuple-element.46), channel_id=1, source_target_pairs={{0,2},{1,3},{2,0},{3,1},{4,6},{5,7},{6,4},{7,5},{8,10},{9,11},{10,... | collective-permute-start | bytes 1572872 | tf_op jit(solution)/shard_map/ppermute | solution.py:601
  21.2 3.0 %shard_map.79 = (f32[4,128,512]{2,1,0:T(8,128)S(1)}, f32[2,32,128]{2,1,0:T(8,128)S(1)}) custom-call(bf16[32,456]{1,0:T(8,128)(2,1)S(1)} %get-tuple-element.38.refs_0_, bf16[4,32,456]{2,1,0:T(8,128)(2,1)S(1)} %collective-permute-done.refs_1_, bf16[32,456]{1,0:T(8,128)(2,1)S(1)} %collective-permute-done.1.refs_2_, ...), custom_call_target="tpu_custom_call" | custom-call | flops 2181562368 | bytes 4194304 | tf_op jit(solution)/shard_map/pallas_call | solution.py:300
  24.3 0.7 %shard_map.81 = (f32[32,128]{1,0:T(8,128)S(1)}, f32[32,128]{1,0:T(8,128)S(1)}, bf16[8,128,1024]{2,1,0:T(8,128)(2,1)S(1)}, bf16[8,128,1024]{2,1,0:T(8,128)(2,1)S(1)}) custom-call(s32[8,1,1024]{2,1,0:T(1,128)S(1)} %get-tuple-element.36.code_ref, s32[8,1,1024]{2,1,0:T(1,128)S(1)} %get-tuple-element.37.lane_ref, f32[2,32,128]{2,1,0:T(8,128)S(1)} %get-tuple-element.47.refs_0_, ...), custom_call_target="tpu_custom_call" | custom-call | flops 10000000000 | tf_op jit(solution)/shard_map/pallas_call | solution.py:353
  25.0 0.6 %collective-permute-start.10 = (f32[32,128]{1,0:T(8,128)S(1)}, f32[32,128]{1,0:T(8,128)S(1)}, u32[]{:S(2)}, u32[]{:S(2)}) collective-permute-start(f32[32,128]{1,0:T(8,128)S(1)} %get-tuple-element.49), channel_id=1, source_target_pairs={{0,4},{8,12},{16,20},{24,28},{4,0},{12,8},{20,16},{28,24},{1,5},{9... | collective-permute-start | bytes 49160 | tf_op jit(solution)/shard_map/ppermute | solution.py:550
  25.6 5.1 %collective-permute-start.11 = (f32[32,128]{1,0:T(8,128)S(1)}, f32[32,128]{1,0:T(8,128)S(1)}, u32[]{:S(2)}, u32[]{:S(2)}) collective-permute-start(f32[32,128]{1,0:T(8,128)S(1)} %get-tuple-element.50), channel_id=1, source_target_pairs={{4,8},{12,16},{20,24},{8,4},{16,12},{24,20},{5,9},{13,17},{21,25},... | collective-permute-start | bytes 49160 | tf_op jit(solution)/shard_map/ppermute | solution.py:550
  30.7 1.8 %collective-permute-done.11.second_ref = f32[32,128]{1,0:T(8,128)S(1)} collective-permute-done((f32[32,128]{1,0:T(8,128)S(1)}, f32[32,128]{1,0:T(8,128)S(1)}, u32[]{:S(2)}, u32[]{:S(2)}) %collective-permute-start.11) | collective-permute-done | bytes 16416 | tf_op jit(solution)/shard_map/ppermute | solution.py:550
  32.6 1.2 %collective-permute-done.8 = bf16[4,128,512]{2,1,0:T(8,128)(2,1)S(1)} collective-permute-done((bf16[4,128,512]{2,1,0:T(8,128)(2,1)S(1)}, bf16[4,128,512]{2,1,0:T(8,128)(2,1)S(1)}, u32[]{:S(2)}, u32[]{:S(2)}) %collective-permute-start.8) | collective-permute-done | bytes 524320 | tf_op jit(solution)/shard_map/ppermute | solution.py:601
  33.8 2.3 %shard_map.82 = (f32[2112,128]{1,0:T(8,128)S(1)}, f32[2112,128]{1,0:T(8,128)S(1)}, f32[32,128]{1,0:T(8,128)S(1)}, f32[32,128]{1,0:T(8,128)S(1)}) custom-call(s32[16]{0:T(128)S(1)} %get-tuple-element.35.spans_ref, s32[8,1,1024]{2,1,0:T(1,128)S(1)} %get-tuple-element.36.code_ref, s32[8,1,1024]{2,1,0:T(1,128)S(1)} %get-tuple-element.37.lane_ref, ...), custom_call_target="tpu_custom_call" | custom-call | tf_op jit(solution)/shard_map/pallas_call | solution.py:610
  36.1 0.6 %collective-permute-start.12 = (f32[32,128]{1,0:T(8,128)S(1)}, f32[32,128]{1,0:T(8,128)S(1)}, u32[]{:S(2)}, u32[]{:S(2)}) collective-permute-start(f32[32,128]{1,0:T(8,128)S(1)} %get-tuple-element.56), channel_id=1, source_target_pairs={{0,4},{8,12},{16,20},{24,28},{4,0},{12,8},{20,16},{28,24},{1,5},{9... | collective-permute-start | bytes 49160 | tf_op jit(solution)/shard_map/ppermute | solution.py:550
  36.7 5.3 %collective-permute-start.13 = (f32[32,128]{1,0:T(8,128)S(1)}, f32[32,128]{1,0:T(8,128)S(1)}, u32[]{:S(2)}, u32[]{:S(2)}) collective-permute-start(f32[32,128]{1,0:T(8,128)S(1)} %get-tuple-element.57), channel_id=1, source_target_pairs={{4,8},{12,16},{20,24},{8,4},{16,12},{24,20},{5,9},{13,17},{21,25},... | collective-permute-start | bytes 49160 | tf_op jit(solution)/shard_map/ppermute | solution.py:550
  42.0 4.5 %shard_map.83 = (bf16[4,456,128]{2,1,0:T(8,128)(2,1)}, bf16[4,456,128]{2,1,0:T(8,128)(2,1)S(1)}, f32[64,128]{1,0:T(8,128)S(1)}) custom-call(s32[16]{0:T(128)S(1)} %get-tuple-element.35.spans_ref, s32[8,1,1024]{2,1,0:T(1,128)S(1)} %get-tuple-element.36.code_ref, s32[8,1,1024]{2,1,0:T(1,128)S(1)} %get-tuple-element.37.lane_ref, ...), custom_call_target="tpu_custom_call" | custom-call | flops 67108864 | bytes 16777216 | tf_op jit(solution)/shard_map/pallas_call | solution.py:625
  46.5 1.0 %shard_map.84 = bf16[4,456,128]{2,1,0:T(8,128)(2,1)} custom-call(f32[32,128]{1,0:T(8,128)S(1)} %collective-permute-done.12.first_ref, f32[32,128]{1,0:T(8,128)S(1)} %collective-permute-done.13.second_ref, f32[64,128]{1,0:T(8,128)S(1)} %get-tuple-element.58.rows_ref, bf16[4,456,128]{2,1,0:T(8,128)(2,1)S(1)} %get-tuple-element.59.corrected_ref), custom_call_target="tpu_custom_call" | custom-call | tf_op jit(solution)/shard_map/pallas_call | solution.py:648
  (22 shorter events, 0.1 us)
Async XLA Ops:
  0.6 15.5 %collective-permute-start.7 = (bf16[16,456,456]{2,1,0:T(8,128)(2,1)}, bf16[16,456,456]{2,1,0:T(8,128)(2,1)S(1)}, u32[]{:S(2)}, u32[]{:S(2)}) collective-permute-start(bf16[16,456,456]{2,1,0:T(8,128)(2,1)} %operators_hbm.2), channel_id=1, source_target_pairs={{1,0},{0,1},{3,2},{2,3},{5,4},{4,5},{7,6},{6,7},{9,8},{8,9},{11,10... | collective-permute-start | bytes 19961864 | tf_op jit(solution)/shard_map/ppermute | solution.py:568
  2.6 5.9 %collective-permute-start = (bf16[4,32,456]{2,1,0:T(8,128)(2,1)S(1)}, bf16[4,32,456]{2,1,0:T(8,128)(2,1)S(1)}, u32[]{:S(2)}, u32[]{:S(2)}) collective-permute-start(bf16[4,32,456]{2,1,0:T(8,128)(2,1)S(1)} %get-tuple-element.31), channel_id=1, source_target_pairs={{0,4},{4,0},{8,12},{12,8},{16,20},{20,16},{24,28},{28,24},{1,5},{5... | collective-permute-start | bytes 350216 | tf_op jit(solution)/shard_map/ppermute | solution.py:146
  3.2 7.0 %collective-permute-start.1 = (bf16[32,456]{1,0:T(8,128)(2,1)S(1)}, bf16[32,456]{1,0:T(8,128)(2,1)S(1)}, u32[]{:S(2)}, u32[]{:S(2)}) collective-permute-start(bf16[32,456]{1,0:T(8,128)(2,1)S(1)} %get-tuple-element.39), channel_id=1, source_target_pairs={{0,8},{4,12},{8,0},{12,4},{16,24},{20,28},{24,16},{28,20},{1,9},{5... | collective-permute-start | bytes 87560 | tf_op jit(solution)/shard_map/ppermute | solution.py:146
  3.2 8.2 %collective-permute-start.3 = (bf16[32,456]{1,0:T(8,128)(2,1)S(1)}, bf16[32,456]{1,0:T(8,128)(2,1)S(1)}, u32[]{:S(2)}, u32[]{:S(2)}) collective-permute-start(bf16[32,456]{1,0:T(8,128)(2,1)S(1)} %get-tuple-element.40), channel_id=1, source_target_pairs={{0,16},{4,20},{8,24},{12,28},{16,0},{20,4},{24,8},{28,12},{1,17},{... | collective-permute-start | bytes 87560 | tf_op jit(solution)/shard_map/ppermute | solution.py:146
  6.3 9.8 %collective-permute-start.5 = (bf16[32,456]{1,0:T(8,128)(2,1)S(1)}, bf16[32,456]{1,0:T(8,128)(2,1)S(1)}, u32[]{:S(2)}, u32[]{:S(2)}) collective-permute-start(bf16[32,456]{1,0:T(8,128)(2,1)S(1)} %get-tuple-element.41), channel_id=1, source_target_pairs={{0,24},{4,28},{8,16},{12,20},{16,8},{20,12},{24,0},{28,4},{1,25},{... | collective-permute-start | bytes 87560 | tf_op jit(solution)/shard_map/ppermute | solution.py:146
  8.6 7.5 %collective-permute-start.6 = (bf16[32,456]{1,0:T(8,128)(2,1)S(1)}, bf16[32,456]{1,0:T(8,128)(2,1)S(1)}, u32[]{:S(2)}, u32[]{:S(2)}) collective-permute-start(bf16[32,456]{1,0:T(8,128)(2,1)S(1)} %get-tuple-element.60), channel_id=1, source_target_pairs={{0,24},{4,28},{8,16},{12,20},{16,8},{20,12},{24,0},{28,4},{1,25},{... | collective-permute-start | bytes 87560 | tf_op jit(solution)/shard_map/ppermute | solution.py:146
  10.2 5.8 %collective-permute-start.4 = (bf16[32,456]{1,0:T(8,128)(2,1)S(1)}, bf16[32,456]{1,0:T(8,128)(2,1)S(1)}, u32[]{:S(2)}, u32[]{:S(2)}) collective-permute-start(bf16[32,456]{1,0:T(8,128)(2,1)S(1)} %get-tuple-element.61), channel_id=1, source_target_pairs={{0,16},{4,20},{8,24},{12,28},{16,0},{20,4},{24,8},{28,12},{1,17},{... | collective-permute-start | bytes 87560 | tf_op jit(solution)/shard_map/ppermute | solution.py:146
  11.5 4.6 %collective-permute-start.2 = (bf16[32,456]{1,0:T(8,128)(2,1)S(1)}, bf16[32,456]{1,0:T(8,128)(2,1)S(1)}, u32[]{:S(2)}, u32[]{:S(2)}) collective-permute-start(bf16[32,456]{1,0:T(8,128)(2,1)S(1)} %get-tuple-element.62), channel_id=1, source_target_pairs={{0,8},{4,12},{8,0},{12,4},{16,24},{20,28},{24,16},{28,20},{1,9},{5... | collective-permute-start | bytes 87560 | tf_op jit(solution)/shard_map/ppermute | solution.py:146
  19.1 5.1 %collective-permute-start.9 = (f32[2,32,128]{2,1,0:T(8,128)S(1)}, f32[2,32,128]{2,1,0:T(8,128)S(1)}, u32[]{:S(2)}, u32[]{:S(2)}) collective-permute-start(f32[2,32,128]{2,1,0:T(8,128)S(1)} %get-tuple-element.48), channel_id=1, source_target_pairs={{0,2},{1,3},{2,0},{3,1},{4,6},{5,7},{6,4},{7,5},{8,10},{9,11},{10,... | collective-permute-start | bytes 98312 | tf_op jit(solution)/shard_map/ppermute | solution.py:600
  20.7 13.0 %collective-permute-start.8 = (bf16[4,128,512]{2,1,0:T(8,128)(2,1)S(1)}, bf16[4,128,512]{2,1,0:T(8,128)(2,1)S(1)}, u32[]{:S(2)}, u32[]{:S(2)}) collective-permute-start(bf16[4,128,512]{2,1,0:T(8,128)(2,1)S(1)} %get-tuple-element.46), channel_id=1, source_target_pairs={{0,2},{1,3},{2,0},{3,1},{4,6},{5,7},{6,4},{7,5},{8,10},{9,11},{10,... | collective-permute-start | bytes 1572872 | tf_op jit(solution)/shard_map/ppermute | solution.py:601
  24.3 9.5 %slice-start = ((s8[16777216]{0:T(1024)(128)(4,1)}), s8[4194304]{0:T(1024)(128)(4,1)S(1)}, s32[]{:S(2)}) async-start(s8[16777216]{0:T(1024)(128)(4,1)} %bitcast.14), calls=%async_computation | async-start | bytes 8388608
  24.3 9.5 %slice-start.1 = ((s8[16777216]{0:T(1024)(128)(4,1)}), s8[4194304]{0:T(1024)(128)(4,1)S(1)}, s32[]{:S(2)}) async-start(s8[16777216]{0:T(1024)(128)(4,1)} %bitcast.14), calls=%async_computation.1 | async-start | bytes 8388608
  24.3 9.5 %slice-start.2 = ((s8[16777216]{0:T(1024)(128)(4,1)}), s8[4194304]{0:T(1024)(128)(4,1)S(1)}, s32[]{:S(2)}) async-start(s8[16777216]{0:T(1024)(128)(4,1)} %bitcast.14), calls=%async_computation.2 | async-start | bytes 8388608
  24.3 9.5 %slice-start.3 = ((s8[16777216]{0:T(1024)(128)(4,1)}), s8[4194304]{0:T(1024)(128)(4,1)S(1)}, s32[]{:S(2)}) async-start(s8[16777216]{0:T(1024)(128)(4,1)} %bitcast.14), calls=%async_computation.3 | async-start | bytes 8388608
  25.0 5.7 %collective-permute-start.10 = (f32[32,128]{1,0:T(8,128)S(1)}, f32[32,128]{1,0:T(8,128)S(1)}, u32[]{:S(2)}, u32[]{:S(2)}) collective-permute-start(f32[32,128]{1,0:T(8,128)S(1)} %get-tuple-element.49), channel_id=1, source_target_pairs={{0,4},{8,12},{16,20},{24,28},{4,0},{12,8},{20,16},{28,24},{1,5},{9... | collective-permute-start | bytes 49160 | tf_op jit(solution)/shard_map/ppermute | solution.py:550
  25.6 6.9 %collective-permute-start.11 = (f32[32,128]{1,0:T(8,128)S(1)}, f32[32,128]{1,0:T(8,128)S(1)}, u32[]{:S(2)}, u32[]{:S(2)}) collective-permute-start(f32[32,128]{1,0:T(8,128)S(1)} %get-tuple-element.50), channel_id=1, source_target_pairs={{4,8},{12,16},{20,24},{8,4},{16,12},{24,20},{5,9},{13,17},{21,25},... | collective-permute-start | bytes 49160 | tf_op jit(solution)/shard_map/ppermute | solution.py:550
  36.1 10.4 %collective-permute-start.12 = (f32[32,128]{1,0:T(8,128)S(1)}, f32[32,128]{1,0:T(8,128)S(1)}, u32[]{:S(2)}, u32[]{:S(2)}) collective-permute-start(f32[32,128]{1,0:T(8,128)S(1)} %get-tuple-element.56), channel_id=1, source_target_pairs={{0,4},{8,12},{16,20},{24,28},{4,0},{12,8},{20,16},{28,24},{1,5},{9... | collective-permute-start | bytes 49160 | tf_op jit(solution)/shard_map/ppermute | solution.py:550
  36.7 9.8 %collective-permute-start.13 = (f32[32,128]{1,0:T(8,128)S(1)}, f32[32,128]{1,0:T(8,128)S(1)}, u32[]{:S(2)}, u32[]{:S(2)}) collective-permute-start(f32[32,128]{1,0:T(8,128)S(1)} %get-tuple-element.57), channel_id=1, source_target_pairs={{4,8},{12,16},{20,24},{8,4},{16,12},{24,20},{5,9},{13,17},{21,25},... | collective-permute-start | bytes 49160 | tf_op jit(solution)/shard_map/ppermute | solution.py:550

commit v6 on v5

--- a/solution.py
+++ b/solution.py
@@ -280,14 +280,54 @@
                 c * slots : (c + 1) * slots
             ]
     total = jnp.dot(picks_ref[...], terms[...], preferred_element_type=jnp.float32)
-    total = total.astype(out_ref.dtype)
+    if out_ref.shape[0] != share:
+        total = total.astype(out_ref.dtype).astype(jnp.float32)
+        for at, part in enumerate(pack_columns(total, share, tiles, width)):
+            out_ref[at] = part.astype(out_ref.dtype)
     for c in range(share):
-        out_ref[c] = total[:, c * stride : (c + 1) * stride]
+        if out_ref.shape[0] == share:
+            out_ref[c] = total[:, c * stride : (c + 1) * stride].astype(out_ref.dtype)
         for t in range(tiles):
             at = (c * tiles + t) * LANES
             to = pl.ds(c * tiles + t, RIM, stride=share * tiles)
-            edge_ref[0, to, :] = total[:RIM, at : at + LANES].astype(jnp.float32)
-            edge_ref[1, to, :] = total[boxes - RIM :, at : at + LANES].astype(jnp.float32)
+            edge_ref[0, to, :] = total[:RIM, at : at + LANES]
+            edge_ref[1, to, :] = total[boxes - RIM :, at : at + LANES]
+
+
+def pack_columns(total, share, tiles, width):
+    last = width - (tiles - 1) * LANES
+    blocks, tails = [], []
+    for c in range(share):
+        for t in range(tiles):
+            at = (c * tiles + t) * LANES
+            if t < tiles - 1:
+                blocks.append(total[:, at : at + LANES])
+            else:
+                tails.append(total[:, at : at + last])
+    rest = -(share * last) % LANES
+    if rest:
+        tails.append(jnp.zeros((total.shape[0], rest), total.dtype))
+    tails = jnp.concatenate(tails, axis=1)
+    return blocks + [tails[:, at : at + LANES] for at in range(0, tails.shape[1], LANES)]
+
+
+def packed_blocks(share, tiles, width):
+    last = width - (tiles - 1) * LANES
+    return share * (tiles - 1) + round_up(share * last, LANES) // LANES
+
+
+def unpack_columns(blocks, share, tiles, width):
+    last = width - (tiles - 1) * LANES
+    full = share * (tiles - 1)
+    tails = jnp.concatenate(blocks[full:], axis=1)
+    blank = jnp.zeros((tails.shape[0], LANES - last), tails.dtype)
+    columns = []
+    for c in range(share):
+        tail = tails[:, c * last : (c + 1) * last]
+        if last < LANES:
+            tail = jnp.concatenate([tail, blank], axis=1)
+        columns.append(blocks[c * (tiles - 1) : (c + 1) * (tiles - 1)] + [tail])
+    return columns
 
 
 def field_call(imported, picks, ready, pending, share, capacity, group, dtype):
@@ -295,6 +335,9 @@
     boxes, all_slots = picks.shape
     arrivals = len(imported)
     stride = round_up(width, LANES)
+    shape = (share, boxes, stride)
+    if dtype == jnp.bfloat16:
+        shape = (packed_blocks(share, stride // LANES, width), boxes, LANES)
     fetched = sum(count for _, _, count, _ in pending)
     held = all_slots * share * stride * 2 + fetched * width * stride * 2
     return pl.pallas_call(
@@ -303,7 +346,7 @@
             [at for _, at in ready], [entry[1:] for entry in pending],
         ),
         out_shape=[
-            jax.ShapeDtypeStruct((share, boxes, stride), dtype),
+            jax.ShapeDtypeStruct(shape, dtype),
             jax.ShapeDtypeStruct((2, RIM * share * (stride // LANES), LANES), jnp.float32),
         ],
         in_specs=[VMEM] * (arrivals + 1 + len(ready)) + [ANY] * len(pending),
@@ -417,7 +460,7 @@
 
 
 def early_kernel(
-    spans_ref, code_ref, lane_ref, own_ref, received_ref, inverses_ref, first_ref, second_ref,
+    width, spans_ref, code_ref, lane_ref, own_ref, received_ref, inverses_ref, first_ref, second_ref,
     rows_in, lanes_in,
     ext, spread, first_out, second_out, order_ref,
 ):
@@ -433,11 +476,15 @@
     spread[...] = jnp.zeros_like(spread)
     ext[:rim, :] = jnp.where(even, second, first)
     ext[end:, :] = jnp.where(even, first, second)
+    received = []
+    for r in range(received_ref.shape[0]):
+        blocks = [received_ref[r, k].astype(jnp.float32) for k in range(received_ref.shape[1])]
+        received.append(unpack_columns(blocks, share, tiles, width))
     for c in range(share):
         for t in range(tiles):
             part = own_ref[c, :, t * LANES : (t + 1) * LANES]
-            for r in range(received_ref.shape[0]):
-                part = part + received_ref[r, c, :, t * LANES : (t + 1) * LANES].astype(jnp.float32)
+            for columns in received:
+                part = part + columns[c][t]
             part = part.astype(jnp.bfloat16).astype(jnp.float32)
             ext[pl.ds(rim + c * tiles + t, boxes, stride=per_box), :] = part
     batch = batch_size(patches)
@@ -608,7 +655,7 @@
     rim = RIM * per_box
     side = jax.ShapeDtypeStruct((rim, LANES), jnp.float32)
     ext, early, first, second = pl.pallas_call(
-        early_kernel,
+        functools.partial(early_kernel, width),
         out_shape=[
             pltpu.VMEM((ext_rows, LANES), jnp.float32),
             pltpu.VMEM((ext_rows, LANES), jnp.float32),

time: 47.3 us -> 46.6 us (0.985); the launches traced: 47.6 us -> 46.3 us
  starting transfers between devices: 22.1 us -> 21.1 us
  waiting for transfers between devices: 4.92 us -> 4.21 us
    ppermute x2, starting transfers between devices: 10.4 us -> 8.93 us  [swap_sides(): lax.ppermute(second, 'box', moves(1))]
    ppermute x1, waiting for transfers between devices: 1.21 us -> 0.5 us  [body(): parts.append(lax.ppermute(part, 'col', moves))]
  transfers between devices with their start and end apart: 14 -> 14, of which waited for: 3 -> 3; matrix products, arithmetic and copies ran while one was open for 0% -> 0% of each run, Pallas kernels for 28% -> 29%
where the time goes in v6:
time: 46.6 us; the launch traced here: 46.3 us
  starting transfers between devices  21.1 us (45%)
  Pallas kernels  20 us (43%)
  waiting for transfers between devices  4.21 us (9%)
  between operations  1 us (2%)
    ppermute x2, starting transfers between devices, swap_sides(): lax.ppermute(second, 'box', moves(1))  8.93 us
    ppermute x7, starting transfers between devices, swap(): return lax.ppermute(x, 'box', [(i, i ^ mask) for i in range(count)])  8.28 us
    pallas_call x2, Pallas kernels, field_call(): pl.pallas_call(functools.partial(field_kernel, share, capacity, group, ar...  6.12 us
    pallas_call x1, Pallas kernels, body(): pl.pallas_call(late_kernel, out_shape=[jax.ShapeDtypeStruct((share, width...  4.7 us
    pallas_call x1, Pallas kernels, prepare_call(): pl.pallas_call(functools.partial(prepare_kernel, slots, tiles, width, loc...  3.25 us
    pallas_call x1, Pallas kernels, body(): pl.pallas_call(functools.partial(early_kernel, width), out_shape=[pltpu.V...  2.28 us
    pallas_call x1, Pallas kernels, pick_call(): pl.pallas_call(functools.partial(pick_kernel, share, swaps, load), out_sh...  1.92 us
    ppermute x7, waiting for transfers between devices, swap(): return lax.ppermute(x, 'box', [(i, i ^ mask) for i in range(count)])  1.87 us
  transfers between devices with their start and end apart: 14, of which 3 were waited for; matrix products, arithmetic and copies ran while one was open for 0% of the time, Pallas kernels for 29%

profile of v6, /device:TPU:10, one launch (start us, length us, event | category | flops | bytes accessed | tf_op | source)
XLA Modules:
  0.0 46.3 jit_solution(10327599244812205708)
XLA Ops:
  0.6 0.1 collective-permute-start.7
  0.7 1.9 %shard_map.77 = (bf16[32,456]{1,0:T(8,128)(2,1)S(1)}, bf16[32,456]{1,0:T(8,128)(2,1)S(1)}, bf16[32,456]{1,0:T(8,128)(2,1)S(1)}, bf16[32,456]{1,0:T(8,128)(2,1)S(...) custom-call(s32[4,8]{1,0:T(4,128)} %bitcast.20, bf16[16,456,128]{2,1,0:T(8,128)(2,1)} %bitcast.17, ...), custom_call_target="tpu_custom_call" | custom-call | tf_op jit(solution)/shard_map/pallas_call | solution.py:122
  2.6 0.6 %collective-permute-start = (bf16[4,32,456]{2,1,0:T(8,128)(2,1)S(1)}, bf16[4,32,456]{2,1,0:T(8,128)(2,1)S(1)}, u32[]{:S(2)}, u32[]{:S(2)}) collective-permute-start(bf16[4,32,456]{2,1,0:T(8,128)(2,1)S(1)} %get-tuple-element.31), channel_id=1, source_target_pairs={{0,4},{4,0},{8,12},{12,8},{16,20},{20,16},{24,28},{28,24},{1,5},{5... | collective-permute-start | bytes 350216 | tf_op jit(solution)/shard_map/ppermute | solution.py:146
  3.2 3.0 %collective-permute-start.3 = (bf16[32,456]{1,0:T(8,128)(2,1)S(1)}, bf16[32,456]{1,0:T(8,128)(2,1)S(1)}, u32[]{:S(2)}, u32[]{:S(2)}) collective-permute-start(bf16[32,456]{1,0:T(8,128)(2,1)S(1)} %get-tuple-element.40), channel_id=1, source_target_pairs={{0,16},{4,20},{8,24},{12,28},{16,0},{20,4},{24,8},{28,12},{1,17},{... | collective-permute-start | bytes 87560 | tf_op jit(solution)/shard_map/ppermute | solution.py:146
  6.3 0.5 collective-permute-start.5
  6.7 1.9 %collective-permute-done.refs_1_ = bf16[4,32,456]{2,1,0:T(8,128)(2,1)S(1)} collective-permute-done((bf16[4,32,456]{2,1,0:T(8,128)(2,1)S(1)}, bf16[4,32,456]{2,1,0:T(8,128)(2,1)S(1)}, u32[]{:S(2)}, u32[]{:S(2)}) %collective-permute-start) | collective-permute-done | bytes 116768 | tf_op jit(solution)/shard_map/ppermute | solution.py:146
  8.6 1.6 %collective-permute-start.6 = (bf16[32,456]{1,0:T(8,128)(2,1)S(1)}, bf16[32,456]{1,0:T(8,128)(2,1)S(1)}, u32[]{:S(2)}, u32[]{:S(2)}) collective-permute-start(bf16[32,456]{1,0:T(8,128)(2,1)S(1)} %get-tuple-element.60), channel_id=1, source_target_pairs={{0,24},{4,28},{8,16},{12,20},{16,8},{20,12},{24,0},{28,4},{1,25},{... | collective-permute-start | bytes 87560 | tf_op jit(solution)/shard_map/ppermute | solution.py:146
  10.2 1.2 %collective-permute-start.4 = (bf16[32,456]{1,0:T(8,128)(2,1)S(1)}, bf16[32,456]{1,0:T(8,128)(2,1)S(1)}, u32[]{:S(2)}, u32[]{:S(2)}) collective-permute-start(bf16[32,456]{1,0:T(8,128)(2,1)S(1)} %get-tuple-element.61), channel_id=1, source_target_pairs={{0,16},{4,20},{8,24},{12,28},{16,0},{20,4},{24,8},{28,12},{1,17},{... | collective-permute-start | bytes 87560 | tf_op jit(solution)/shard_map/ppermute | solution.py:146
  11.5 1.3 %collective-permute-start.2 = (bf16[32,456]{1,0:T(8,128)(2,1)S(1)}, bf16[32,456]{1,0:T(8,128)(2,1)S(1)}, u32[]{:S(2)}, u32[]{:S(2)}) collective-permute-start(bf16[32,456]{1,0:T(8,128)(2,1)S(1)} %get-tuple-element.62), channel_id=1, source_target_pairs={{0,8},{4,12},{8,0},{12,4},{16,24},{20,28},{24,16},{28,20},{1,9},{5... | collective-permute-start | bytes 87560 | tf_op jit(solution)/shard_map/ppermute | solution.py:146
  12.8 3.2 %shard_map.78 = (bf16[128,1024]{1,0:T(8,128)(2,1)S(1)}, s32[8,1,1024]{2,1,0:T(1,128)S(1)}, s32[8,1,1024]{2,1,0:T(1,128)S(1)}, s32[16]{0:T(128)S(1)}, bf16[12,456,456]{2,1,0:T(8,128)(2,1)S(1)}) custom-call(s32[64,128]{1,0:T(8,128)} %bitcast.19, s32[8,1024]{1,0:T(8,128)} %points_hbm, bf16[16,456,456]{2,1,0:T(8,128)(2,1)} %operators_hbm.2), custom_call_target="tpu_custom_call" | custom-call | tf_op jit(solution)/shard_map/pallas_call | solution.py:207
  16.1 3.1 %shard_map.80 = (bf16[15,128,128]{2,1,0:T(8,128)(2,1)S(1)}, f32[2,32,128]{2,1,0:T(8,128)S(1)}) custom-call(bf16[32,456]{1,0:T(8,128)(2,1)S(1)} %get-tuple-element.38.refs_0_, bf16[4,32,456]{2,1,0:T(8,128)(2,1)S(1)} %collective-permute-done.refs_1_, bf16[32,456]{1,0:T(8,128)(2,1)S(1)} %collective-permute-done.1.refs_2_, ...), custom_call_target="tpu_custom_call" | custom-call | flops 2181562368 | bytes 4194304 | tf_op jit(solution)/shard_map/pallas_call | solution.py:343
  19.2 1.6 %collective-permute-start.9 = (f32[2,32,128]{2,1,0:T(8,128)S(1)}, f32[2,32,128]{2,1,0:T(8,128)S(1)}, u32[]{:S(2)}, u32[]{:S(2)}) collective-permute-start(f32[2,32,128]{2,1,0:T(8,128)S(1)} %get-tuple-element.48), channel_id=1, source_target_pairs={{0,2},{1,3},{2,0},{3,1},{4,6},{5,7},{6,4},{7,5},{8,10},{9,11},{10,... | collective-permute-start | bytes 98312 | tf_op jit(solution)/shard_map/ppermute | solution.py:647
  20.8 0.5 %collective-permute-start.8 = (bf16[15,128,128]{2,1,0:T(8,128)(2,1)S(1)}, bf16[15,128,128]{2,1,0:T(8,128)(2,1)S(1)}, u32[]{:S(2)}, u32[]{:S(2)}) collective-permute-start(bf16[15,128,128]{2,1,0:T(8,128)(2,1)S(1)} %get-tuple-element.46), channel_id=1, source_target_pairs={{0,2},{1,3},{2,0},{3,1},{4,6},{5,7},{6,4},{7,5},{8,10},{9,11},{10,... | collective-permute-start | bytes 1474568 | tf_op jit(solution)/shard_map/ppermute | solution.py:648
  21.3 3.0 %shard_map.79 = (f32[4,128,512]{2,1,0:T(8,128)S(1)}, f32[2,32,128]{2,1,0:T(8,128)S(1)}) custom-call(bf16[32,456]{1,0:T(8,128)(2,1)S(1)} %get-tuple-element.38.refs_0_, bf16[4,32,456]{2,1,0:T(8,128)(2,1)S(1)} %collective-permute-done.refs_1_, bf16[32,456]{1,0:T(8,128)(2,1)S(1)} %collective-permute-done.1.refs_2_, ...), custom_call_target="tpu_custom_call" | custom-call | flops 2181562368 | bytes 4194304 | tf_op jit(solution)/shard_map/pallas_call | solution.py:343
  24.4 0.7 %shard_map.81 = (f32[32,128]{1,0:T(8,128)S(1)}, f32[32,128]{1,0:T(8,128)S(1)}, bf16[8,128,1024]{2,1,0:T(8,128)(2,1)S(1)}, bf16[8,128,1024]{2,1,0:T(8,128)(2,1)S(1)}) custom-call(s32[8,1,1024]{2,1,0:T(1,128)S(1)} %get-tuple-element.36.code_ref, s32[8,1,1024]{2,1,0:T(1,128)S(1)} %get-tuple-element.37.lane_ref, f32[2,32,128]{2,1,0:T(8,128)S(1)} %get-tuple-element.47.refs_0_, ...), custom_call_target="tpu_custom_call" | custom-call | flops 10000000000 | tf_op jit(solution)/shard_map/pallas_call | solution.py:396
  25.1 0.6 %collective-permute-start.10 = (f32[32,128]{1,0:T(8,128)S(1)}, f32[32,128]{1,0:T(8,128)S(1)}, u32[]{:S(2)}, u32[]{:S(2)}) collective-permute-start(f32[32,128]{1,0:T(8,128)S(1)} %get-tuple-element.49), channel_id=1, source_target_pairs={{0,4},{8,12},{16,20},{24,28},{4,0},{12,8},{20,16},{28,24},{1,5},{9... | collective-permute-start | bytes 49160 | tf_op jit(solution)/shard_map/ppermute | solution.py:597
  25.7 5.1 %collective-permute-start.11 = (f32[32,128]{1,0:T(8,128)S(1)}, f32[32,128]{1,0:T(8,128)S(1)}, u32[]{:S(2)}, u32[]{:S(2)}) collective-permute-start(f32[32,128]{1,0:T(8,128)S(1)} %get-tuple-element.50), channel_id=1, source_target_pairs={{4,8},{12,16},{20,24},{8,4},{16,12},{24,20},{5,9},{13,17},{21,25},... | collective-permute-start | bytes 49160 | tf_op jit(solution)/shard_map/ppermute | solution.py:597
  30.8 1.8 %collective-permute-done.11.second_ref = f32[32,128]{1,0:T(8,128)S(1)} collective-permute-done((f32[32,128]{1,0:T(8,128)S(1)}, f32[32,128]{1,0:T(8,128)S(1)}, u32[]{:S(2)}, u32[]{:S(2)}) %collective-permute-start.11) | collective-permute-done | bytes 16416 | tf_op jit(solution)/shard_map/ppermute | solution.py:597
  32.6 0.5 %collective-permute-done.8 = bf16[15,128,128]{2,1,0:T(8,128)(2,1)S(1)} collective-permute-done((bf16[15,128,128]{2,1,0:T(8,128)(2,1)S(1)}, bf16[15,128,128]{2,1,0:T(8,128)(2,1)S(1)}, u32[]{:S(2)}, u32[]{:S(2)}) %collective-permute-start.8) | collective-permute-done | bytes 491552 | tf_op jit(solution)/shard_map/ppermute | solution.py:648
  33.1 2.3 %shard_map.82 = (f32[2112,128]{1,0:T(8,128)S(1)}, f32[2112,128]{1,0:T(8,128)S(1)}, f32[32,128]{1,0:T(8,128)S(1)}, f32[32,128]{1,0:T(8,128)S(1)}) custom-call(s32[16]{0:T(128)S(1)} %get-tuple-element.35.spans_ref, s32[8,1,1024]{2,1,0:T(1,128)S(1)} %get-tuple-element.36.code_ref, s32[8,1,1024]{2,1,0:T(1,128)S(1)} %get-tuple-element.37.lane_ref, ...), custom_call_target="tpu_custom_call" | custom-call | tf_op jit(solution)/shard_map/pallas_call | solution.py:657
  35.4 1.1 %collective-permute-start.12 = (f32[32,128]{1,0:T(8,128)S(1)}, f32[32,128]{1,0:T(8,128)S(1)}, u32[]{:S(2)}, u32[]{:S(2)}) collective-permute-start(f32[32,128]{1,0:T(8,128)S(1)} %get-tuple-element.56), channel_id=1, source_target_pairs={{0,4},{8,12},{16,20},{24,28},{4,0},{12,8},{20,16},{28,24},{1,5},{9... | collective-permute-start | bytes 49160 | tf_op jit(solution)/shard_map/ppermute | solution.py:597
  36.5 3.9 %collective-permute-start.13 = (f32[32,128]{1,0:T(8,128)S(1)}, f32[32,128]{1,0:T(8,128)S(1)}, u32[]{:S(2)}, u32[]{:S(2)}) collective-permute-start(f32[32,128]{1,0:T(8,128)S(1)} %get-tuple-element.57), channel_id=1, source_target_pairs={{4,8},{12,16},{20,24},{8,4},{16,12},{24,20},{5,9},{13,17},{21,25},... | collective-permute-start | bytes 49160 | tf_op jit(solution)/shard_map/ppermute | solution.py:597
  40.4 4.7 %shard_map.83 = (bf16[4,456,128]{2,1,0:T(8,128)(2,1)}, bf16[4,456,128]{2,1,0:T(8,128)(2,1)S(1)}, f32[64,128]{1,0:T(8,128)S(1)}) custom-call(s32[16]{0:T(128)S(1)} %get-tuple-element.35.spans_ref, s32[8,1,1024]{2,1,0:T(1,128)S(1)} %get-tuple-element.36.code_ref, s32[8,1,1024]{2,1,0:T(1,128)S(1)} %get-tuple-element.37.lane_ref, ...), custom_call_target="tpu_custom_call" | custom-call | flops 67108864 | bytes 16777216 | tf_op jit(solution)/shard_map/pallas_call | solution.py:672
  45.1 1.0 %shard_map.84 = bf16[4,456,128]{2,1,0:T(8,128)(2,1)} custom-call(f32[32,128]{1,0:T(8,128)S(1)} %collective-permute-done.12.first_ref, f32[32,128]{1,0:T(8,128)S(1)} %collective-permute-done.13.second_ref, f32[64,128]{1,0:T(8,128)S(1)} %get-tuple-element.58.rows_ref, bf16[4,456,128]{2,1,0:T(8,128)(2,1)S(1)} %get-tuple-element.59.corrected_ref), custom_call_target="tpu_custom_call" | custom-call | tf_op jit(solution)/shard_map/pallas_call | solution.py:695
  (22 shorter events, 0.1 us)
Async XLA Ops:
  0.6 15.5 %collective-permute-start.7 = (bf16[16,456,456]{2,1,0:T(8,128)(2,1)}, bf16[16,456,456]{2,1,0:T(8,128)(2,1)S(1)}, u32[]{:S(2)}, u32[]{:S(2)}) collective-permute-start(bf16[16,456,456]{2,1,0:T(8,128)(2,1)} %operators_hbm.2), channel_id=1, source_target_pairs={{1,0},{0,1},{3,2},{2,3},{5,4},{4,5},{7,6},{6,7},{9,8},{8,9},{11,10... | collective-permute-start | bytes 19961864 | tf_op jit(solution)/shard_map/ppermute | solution.py:615
  2.6 5.9 %collective-permute-start = (bf16[4,32,456]{2,1,0:T(8,128)(2,1)S(1)}, bf16[4,32,456]{2,1,0:T(8,128)(2,1)S(1)}, u32[]{:S(2)}, u32[]{:S(2)}) collective-permute-start(bf16[4,32,456]{2,1,0:T(8,128)(2,1)S(1)} %get-tuple-element.31), channel_id=1, source_target_pairs={{0,4},{4,0},{8,12},{12,8},{16,20},{20,16},{24,28},{28,24},{1,5},{5... | collective-permute-start | bytes 350216 | tf_op jit(solution)/shard_map/ppermute | solution.py:146
  3.2 7.0 %collective-permute-start.1 = (bf16[32,456]{1,0:T(8,128)(2,1)S(1)}, bf16[32,456]{1,0:T(8,128)(2,1)S(1)}, u32[]{:S(2)}, u32[]{:S(2)}) collective-permute-start(bf16[32,456]{1,0:T(8,128)(2,1)S(1)} %get-tuple-element.39), channel_id=1, source_target_pairs={{0,8},{4,12},{8,0},{12,4},{16,24},{20,28},{24,16},{28,20},{1,9},{5... | collective-permute-start | bytes 87560 | tf_op jit(solution)/shard_map/ppermute | solution.py:146
  3.2 8.2 %collective-permute-start.3 = (bf16[32,456]{1,0:T(8,128)(2,1)S(1)}, bf16[32,456]{1,0:T(8,128)(2,1)S(1)}, u32[]{:S(2)}, u32[]{:S(2)}) collective-permute-start(bf16[32,456]{1,0:T(8,128)(2,1)S(1)} %get-tuple-element.40), channel_id=1, source_target_pairs={{0,16},{4,20},{8,24},{12,28},{16,0},{20,4},{24,8},{28,12},{1,17},{... | collective-permute-start | bytes 87560 | tf_op jit(solution)/shard_map/ppermute | solution.py:146
  6.3 9.8 %collective-permute-start.5 = (bf16[32,456]{1,0:T(8,128)(2,1)S(1)}, bf16[32,456]{1,0:T(8,128)(2,1)S(1)}, u32[]{:S(2)}, u32[]{:S(2)}) collective-permute-start(bf16[32,456]{1,0:T(8,128)(2,1)S(1)} %get-tuple-element.41), channel_id=1, source_target_pairs={{0,24},{4,28},{8,16},{12,20},{16,8},{20,12},{24,0},{28,4},{1,25},{... | collective-permute-start | bytes 87560 | tf_op jit(solution)/shard_map/ppermute | solution.py:146
  8.6 7.5 %collective-permute-start.6 = (bf16[32,456]{1,0:T(8,128)(2,1)S(1)}, bf16[32,456]{1,0:T(8,128)(2,1)S(1)}, u32[]{:S(2)}, u32[]{:S(2)}) collective-permute-start(bf16[32,456]{1,0:T(8,128)(2,1)S(1)} %get-tuple-element.60), channel_id=1, source_target_pairs={{0,24},{4,28},{8,16},{12,20},{16,8},{20,12},{24,0},{28,4},{1,25},{... | collective-permute-start | bytes 87560 | tf_op jit(solution)/shard_map/ppermute | solution.py:146
  10.2 5.8 %collective-permute-start.4 = (bf16[32,456]{1,0:T(8,128)(2,1)S(1)}, bf16[32,456]{1,0:T(8,128)(2,1)S(1)}, u32[]{:S(2)}, u32[]{:S(2)}) collective-permute-start(bf16[32,456]{1,0:T(8,128)(2,1)S(1)} %get-tuple-element.61), channel_id=1, source_target_pairs={{0,16},{4,20},{8,24},{12,28},{16,0},{20,4},{24,8},{28,12},{1,17},{... | collective-permute-start | bytes 87560 | tf_op jit(solution)/shard_map/ppermute | solution.py:146
  11.5 4.6 %collective-permute-start.2 = (bf16[32,456]{1,0:T(8,128)(2,1)S(1)}, bf16[32,456]{1,0:T(8,128)(2,1)S(1)}, u32[]{:S(2)}, u32[]{:S(2)}) collective-permute-start(bf16[32,456]{1,0:T(8,128)(2,1)S(1)} %get-tuple-element.62), channel_id=1, source_target_pairs={{0,8},{4,12},{8,0},{12,4},{16,24},{20,28},{24,16},{28,20},{1,9},{5... | collective-permute-start | bytes 87560 | tf_op jit(solution)/shard_map/ppermute | solution.py:146
  19.2 5.1 %collective-permute-start.9 = (f32[2,32,128]{2,1,0:T(8,128)S(1)}, f32[2,32,128]{2,1,0:T(8,128)S(1)}, u32[]{:S(2)}, u32[]{:S(2)}) collective-permute-start(f32[2,32,128]{2,1,0:T(8,128)S(1)} %get-tuple-element.48), channel_id=1, source_target_pairs={{0,2},{1,3},{2,0},{3,1},{4,6},{5,7},{6,4},{7,5},{8,10},{9,11},{10,... | collective-permute-start | bytes 98312 | tf_op jit(solution)/shard_map/ppermute | solution.py:647
  20.8 12.3 %collective-permute-start.8 = (bf16[15,128,128]{2,1,0:T(8,128)(2,1)S(1)}, bf16[15,128,128]{2,1,0:T(8,128)(2,1)S(1)}, u32[]{:S(2)}, u32[]{:S(2)}) collective-permute-start(bf16[15,128,128]{2,1,0:T(8,128)(2,1)S(1)} %get-tuple-element.46), channel_id=1, source_target_pairs={{0,2},{1,3},{2,0},{3,1},{4,6},{5,7},{6,4},{7,5},{8,10},{9,11},{10,... | collective-permute-start | bytes 1474568 | tf_op jit(solution)/shard_map/ppermute | solution.py:648
  24.3 8.8 %slice-start = ((s8[16777216]{0:T(1024)(128)(4,1)}), s8[4194304]{0:T(1024)(128)(4,1)S(1)}, s32[]{:S(2)}) async-start(s8[16777216]{0:T(1024)(128)(4,1)} %bitcast.14), calls=%async_computation | async-start | bytes 8388608
  24.4 8.8 %slice-start.1 = ((s8[16777216]{0:T(1024)(128)(4,1)}), s8[4194304]{0:T(1024)(128)(4,1)S(1)}, s32[]{:S(2)}) async-start(s8[16777216]{0:T(1024)(128)(4,1)} %bitcast.14), calls=%async_computation.1 | async-start | bytes 8388608
  24.4 8.8 %slice-start.2 = ((s8[16777216]{0:T(1024)(128)(4,1)}), s8[4194304]{0:T(1024)(128)(4,1)S(1)}, s32[]{:S(2)}) async-start(s8[16777216]{0:T(1024)(128)(4,1)} %bitcast.14), calls=%async_computation.2 | async-start | bytes 8388608
  24.4 8.7 %slice-start.3 = ((s8[16777216]{0:T(1024)(128)(4,1)}), s8[4194304]{0:T(1024)(128)(4,1)S(1)}, s32[]{:S(2)}) async-start(s8[16777216]{0:T(1024)(128)(4,1)} %bitcast.14), calls=%async_computation.3 | async-start | bytes 8388608
  25.1 5.7 %collective-permute-start.10 = (f32[32,128]{1,0:T(8,128)S(1)}, f32[32,128]{1,0:T(8,128)S(1)}, u32[]{:S(2)}, u32[]{:S(2)}) collective-permute-start(f32[32,128]{1,0:T(8,128)S(1)} %get-tuple-element.49), channel_id=1, source_target_pairs={{0,4},{8,12},{16,20},{24,28},{4,0},{12,8},{20,16},{28,24},{1,5},{9... | collective-permute-start | bytes 49160 | tf_op jit(solution)/shard_map/ppermute | solution.py:597
  25.7 6.9 %collective-permute-start.11 = (f32[32,128]{1,0:T(8,128)S(1)}, f32[32,128]{1,0:T(8,128)S(1)}, u32[]{:S(2)}, u32[]{:S(2)}) collective-permute-start(f32[32,128]{1,0:T(8,128)S(1)} %get-tuple-element.50), channel_id=1, source_target_pairs={{4,8},{12,16},{20,24},{8,4},{16,12},{24,20},{5,9},{13,17},{21,25},... | collective-permute-start | bytes 49160 | tf_op jit(solution)/shard_map/ppermute | solution.py:597
  35.4 9.6 %collective-permute-start.12 = (f32[32,128]{1,0:T(8,128)S(1)}, f32[32,128]{1,0:T(8,128)S(1)}, u32[]{:S(2)}, u32[]{:S(2)}) collective-permute-start(f32[32,128]{1,0:T(8,128)S(1)} %get-tuple-element.56), channel_id=1, source_target_pairs={{0,4},{8,12},{16,20},{24,28},{4,0},{12,8},{20,16},{28,24},{1,5},{9... | collective-permute-start | bytes 49160 | tf_op jit(solution)/shard_map/ppermute | solution.py:597
  36.5 8.6 %collective-permute-start.13 = (f32[32,128]{1,0:T(8,128)S(1)}, f32[32,128]{1,0:T(8,128)S(1)}, u32[]{:S(2)}, u32[]{:S(2)}) collective-permute-start(f32[32,128]{1,0:T(8,128)S(1)} %get-tuple-element.57), channel_id=1, source_target_pairs={{4,8},{12,16},{20,24},{8,4},{16,12},{24,20},{5,9},{13,17},{21,25},... | collective-permute-start | bytes 49160 | tf_op jit(solution)/shard_map/ppermute | solution.py:597

commit v7 on v5

--- a/solution.py
+++ b/solution.py
@@ -103,9 +103,10 @@
     if not swaps:
         out_refs[0][...] = total
         return
-    for k, ref in enumerate(out_refs[:-1]):
-        ref[...] = total[2 * k]
-        out_refs[-1][k] = total[2 * k + 1]
+    out_refs[0][...] = total[0]
+    out_refs[1][...] = total[1]
+    for k, ref in enumerate(out_refs[2:], 1):
+        ref[...] = total[2 * k : 2 * k + 2]
     if load:
         operators_copy.wait()
 
@@ -116,7 +117,7 @@
     _, outer = handled_groups()
     block = (outer * share * capacity, width)
     if swaps:
-        shapes = [block] * (sources // 2) + [(sources // 2,) + block]
+        shapes = [block] * 2 + [(2,) + block] * (sources // 2 - 1)
     else:
         shapes = [(sources,) + block]
     return pl.pallas_call(
@@ -138,18 +139,21 @@
     )
 
 
-def swap_blocks(outgoing):
-    *keeps, send = outgoing
+def swap_mask(x, mask):
     count = lax.axis_size("box")
-
-    def swap(x, mask):
-        return lax.ppermute(x, "box", [(i, i ^ mask) for i in range(count)])
-
-    received = swap(send, 1)
-    blocks = [keeps[0], received]
-    for k in range(1, len(keeps)):
-        blocks += [swap(keeps[k], 2 * k), swap(received[k], 2 * k)]
-    return blocks
+    return lax.ppermute(x, "box", [(i, i ^ mask) for i in range(count)])
+
+
+def swap_far(outgoing):
+    return [swap_mask(pair, 2 * k) for k, pair in enumerate(outgoing[2:], 1)]
+
+
+def swap_near(outgoing, pairs, prepared):
+    blocks = [outgoing[0], swap_mask(outgoing[1], 1)]
+    for pair in pairs:
+        second, prepared = lax.optimization_barrier((pair[1], prepared))
+        blocks += [pair, swap_mask(second, 1)]
+    return blocks, prepared
 
 
 def prepare_kernel(
@@ -252,7 +256,7 @@
     else:
         sources = arrivals
         per_source, width = imported_refs[0].shape
-        pieces = [ref[0] if i == 1 else ref[...] for i, ref in enumerate(imported_refs)]
+        pieces = [ref[0] if len(ref.shape) == 3 else ref[...] for ref in imported_refs]
         flat = jnp.concatenate(pieces, axis=0)
         swapped = lax.axis_index("box")
     boxes = picks_ref.shape[0]
@@ -577,14 +581,17 @@
         *outgoing, first_ops = outgoing
         ready.append((first_ops, 0))
     if swaps:
-        imported = swap_blocks(outgoing)
+        pairs = swap_far(outgoing)
     else:
         imported = [lax.all_to_all(outgoing[0], "box", split_axis=0, concat_axis=0, tiled=True)]
 
     _, *later = lax.optimization_barrier(
         (outgoing[-1], list_slot.T, patch_points, translations)
     )
-    picks, code, lane, spans, *loaded = prepare_call(*later, load, sources * capacity, tiles)
+    prepared = list(prepare_call(*later, load, sources * capacity, tiles))
+    if swaps:
+        imported, prepared[3] = swap_near(outgoing, pairs, prepared[3])
+    picks, code, lane, spans, *loaded = prepared
     arrived = [(other, (i + 1) * local_ops) for i, other in enumerate(others)]
     pending = []
     if swaps:

time: 47.3 us -> 49.7 us (1.051)
  the two profiles are of different devices: /device:TPU:10 before, /device:TPU:0 now
where the time goes in v7:
time: 49.7 us; the launch traced here: 49.4 us
  Pallas kernels  19.7 us (40%)
  starting transfers between devices  17.7 us (36%)
  waiting for transfers between devices  11 us (22%)
  between operations  0.82 us (2%)
    ppermute x7, starting transfers between devices, swap_mask(): return lax.ppermute(x, 'box', [(i, i ^ mask) for i in range(count)])  9.53 us
    pallas_call x2, Pallas kernels, field_call(): pl.pallas_call(functools.partial(field_kernel, share, capacity, group, ar...  6.05 us
    ppermute x7, waiting for transfers between devices, swap_mask(): return lax.ppermute(x, 'box', [(i, i ^ mask) for i in range(count)])  5.92 us
    pallas_call x1, Pallas kernels, body(): pl.pallas_call(late_kernel, out_shape=[jax.ShapeDtypeStruct((share, width...  4.5 us
    ppermute x2, starting transfers between devices, swap_sides(): lax.ppermute(first, 'box', moves(0))  4.17 us
    pallas_call x1, Pallas kernels, prepare_call(): pl.pallas_call(functools.partial(prepare_kernel, slots, tiles, width, loc...  3.25 us
    ppermute x1, waiting for transfers between devices, body(): parts.append(lax.ppermute(part, 'col', moves))  2.69 us
    ppermute x2, waiting for transfers between devices, swap_sides(): lax.ppermute(first, 'box', moves(0))  2.41 us
  transfers between devices with their start and end apart: 14, of which 6 were waited for; matrix products, arithmetic and copies ran while one was open for 0% of the time, Pallas kernels for 27%

profile of v7, /device:TPU:0, one launch (start us, length us, event | category | flops | bytes accessed | tf_op | source)
XLA Modules:
  0.0 49.4 jit_solution(17682957286791833571)
XLA Ops:
  1.1 1.9 %shard_map.77 = (bf16[32,456]{1,0:T(8,128)(2,1)S(1)}, bf16[32,456]{1,0:T(8,128)(2,1)S(1)}, bf16[2,32,456]{2,1,0:T(8,128)(2,1)S(1)}, bf16[2,32,456]{2,1,0:T(8,128...) custom-call(s32[4,8]{1,0:T(4,128)} %bitcast.20, bf16[16,456,128]{2,1,0:T(8,128)(2,1)} %bitcast.17, ...), custom_call_target="tpu_custom_call" | custom-call | tf_op jit(solution)/shard_map/pallas_call | solution.py:123
  3.1 3.7 %collective-permute-start.1 = (bf16[2,32,456]{2,1,0:T(8,128)(2,1)S(1)}, bf16[2,32,456]{2,1,0:T(8,128)(2,1)S(1)}, u32[]{:S(2)}, u32[]{:S(2)}) collective-permute-start(bf16[2,32,456]{2,1,0:T(8,128)(2,1)S(1)} %get-tuple-element.38), channel_id=1, source_target_pairs={{0,16},{4,20},{8,24},{12,28},{16,0},{20,4},{24,8},{28,12},{1,17},{... | collective-permute-start | bytes 175112 | tf_op jit(solution)/shard_map/ppermute | solution.py:144
  6.7 1.5 %collective-permute-start.3 = (bf16[32,456]{1,0:T(8,128)(2,1)S(1)}, bf16[32,456]{1,0:T(8,128)(2,1)S(1)}, u32[]{:S(2)}, u32[]{:S(2)}) collective-permute-start(bf16[32,456]{1,0:T(8,128)(2,1)S(1)} %get-tuple-element.50), channel_id=1, source_target_pairs={{0,4},{4,0},{8,12},{12,8},{16,20},{20,16},{24,28},{28,24},{1,5},{5... | collective-permute-start | bytes 87560 | tf_op jit(solution)/shard_map/ppermute | solution.py:144
  8.2 1.6 %collective-permute-start.2 = (bf16[2,32,456]{2,1,0:T(8,128)(2,1)S(1)}, bf16[2,32,456]{2,1,0:T(8,128)(2,1)S(1)}, u32[]{:S(2)}, u32[]{:S(2)}) collective-permute-start(bf16[2,32,456]{2,1,0:T(8,128)(2,1)S(1)} %get-tuple-element.39), channel_id=1, source_target_pairs={{0,8},{4,12},{8,0},{12,4},{16,24},{20,28},{24,16},{28,20},{1,9},{5... | collective-permute-start | bytes 175112 | tf_op jit(solution)/shard_map/ppermute | solution.py:144
  10.0 3.2 %shard_map.78 = (bf16[128,1024]{1,0:T(8,128)(2,1)S(1)}, s32[8,1,1024]{2,1,0:T(1,128)S(1)}, s32[8,1,1024]{2,1,0:T(1,128)S(1)}, s32[16]{0:T(128)S(1)}, bf16[12,456,456]{2,1,0:T(8,128)(2,1)S(1)}) custom-call(s32[64,128]{1,0:T(8,128)} %bitcast.19, s32[8,1024]{1,0:T(8,128)} %points_hbm, bf16[16,456,456]{2,1,0:T(8,128)(2,1)} %operators_hbm.2), custom_call_target="tpu_custom_call" | custom-call | tf_op jit(solution)/shard_map/pallas_call | solution.py:211
  13.3 2.5 %collective-permute-done.refs_6_ = bf16[2,32,456]{2,1,0:T(8,128)(2,1)S(1)} collective-permute-done((bf16[2,32,456]{2,1,0:T(8,128)(2,1)S(1)}, bf16[2,32,456]{2,1,0:T(8,128)(2,1)S(1)}, u32[]{:S(2)}, u32[]{:S(2)}) %collective-permute-start) | collective-permute-done | bytes 58400 | tf_op jit(solution)/shard_map/ppermute | solution.py:144
  15.9 0.5 %collective-permute-start.6 = (bf16[32,456]{1,0:T(8,128)(2,1)S(1)}, bf16[32,456]{1,0:T(8,128)(2,1)S(1)}, u32[]{:S(2)}, u32[]{:S(2)}) collective-permute-start(bf16[32,456]{1,0:T(8,128)(2,1)S(1)} %slice_bitcast_fusion.2), channel_id=1, source_target_pairs={{0,4},{4,0},{8,12},{12,8},{16,20},{20,16},{24,28},{28,24},{1,5},{5... | collective-permute-start | bytes 87560 | tf_op jit(solution)/shard_map/ppermute | solution.py:144
  16.4 1.5 %collective-permute-start.5 = (bf16[32,456]{1,0:T(8,128)(2,1)S(1)}, bf16[32,456]{1,0:T(8,128)(2,1)S(1)}, u32[]{:S(2)}, u32[]{:S(2)}) collective-permute-start(bf16[32,456]{1,0:T(8,128)(2,1)S(1)} %slice_bitcast_fusion.1), channel_id=1, source_target_pairs={{0,4},{4,0},{8,12},{12,8},{16,20},{20,16},{24,28},{28,24},{1,5},{5... | collective-permute-start | bytes 87560 | tf_op jit(solution)/shard_map/ppermute | solution.py:144
  17.9 0.5 %collective-permute-start.4 = (bf16[32,456]{1,0:T(8,128)(2,1)S(1)}, bf16[32,456]{1,0:T(8,128)(2,1)S(1)}, u32[]{:S(2)}, u32[]{:S(2)}) collective-permute-start(bf16[32,456]{1,0:T(8,128)(2,1)S(1)} %slice_bitcast_fusion), channel_id=1, source_target_pairs={{0,4},{4,0},{8,12},{12,8},{16,20},{20,16},{24,28},{28,24},{1,5},{5... | collective-permute-start | bytes 87560 | tf_op jit(solution)/shard_map/ppermute | solution.py:144
  18.4 1.3 %collective-permute-done.6.refs_7_ = bf16[32,456]{1,0:T(8,128)(2,1)S(1)} collective-permute-done((bf16[32,456]{1,0:T(8,128)(2,1)S(1)}, bf16[32,456]{1,0:T(8,128)(2,1)S(1)}, u32[]{:S(2)}, u32[]{:S(2)}) %collective-permute-start.6) | collective-permute-done | bytes 29216 | tf_op jit(solution)/shard_map/ppermute | solution.py:144
  20.3 1.5 %collective-permute-done.4.refs_3_ = bf16[32,456]{1,0:T(8,128)(2,1)S(1)} collective-permute-done((bf16[32,456]{1,0:T(8,128)(2,1)S(1)}, bf16[32,456]{1,0:T(8,128)(2,1)S(1)}, u32[]{:S(2)}, u32[]{:S(2)}) %collective-permute-start.4) | collective-permute-done | bytes 29216 | tf_op jit(solution)/shard_map/ppermute | solution.py:144
  21.8 3.0 %shard_map.80 = (bf16[4,128,512]{2,1,0:T(8,128)(2,1)S(1)}, f32[2,32,128]{2,1,0:T(8,128)S(1)}) custom-call(bf16[32,456]{1,0:T(8,128)(2,1)S(1)} %get-tuple-element.49.refs_0_, bf16[32,456]{1,0:T(8,128)(2,1)S(1)} %collective-permute-done.3.refs_1_, bf16[2,32,456]{2,1,0:T(8,128)(2,1)S(1)} %collective-permute-done.2.refs_2_, ...), custom_call_target="tpu_custom_call" | custom-call | flops 2181562368 | bytes 4194304 | tf_op jit(solution)/shard_map/pallas_call | solution.py:304
  24.9 1.6 %collective-permute-start.9 = (f32[2,32,128]{2,1,0:T(8,128)S(1)}, f32[2,32,128]{2,1,0:T(8,128)S(1)}, u32[]{:S(2)}, u32[]{:S(2)}) collective-permute-start(f32[2,32,128]{2,1,0:T(8,128)S(1)} %get-tuple-element.60), channel_id=1, source_target_pairs={{0,2},{1,3},{2,0},{3,1},{4,6},{5,7},{6,4},{7,5},{8,10},{9,11},{10,... | collective-permute-start | bytes 98312 | tf_op jit(solution)/shard_map/ppermute | solution.py:607
  26.9 3.0 %shard_map.79 = (f32[4,128,512]{2,1,0:T(8,128)S(1)}, f32[2,32,128]{2,1,0:T(8,128)S(1)}) custom-call(bf16[32,456]{1,0:T(8,128)(2,1)S(1)} %get-tuple-element.49.refs_0_, bf16[32,456]{1,0:T(8,128)(2,1)S(1)} %collective-permute-done.3.refs_1_, bf16[2,32,456]{2,1,0:T(8,128)(2,1)S(1)} %collective-permute-done.2.refs_2_, ...), custom_call_target="tpu_custom_call" | custom-call | flops 2181562368 | bytes 4194304 | tf_op jit(solution)/shard_map/pallas_call | solution.py:304
  30.0 0.7 %shard_map.81 = (f32[32,128]{1,0:T(8,128)S(1)}, f32[32,128]{1,0:T(8,128)S(1)}, bf16[8,128,1024]{2,1,0:T(8,128)(2,1)S(1)}, bf16[8,128,1024]{2,1,0:T(8,128)(2,1)S(1)}) custom-call(s32[8,1,1024]{2,1,0:T(1,128)S(1)} %get-tuple-element.47.code_ref, s32[8,1,1024]{2,1,0:T(1,128)S(1)} %get-tuple-element.48.lane_ref, f32[2,32,128]{2,1,0:T(8,128)S(1)} %get-tuple-element.59.refs_0_, ...), custom_call_target="tpu_custom_call" | custom-call | flops 10000000000 | tf_op jit(solution)/shard_map/pallas_call | solution.py:357
  30.7 0.6 %collective-permute-start.10 = (f32[32,128]{1,0:T(8,128)S(1)}, f32[32,128]{1,0:T(8,128)S(1)}, u32[]{:S(2)}, u32[]{:S(2)}) collective-permute-start(f32[32,128]{1,0:T(8,128)S(1)} %get-tuple-element.61), channel_id=1, source_target_pairs={{0,4},{8,12},{16,20},{24,28},{4,0},{12,8},{20,16},{28,24},{1,5},{9... | collective-permute-start | bytes 49160 | tf_op jit(solution)/shard_map/ppermute | solution.py:554
  31.3 0.8 %collective-permute-start.11 = (f32[32,128]{1,0:T(8,128)S(1)}, f32[32,128]{1,0:T(8,128)S(1)}, u32[]{:S(2)}, u32[]{:S(2)}) collective-permute-start(f32[32,128]{1,0:T(8,128)S(1)} %get-tuple-element.62), channel_id=1, source_target_pairs={{4,8},{12,16},{20,24},{8,4},{16,12},{24,20},{5,9},{13,17},{21,25},... | collective-permute-start | bytes 49160 | tf_op jit(solution)/shard_map/ppermute | solution.py:554
  32.1 2.4 %collective-permute-done.10.first_ref = f32[32,128]{1,0:T(8,128)S(1)} collective-permute-done((f32[32,128]{1,0:T(8,128)S(1)}, f32[32,128]{1,0:T(8,128)S(1)}, u32[]{:S(2)}, u32[]{:S(2)}) %collective-permute-start.10) | collective-permute-done | bytes 16416 | tf_op jit(solution)/shard_map/ppermute | solution.py:554
  34.5 2.7 %collective-permute-done.8 = bf16[4,128,512]{2,1,0:T(8,128)(2,1)S(1)} collective-permute-done((bf16[4,128,512]{2,1,0:T(8,128)(2,1)S(1)}, bf16[4,128,512]{2,1,0:T(8,128)(2,1)S(1)}, u32[]{:S(2)}, u32[]{:S(2)}) %collective-permute-start.8) | collective-permute-done | bytes 524320 | tf_op jit(solution)/shard_map/ppermute | solution.py:608
  37.3 2.3 %shard_map.82 = (f32[2112,128]{1,0:T(8,128)S(1)}, f32[2112,128]{1,0:T(8,128)S(1)}, f32[32,128]{1,0:T(8,128)S(1)}, f32[32,128]{1,0:T(8,128)S(1)}) custom-call(s32[16]{0:T(128)S(1)} %get-tuple-element.46.spans_ref, s32[8,1,1024]{2,1,0:T(1,128)S(1)} %get-tuple-element.47.code_ref, s32[8,1,1024]{2,1,0:T(1,128)S(1)} %get-tuple-element.48.lane_ref, ...), custom_call_target="tpu_custom_call" | custom-call | tf_op jit(solution)/shard_map/pallas_call | solution.py:617
  39.6 3.6 %collective-permute-start.12 = (f32[32,128]{1,0:T(8,128)S(1)}, f32[32,128]{1,0:T(8,128)S(1)}, u32[]{:S(2)}, u32[]{:S(2)}) collective-permute-start(f32[32,128]{1,0:T(8,128)S(1)} %get-tuple-element.68), channel_id=1, source_target_pairs={{0,4},{8,12},{16,20},{24,28},{4,0},{12,8},{20,16},{28,24},{1,5},{9... | collective-permute-start | bytes 49160 | tf_op jit(solution)/shard_map/ppermute | solution.py:554
  43.1 0.7 %collective-permute-start.13 = (f32[32,128]{1,0:T(8,128)S(1)}, f32[32,128]{1,0:T(8,128)S(1)}, u32[]{:S(2)}, u32[]{:S(2)}) collective-permute-start(f32[32,128]{1,0:T(8,128)S(1)} %get-tuple-element.69), channel_id=1, source_target_pairs={{4,8},{12,16},{20,24},{8,4},{16,12},{24,20},{5,9},{13,17},{21,25},... | collective-permute-start | bytes 49160 | tf_op jit(solution)/shard_map/ppermute | solution.py:554
  43.8 4.5 %shard_map.83 = (bf16[4,456,128]{2,1,0:T(8,128)(2,1)}, bf16[4,456,128]{2,1,0:T(8,128)(2,1)S(1)}, f32[64,128]{1,0:T(8,128)S(1)}) custom-call(s32[16]{0:T(128)S(1)} %get-tuple-element.46.spans_ref, s32[8,1,1024]{2,1,0:T(1,128)S(1)} %get-tuple-element.47.code_ref, s32[8,1,1024]{2,1,0:T(1,128)S(1)} %get-tuple-element.48.lane_ref, ...), custom_call_target="tpu_custom_call" | custom-call | flops 67108864 | bytes 16777216 | tf_op jit(solution)/shard_map/pallas_call | solution.py:632
  48.3 1.0 %shard_map.84 = bf16[4,456,128]{2,1,0:T(8,128)(2,1)} custom-call(f32[32,128]{1,0:T(8,128)S(1)} %collective-permute-done.12.first_ref, f32[32,128]{1,0:T(8,128)S(1)} %collective-permute-done.13.second_ref, f32[64,128]{1,0:T(8,128)S(1)} %get-tuple-element.70.rows_ref, bf16[4,456,128]{2,1,0:T(8,128)(2,1)S(1)} %get-tuple-element.71.corrected_ref), custom_call_target="tpu_custom_call" | custom-call | tf_op jit(solution)/shard_map/pallas_call | solution.py:655
  (24 shorter events, 1.8 us)
Async XLA Ops:
  0.6 21.2 %collective-permute-start.7 = (bf16[16,456,456]{2,1,0:T(8,128)(2,1)}, bf16[16,456,456]{2,1,0:T(8,128)(2,1)S(1)}, u32[]{:S(2)}, u32[]{:S(2)}) collective-permute-start(bf16[16,456,456]{2,1,0:T(8,128)(2,1)} %operators_hbm.2), channel_id=1, source_target_pairs={{1,0},{0,1},{3,2},{2,3},{5,4},{4,5},{7,6},{6,7},{9,8},{8,9},{11,10... | collective-permute-start | bytes 19961864 | tf_op jit(solution)/shard_map/ppermute | solution.py:572
  3.1 10.2 %collective-permute-start.1 = (bf16[2,32,456]{2,1,0:T(8,128)(2,1)S(1)}, bf16[2,32,456]{2,1,0:T(8,128)(2,1)S(1)}, u32[]{:S(2)}, u32[]{:S(2)}) collective-permute-start(bf16[2,32,456]{2,1,0:T(8,128)(2,1)S(1)} %get-tuple-element.38), channel_id=1, source_target_pairs={{0,16},{4,20},{8,24},{12,28},{16,0},{20,4},{24,8},{28,12},{1,17},{... | collective-permute-start | bytes 175112 | tf_op jit(solution)/shard_map/ppermute | solution.py:144
  6.7 11.7 %collective-permute-start.3 = (bf16[32,456]{1,0:T(8,128)(2,1)S(1)}, bf16[32,456]{1,0:T(8,128)(2,1)S(1)}, u32[]{:S(2)}, u32[]{:S(2)}) collective-permute-start(bf16[32,456]{1,0:T(8,128)(2,1)S(1)} %get-tuple-element.50), channel_id=1, source_target_pairs={{0,4},{4,0},{8,12},{12,8},{16,20},{20,16},{24,28},{28,24},{1,5},{5... | collective-permute-start | bytes 87560 | tf_op jit(solution)/shard_map/ppermute | solution.py:144
  8.2 5.1 %collective-permute-start.2 = (bf16[2,32,456]{2,1,0:T(8,128)(2,1)S(1)}, bf16[2,32,456]{2,1,0:T(8,128)(2,1)S(1)}, u32[]{:S(2)}, u32[]{:S(2)}) collective-permute-start(bf16[2,32,456]{2,1,0:T(8,128)(2,1)S(1)} %get-tuple-element.39), channel_id=1, source_target_pairs={{0,8},{4,12},{8,0},{12,4},{16,24},{20,28},{24,16},{28,20},{1,9},{5... | collective-permute-start | bytes 175112 | tf_op jit(solution)/shard_map/ppermute | solution.py:144
  9.8 6.1 %collective-permute-start = (bf16[2,32,456]{2,1,0:T(8,128)(2,1)S(1)}, bf16[2,32,456]{2,1,0:T(8,128)(2,1)S(1)}, u32[]{:S(2)}, u32[]{:S(2)}) collective-permute-start(bf16[2,32,456]{2,1,0:T(8,128)(2,1)S(1)} %get-tuple-element.37), channel_id=1, source_target_pairs={{0,24},{4,28},{8,16},{12,20},{16,8},{20,12},{24,0},{28,4},{1,25},{... | collective-permute-start | bytes 175112 | tf_op jit(solution)/shard_map/ppermute | solution.py:144
  15.9 3.9 %collective-permute-start.6 = (bf16[32,456]{1,0:T(8,128)(2,1)S(1)}, bf16[32,456]{1,0:T(8,128)(2,1)S(1)}, u32[]{:S(2)}, u32[]{:S(2)}) collective-permute-start(bf16[32,456]{1,0:T(8,128)(2,1)S(1)} %slice_bitcast_fusion.2), channel_id=1, source_target_pairs={{0,4},{4,0},{8,12},{12,8},{16,20},{20,16},{24,28},{28,24},{1,5},{5... | collective-permute-start | bytes 87560 | tf_op jit(solution)/shard_map/ppermute | solution.py:144
  16.4 3.9 %collective-permute-start.5 = (bf16[32,456]{1,0:T(8,128)(2,1)S(1)}, bf16[32,456]{1,0:T(8,128)(2,1)S(1)}, u32[]{:S(2)}, u32[]{:S(2)}) collective-permute-start(bf16[32,456]{1,0:T(8,128)(2,1)S(1)} %slice_bitcast_fusion.1), channel_id=1, source_target_pairs={{0,4},{4,0},{8,12},{12,8},{16,20},{20,16},{24,28},{28,24},{1,5},{5... | collective-permute-start | bytes 87560 | tf_op jit(solution)/shard_map/ppermute | solution.py:144
  17.9 3.9 %collective-permute-start.4 = (bf16[32,456]{1,0:T(8,128)(2,1)S(1)}, bf16[32,456]{1,0:T(8,128)(2,1)S(1)}, u32[]{:S(2)}, u32[]{:S(2)}) collective-permute-start(bf16[32,456]{1,0:T(8,128)(2,1)S(1)} %slice_bitcast_fusion), channel_id=1, source_target_pairs={{0,4},{4,0},{8,12},{12,8},{16,20},{20,16},{24,28},{28,24},{1,5},{5... | collective-permute-start | bytes 87560 | tf_op jit(solution)/shard_map/ppermute | solution.py:144
  24.9 5.1 %collective-permute-start.9 = (f32[2,32,128]{2,1,0:T(8,128)S(1)}, f32[2,32,128]{2,1,0:T(8,128)S(1)}, u32[]{:S(2)}, u32[]{:S(2)}) collective-permute-start(f32[2,32,128]{2,1,0:T(8,128)S(1)} %get-tuple-element.60), channel_id=1, source_target_pairs={{0,2},{1,3},{2,0},{3,1},{4,6},{5,7},{6,4},{7,5},{8,10},{9,11},{10,... | collective-permute-start | bytes 98312 | tf_op jit(solution)/shard_map/ppermute | solution.py:607
  26.4 10.8 %collective-permute-start.8 = (bf16[4,128,512]{2,1,0:T(8,128)(2,1)S(1)}, bf16[4,128,512]{2,1,0:T(8,128)(2,1)S(1)}, u32[]{:S(2)}, u32[]{:S(2)}) collective-permute-start(bf16[4,128,512]{2,1,0:T(8,128)(2,1)S(1)} %get-tuple-element.58), channel_id=1, source_target_pairs={{0,2},{1,3},{2,0},{3,1},{4,6},{5,7},{6,4},{7,5},{8,10},{9,11},{10,... | collective-permute-start | bytes 1572872 | tf_op jit(solution)/shard_map/ppermute | solution.py:608
  30.0 7.2 %slice-start = ((s8[16777216]{0:T(1024)(128)(4,1)}), s8[4194304]{0:T(1024)(128)(4,1)S(1)}, s32[]{:S(2)}) async-start(s8[16777216]{0:T(1024)(128)(4,1)} %bitcast.14), calls=%async_computation | async-start | bytes 8388608
  30.0 7.2 %slice-start.1 = ((s8[16777216]{0:T(1024)(128)(4,1)}), s8[4194304]{0:T(1024)(128)(4,1)S(1)}, s32[]{:S(2)}) async-start(s8[16777216]{0:T(1024)(128)(4,1)} %bitcast.14), calls=%async_computation.1 | async-start | bytes 8388608
  30.0 7.2 %slice-start.2 = ((s8[16777216]{0:T(1024)(128)(4,1)}), s8[4194304]{0:T(1024)(128)(4,1)S(1)}, s32[]{:S(2)}) async-start(s8[16777216]{0:T(1024)(128)(4,1)} %bitcast.14), calls=%async_computation.2 | async-start | bytes 8388608
  30.0 7.2 %slice-start.3 = ((s8[16777216]{0:T(1024)(128)(4,1)}), s8[4194304]{0:T(1024)(128)(4,1)S(1)}, s32[]{:S(2)}) async-start(s8[16777216]{0:T(1024)(128)(4,1)} %bitcast.14), calls=%async_computation.3 | async-start | bytes 8388608
  30.7 3.8 %collective-permute-start.10 = (f32[32,128]{1,0:T(8,128)S(1)}, f32[32,128]{1,0:T(8,128)S(1)}, u32[]{:S(2)}, u32[]{:S(2)}) collective-permute-start(f32[32,128]{1,0:T(8,128)S(1)} %get-tuple-element.61), channel_id=1, source_target_pairs={{0,4},{8,12},{16,20},{24,28},{4,0},{12,8},{20,16},{28,24},{1,5},{9... | collective-permute-start | bytes 49160 | tf_op jit(solution)/shard_map/ppermute | solution.py:554
  31.3 3.2 %collective-permute-start.11 = (f32[32,128]{1,0:T(8,128)S(1)}, f32[32,128]{1,0:T(8,128)S(1)}, u32[]{:S(2)}, u32[]{:S(2)}) collective-permute-start(f32[32,128]{1,0:T(8,128)S(1)} %get-tuple-element.62), channel_id=1, source_target_pairs={{4,8},{12,16},{20,24},{8,4},{16,12},{24,20},{5,9},{13,17},{21,25},... | collective-permute-start | bytes 49160 | tf_op jit(solution)/shard_map/ppermute | solution.py:554
  39.6 8.7 %collective-permute-start.12 = (f32[32,128]{1,0:T(8,128)S(1)}, f32[32,128]{1,0:T(8,128)S(1)}, u32[]{:S(2)}, u32[]{:S(2)}) collective-permute-start(f32[32,128]{1,0:T(8,128)S(1)} %get-tuple-element.68), channel_id=1, source_target_pairs={{0,4},{8,12},{16,20},{24,28},{4,0},{12,8},{20,16},{28,24},{1,5},{9... | collective-permute-start | bytes 49160 | tf_op jit(solution)/shard_map/ppermute | solution.py:554
  43.1 5.2 %collective-permute-start.13 = (f32[32,128]{1,0:T(8,128)S(1)}, f32[32,128]{1,0:T(8,128)S(1)}, u32[]{:S(2)}, u32[]{:S(2)}) collective-permute-start(f32[32,128]{1,0:T(8,128)S(1)} %get-tuple-element.69), channel_id=1, source_target_pairs={{4,8},{12,16},{20,24},{8,4},{16,12},{24,20},{5,9},{13,17},{21,25},... | collective-permute-start | bytes 49160 | tf_op jit(solution)/shard_map/ppermute | solution.py:554

commit v8 on v5

--- a/solution.py
+++ b/solution.py
@@ -480,7 +480,7 @@
     reaching = order_patches(spans_ref, order_ref, boxes)
 
     begin = div(reaching + batch - 1, batch) * batch
-    for size in (2 * batch, batch):
+    for size in (3 * batch, batch):
 
         def step(i, carry, size=size, begin=begin):
             chosen = [order_ref[begin + i * size + k] for k in range(size)]

time: 47.3 us -> 46.8 us (0.989); the launches traced: 47.6 us -> 46.5 us
  starting transfers between devices: 22.1 us -> 21 us
    ppermute x2, starting transfers between devices: 10.4 us -> 9.29 us  [swap_sides(): lax.ppermute(second, 'box', moves(1))]
where the time goes in v8:
time: 46.8 us; the launch traced here: 46.5 us
  starting transfers between devices  21 us (45%)
  Pallas kernels  19.6 us (42%)
  waiting for transfers between devices  4.91 us (10%)
  between operations  1 us (2%)
    ppermute x2, starting transfers between devices, swap_sides(): lax.ppermute(second, 'box', moves(1))  9.29 us
    ppermute x7, starting transfers between devices, swap(): return lax.ppermute(x, 'box', [(i, i ^ mask) for i in range(count)])  8.28 us
    pallas_call x2, Pallas kernels, field_call(): pl.pallas_call(functools.partial(field_kernel, share, capacity, group, ar...  6.05 us
    pallas_call x1, Pallas kernels, body(): pl.pallas_call(late_kernel, out_shape=[jax.ShapeDtypeStruct((share, width...  4.36 us
    pallas_call x1, Pallas kernels, prepare_call(): pl.pallas_call(functools.partial(prepare_kernel, slots, tiles, width, loc...  3.25 us
    pallas_call x1, Pallas kernels, body(): pl.pallas_call(early_kernel, out_shape=[pltpu.VMEM((ext_rows, LANES), jnp...  2.29 us
    pallas_call x1, Pallas kernels, pick_call(): pl.pallas_call(functools.partial(pick_kernel, share, swaps, load), out_sh...  1.92 us
    ppermute x7, waiting for transfers between devices, swap(): return lax.ppermute(x, 'box', [(i, i ^ mask) for i in range(count)])  1.87 us
  transfers between devices with their start and end apart: 14, of which 3 were waited for; matrix products, arithmetic and copies ran while one was open for 0% of the time, Pallas kernels for 28%

profile of v8, /device:TPU:10, one launch (start us, length us, event | category | flops | bytes accessed | tf_op | source)
XLA Modules:
  0.0 46.5 jit_solution(3058440109231813855)
XLA Ops:
  0.6 0.1 collective-permute-start.7
  0.7 1.9 %shard_map.77 = (bf16[32,456]{1,0:T(8,128)(2,1)S(1)}, bf16[32,456]{1,0:T(8,128)(2,1)S(1)}, bf16[32,456]{1,0:T(8,128)(2,1)S(1)}, bf16[32,456]{1,0:T(8,128)(2,1)S(...) custom-call(s32[4,8]{1,0:T(4,128)} %bitcast.20, bf16[16,456,128]{2,1,0:T(8,128)(2,1)} %bitcast.17, ...), custom_call_target="tpu_custom_call" | custom-call | tf_op jit(solution)/shard_map/pallas_call | solution.py:122
  2.6 0.6 %collective-permute-start = (bf16[4,32,456]{2,1,0:T(8,128)(2,1)S(1)}, bf16[4,32,456]{2,1,0:T(8,128)(2,1)S(1)}, u32[]{:S(2)}, u32[]{:S(2)}) collective-permute-start(bf16[4,32,456]{2,1,0:T(8,128)(2,1)S(1)} %get-tuple-element.31), channel_id=1, source_target_pairs={{0,4},{4,0},{8,12},{12,8},{16,20},{20,16},{24,28},{28,24},{1,5},{5... | collective-permute-start | bytes 350216 | tf_op jit(solution)/shard_map/ppermute | solution.py:146
  3.2 3.0 %collective-permute-start.3 = (bf16[32,456]{1,0:T(8,128)(2,1)S(1)}, bf16[32,456]{1,0:T(8,128)(2,1)S(1)}, u32[]{:S(2)}, u32[]{:S(2)}) collective-permute-start(bf16[32,456]{1,0:T(8,128)(2,1)S(1)} %get-tuple-element.40), channel_id=1, source_target_pairs={{0,16},{4,20},{8,24},{12,28},{16,0},{20,4},{24,8},{28,12},{1,17},{... | collective-permute-start | bytes 87560 | tf_op jit(solution)/shard_map/ppermute | solution.py:146
  6.3 0.5 collective-permute-start.5
  6.7 1.9 %collective-permute-done.refs_1_ = bf16[4,32,456]{2,1,0:T(8,128)(2,1)S(1)} collective-permute-done((bf16[4,32,456]{2,1,0:T(8,128)(2,1)S(1)}, bf16[4,32,456]{2,1,0:T(8,128)(2,1)S(1)}, u32[]{:S(2)}, u32[]{:S(2)}) %collective-permute-start) | collective-permute-done | bytes 116768 | tf_op jit(solution)/shard_map/ppermute | solution.py:146
  8.6 1.6 %collective-permute-start.6 = (bf16[32,456]{1,0:T(8,128)(2,1)S(1)}, bf16[32,456]{1,0:T(8,128)(2,1)S(1)}, u32[]{:S(2)}, u32[]{:S(2)}) collective-permute-start(bf16[32,456]{1,0:T(8,128)(2,1)S(1)} %get-tuple-element.60), channel_id=1, source_target_pairs={{0,24},{4,28},{8,16},{12,20},{16,8},{20,12},{24,0},{28,4},{1,25},{... | collective-permute-start | bytes 87560 | tf_op jit(solution)/shard_map/ppermute | solution.py:146
  10.2 1.2 %collective-permute-start.4 = (bf16[32,456]{1,0:T(8,128)(2,1)S(1)}, bf16[32,456]{1,0:T(8,128)(2,1)S(1)}, u32[]{:S(2)}, u32[]{:S(2)}) collective-permute-start(bf16[32,456]{1,0:T(8,128)(2,1)S(1)} %get-tuple-element.61), channel_id=1, source_target_pairs={{0,16},{4,20},{8,24},{12,28},{16,0},{20,4},{24,8},{28,12},{1,17},{... | collective-permute-start | bytes 87560 | tf_op jit(solution)/shard_map/ppermute | solution.py:146
  11.5 1.3 %collective-permute-start.2 = (bf16[32,456]{1,0:T(8,128)(2,1)S(1)}, bf16[32,456]{1,0:T(8,128)(2,1)S(1)}, u32[]{:S(2)}, u32[]{:S(2)}) collective-permute-start(bf16[32,456]{1,0:T(8,128)(2,1)S(1)} %get-tuple-element.62), channel_id=1, source_target_pairs={{0,8},{4,12},{8,0},{12,4},{16,24},{20,28},{24,16},{28,20},{1,9},{5... | collective-permute-start | bytes 87560 | tf_op jit(solution)/shard_map/ppermute | solution.py:146
  12.8 3.2 %shard_map.78 = (bf16[128,1024]{1,0:T(8,128)(2,1)S(1)}, s32[8,1,1024]{2,1,0:T(1,128)S(1)}, s32[8,1,1024]{2,1,0:T(1,128)S(1)}, s32[16]{0:T(128)S(1)}, bf16[12,456,456]{2,1,0:T(8,128)(2,1)S(1)}) custom-call(s32[64,128]{1,0:T(8,128)} %bitcast.19, s32[8,1024]{1,0:T(8,128)} %points_hbm, bf16[16,456,456]{2,1,0:T(8,128)(2,1)} %operators_hbm.2), custom_call_target="tpu_custom_call" | custom-call | tf_op jit(solution)/shard_map/pallas_call | solution.py:207
  16.1 3.0 %shard_map.80 = (bf16[4,128,512]{2,1,0:T(8,128)(2,1)S(1)}, f32[2,32,128]{2,1,0:T(8,128)S(1)}) custom-call(bf16[32,456]{1,0:T(8,128)(2,1)S(1)} %get-tuple-element.38.refs_0_, bf16[4,32,456]{2,1,0:T(8,128)(2,1)S(1)} %collective-permute-done.refs_1_, bf16[32,456]{1,0:T(8,128)(2,1)S(1)} %collective-permute-done.1.refs_2_, ...), custom_call_target="tpu_custom_call" | custom-call | flops 2181562368 | bytes 4194304 | tf_op jit(solution)/shard_map/pallas_call | solution.py:300
  19.1 1.6 %collective-permute-start.9 = (f32[2,32,128]{2,1,0:T(8,128)S(1)}, f32[2,32,128]{2,1,0:T(8,128)S(1)}, u32[]{:S(2)}, u32[]{:S(2)}) collective-permute-start(f32[2,32,128]{2,1,0:T(8,128)S(1)} %get-tuple-element.48), channel_id=1, source_target_pairs={{0,2},{1,3},{2,0},{3,1},{4,6},{5,7},{6,4},{7,5},{8,10},{9,11},{10,... | collective-permute-start | bytes 98312 | tf_op jit(solution)/shard_map/ppermute | solution.py:600
  20.7 0.5 %collective-permute-start.8 = (bf16[4,128,512]{2,1,0:T(8,128)(2,1)S(1)}, bf16[4,128,512]{2,1,0:T(8,128)(2,1)S(1)}, u32[]{:S(2)}, u32[]{:S(2)}) collective-permute-start(bf16[4,128,512]{2,1,0:T(8,128)(2,1)S(1)} %get-tuple-element.46), channel_id=1, source_target_pairs={{0,2},{1,3},{2,0},{3,1},{4,6},{5,7},{6,4},{7,5},{8,10},{9,11},{10,... | collective-permute-start | bytes 1572872 | tf_op jit(solution)/shard_map/ppermute | solution.py:601
  21.2 3.0 %shard_map.79 = (f32[4,128,512]{2,1,0:T(8,128)S(1)}, f32[2,32,128]{2,1,0:T(8,128)S(1)}) custom-call(bf16[32,456]{1,0:T(8,128)(2,1)S(1)} %get-tuple-element.38.refs_0_, bf16[4,32,456]{2,1,0:T(8,128)(2,1)S(1)} %collective-permute-done.refs_1_, bf16[32,456]{1,0:T(8,128)(2,1)S(1)} %collective-permute-done.1.refs_2_, ...), custom_call_target="tpu_custom_call" | custom-call | flops 2181562368 | bytes 4194304 | tf_op jit(solution)/shard_map/pallas_call | solution.py:300
  24.3 0.7 %shard_map.81 = (f32[32,128]{1,0:T(8,128)S(1)}, f32[32,128]{1,0:T(8,128)S(1)}, bf16[8,128,1024]{2,1,0:T(8,128)(2,1)S(1)}, bf16[8,128,1024]{2,1,0:T(8,128)(2,1)S(1)}) custom-call(s32[8,1,1024]{2,1,0:T(1,128)S(1)} %get-tuple-element.36.code_ref, s32[8,1,1024]{2,1,0:T(1,128)S(1)} %get-tuple-element.37.lane_ref, f32[2,32,128]{2,1,0:T(8,128)S(1)} %get-tuple-element.47.refs_0_, ...), custom_call_target="tpu_custom_call" | custom-call | flops 10000000000 | tf_op jit(solution)/shard_map/pallas_call | solution.py:353
  25.0 0.6 %collective-permute-start.10 = (f32[32,128]{1,0:T(8,128)S(1)}, f32[32,128]{1,0:T(8,128)S(1)}, u32[]{:S(2)}, u32[]{:S(2)}) collective-permute-start(f32[32,128]{1,0:T(8,128)S(1)} %get-tuple-element.49), channel_id=1, source_target_pairs={{0,4},{8,12},{16,20},{24,28},{4,0},{12,8},{20,16},{28,24},{1,5},{9... | collective-permute-start | bytes 49160 | tf_op jit(solution)/shard_map/ppermute | solution.py:550
  25.6 5.1 %collective-permute-start.11 = (f32[32,128]{1,0:T(8,128)S(1)}, f32[32,128]{1,0:T(8,128)S(1)}, u32[]{:S(2)}, u32[]{:S(2)}) collective-permute-start(f32[32,128]{1,0:T(8,128)S(1)} %get-tuple-element.50), channel_id=1, source_target_pairs={{4,8},{12,16},{20,24},{8,4},{16,12},{24,20},{5,9},{13,17},{21,25},... | collective-permute-start | bytes 49160 | tf_op jit(solution)/shard_map/ppermute | solution.py:550
  30.7 1.8 %collective-permute-done.11.second_ref = f32[32,128]{1,0:T(8,128)S(1)} collective-permute-done((f32[32,128]{1,0:T(8,128)S(1)}, f32[32,128]{1,0:T(8,128)S(1)}, u32[]{:S(2)}, u32[]{:S(2)}) %collective-permute-start.11) | collective-permute-done | bytes 16416 | tf_op jit(solution)/shard_map/ppermute | solution.py:550
  32.5 1.2 %collective-permute-done.8 = bf16[4,128,512]{2,1,0:T(8,128)(2,1)S(1)} collective-permute-done((bf16[4,128,512]{2,1,0:T(8,128)(2,1)S(1)}, bf16[4,128,512]{2,1,0:T(8,128)(2,1)S(1)}, u32[]{:S(2)}, u32[]{:S(2)}) %collective-permute-start.8) | collective-permute-done | bytes 524320 | tf_op jit(solution)/shard_map/ppermute | solution.py:601
  33.8 2.3 %shard_map.82 = (f32[2112,128]{1,0:T(8,128)S(1)}, f32[2112,128]{1,0:T(8,128)S(1)}, f32[32,128]{1,0:T(8,128)S(1)}, f32[32,128]{1,0:T(8,128)S(1)}) custom-call(s32[16]{0:T(128)S(1)} %get-tuple-element.35.spans_ref, s32[8,1,1024]{2,1,0:T(1,128)S(1)} %get-tuple-element.36.code_ref, s32[8,1,1024]{2,1,0:T(1,128)S(1)} %get-tuple-element.37.lane_ref, ...), custom_call_target="tpu_custom_call" | custom-call | tf_op jit(solution)/shard_map/pallas_call | solution.py:610
  36.1 0.6 %collective-permute-start.12 = (f32[32,128]{1,0:T(8,128)S(1)}, f32[32,128]{1,0:T(8,128)S(1)}, u32[]{:S(2)}, u32[]{:S(2)}) collective-permute-start(f32[32,128]{1,0:T(8,128)S(1)} %get-tuple-element.56), channel_id=1, source_target_pairs={{0,4},{8,12},{16,20},{24,28},{4,0},{12,8},{20,16},{28,24},{1,5},{9... | collective-permute-start | bytes 49160 | tf_op jit(solution)/shard_map/ppermute | solution.py:550
  36.7 4.2 %collective-permute-start.13 = (f32[32,128]{1,0:T(8,128)S(1)}, f32[32,128]{1,0:T(8,128)S(1)}, u32[]{:S(2)}, u32[]{:S(2)}) collective-permute-start(f32[32,128]{1,0:T(8,128)S(1)} %get-tuple-element.57), channel_id=1, source_target_pairs={{4,8},{12,16},{20,24},{8,4},{16,12},{24,20},{5,9},{13,17},{21,25},... | collective-permute-start | bytes 49160 | tf_op jit(solution)/shard_map/ppermute | solution.py:550
  40.9 4.4 %shard_map.83 = (bf16[4,456,128]{2,1,0:T(8,128)(2,1)}, bf16[4,456,128]{2,1,0:T(8,128)(2,1)S(1)}, f32[64,128]{1,0:T(8,128)S(1)}) custom-call(s32[16]{0:T(128)S(1)} %get-tuple-element.35.spans_ref, s32[8,1,1024]{2,1,0:T(1,128)S(1)} %get-tuple-element.36.code_ref, s32[8,1,1024]{2,1,0:T(1,128)S(1)} %get-tuple-element.37.lane_ref, ...), custom_call_target="tpu_custom_call" | custom-call | flops 67108864 | bytes 16777216 | tf_op jit(solution)/shard_map/pallas_call | solution.py:625
  45.3 1.0 %shard_map.84 = bf16[4,456,128]{2,1,0:T(8,128)(2,1)} custom-call(f32[32,128]{1,0:T(8,128)S(1)} %collective-permute-done.12.first_ref, f32[32,128]{1,0:T(8,128)S(1)} %collective-permute-done.13.second_ref, f32[64,128]{1,0:T(8,128)S(1)} %get-tuple-element.58.rows_ref, bf16[4,456,128]{2,1,0:T(8,128)(2,1)S(1)} %get-tuple-element.59.corrected_ref), custom_call_target="tpu_custom_call" | custom-call | tf_op jit(solution)/shard_map/pallas_call | solution.py:648
  (22 shorter events, 0.1 us)
Async XLA Ops:
  0.6 15.5 %collective-permute-start.7 = (bf16[16,456,456]{2,1,0:T(8,128)(2,1)}, bf16[16,456,456]{2,1,0:T(8,128)(2,1)S(1)}, u32[]{:S(2)}, u32[]{:S(2)}) collective-permute-start(bf16[16,456,456]{2,1,0:T(8,128)(2,1)} %operators_hbm.2), channel_id=1, source_target_pairs={{1,0},{0,1},{3,2},{2,3},{5,4},{4,5},{7,6},{6,7},{9,8},{8,9},{11,10... | collective-permute-start | bytes 19961864 | tf_op jit(solution)/shard_map/ppermute | solution.py:568
  2.6 5.9 %collective-permute-start = (bf16[4,32,456]{2,1,0:T(8,128)(2,1)S(1)}, bf16[4,32,456]{2,1,0:T(8,128)(2,1)S(1)}, u32[]{:S(2)}, u32[]{:S(2)}) collective-permute-start(bf16[4,32,456]{2,1,0:T(8,128)(2,1)S(1)} %get-tuple-element.31), channel_id=1, source_target_pairs={{0,4},{4,0},{8,12},{12,8},{16,20},{20,16},{24,28},{28,24},{1,5},{5... | collective-permute-start | bytes 350216 | tf_op jit(solution)/shard_map/ppermute | solution.py:146
  3.2 7.0 %collective-permute-start.1 = (bf16[32,456]{1,0:T(8,128)(2,1)S(1)}, bf16[32,456]{1,0:T(8,128)(2,1)S(1)}, u32[]{:S(2)}, u32[]{:S(2)}) collective-permute-start(bf16[32,456]{1,0:T(8,128)(2,1)S(1)} %get-tuple-element.39), channel_id=1, source_target_pairs={{0,8},{4,12},{8,0},{12,4},{16,24},{20,28},{24,16},{28,20},{1,9},{5... | collective-permute-start | bytes 87560 | tf_op jit(solution)/shard_map/ppermute | solution.py:146
  3.2 8.2 %collective-permute-start.3 = (bf16[32,456]{1,0:T(8,128)(2,1)S(1)}, bf16[32,456]{1,0:T(8,128)(2,1)S(1)}, u32[]{:S(2)}, u32[]{:S(2)}) collective-permute-start(bf16[32,456]{1,0:T(8,128)(2,1)S(1)} %get-tuple-element.40), channel_id=1, source_target_pairs={{0,16},{4,20},{8,24},{12,28},{16,0},{20,4},{24,8},{28,12},{1,17},{... | collective-permute-start | bytes 87560 | tf_op jit(solution)/shard_map/ppermute | solution.py:146
  6.3 9.8 %collective-permute-start.5 = (bf16[32,456]{1,0:T(8,128)(2,1)S(1)}, bf16[32,456]{1,0:T(8,128)(2,1)S(1)}, u32[]{:S(2)}, u32[]{:S(2)}) collective-permute-start(bf16[32,456]{1,0:T(8,128)(2,1)S(1)} %get-tuple-element.41), channel_id=1, source_target_pairs={{0,24},{4,28},{8,16},{12,20},{16,8},{20,12},{24,0},{28,4},{1,25},{... | collective-permute-start | bytes 87560 | tf_op jit(solution)/shard_map/ppermute | solution.py:146
  8.6 7.5 %collective-permute-start.6 = (bf16[32,456]{1,0:T(8,128)(2,1)S(1)}, bf16[32,456]{1,0:T(8,128)(2,1)S(1)}, u32[]{:S(2)}, u32[]{:S(2)}) collective-permute-start(bf16[32,456]{1,0:T(8,128)(2,1)S(1)} %get-tuple-element.60), channel_id=1, source_target_pairs={{0,24},{4,28},{8,16},{12,20},{16,8},{20,12},{24,0},{28,4},{1,25},{... | collective-permute-start | bytes 87560 | tf_op jit(solution)/shard_map/ppermute | solution.py:146
  10.2 5.8 %collective-permute-start.4 = (bf16[32,456]{1,0:T(8,128)(2,1)S(1)}, bf16[32,456]{1,0:T(8,128)(2,1)S(1)}, u32[]{:S(2)}, u32[]{:S(2)}) collective-permute-start(bf16[32,456]{1,0:T(8,128)(2,1)S(1)} %get-tuple-element.61), channel_id=1, source_target_pairs={{0,16},{4,20},{8,24},{12,28},{16,0},{20,4},{24,8},{28,12},{1,17},{... | collective-permute-start | bytes 87560 | tf_op jit(solution)/shard_map/ppermute | solution.py:146
  11.5 4.6 %collective-permute-start.2 = (bf16[32,456]{1,0:T(8,128)(2,1)S(1)}, bf16[32,456]{1,0:T(8,128)(2,1)S(1)}, u32[]{:S(2)}, u32[]{:S(2)}) collective-permute-start(bf16[32,456]{1,0:T(8,128)(2,1)S(1)} %get-tuple-element.62), channel_id=1, source_target_pairs={{0,8},{4,12},{8,0},{12,4},{16,24},{20,28},{24,16},{28,20},{1,9},{5... | collective-permute-start | bytes 87560 | tf_op jit(solution)/shard_map/ppermute | solution.py:146
  19.1 5.1 %collective-permute-start.9 = (f32[2,32,128]{2,1,0:T(8,128)S(1)}, f32[2,32,128]{2,1,0:T(8,128)S(1)}, u32[]{:S(2)}, u32[]{:S(2)}) collective-permute-start(f32[2,32,128]{2,1,0:T(8,128)S(1)} %get-tuple-element.48), channel_id=1, source_target_pairs={{0,2},{1,3},{2,0},{3,1},{4,6},{5,7},{6,4},{7,5},{8,10},{9,11},{10,... | collective-permute-start | bytes 98312 | tf_op jit(solution)/shard_map/ppermute | solution.py:600
  20.7 13.0 %collective-permute-start.8 = (bf16[4,128,512]{2,1,0:T(8,128)(2,1)S(1)}, bf16[4,128,512]{2,1,0:T(8,128)(2,1)S(1)}, u32[]{:S(2)}, u32[]{:S(2)}) collective-permute-start(bf16[4,128,512]{2,1,0:T(8,128)(2,1)S(1)} %get-tuple-element.46), channel_id=1, source_target_pairs={{0,2},{1,3},{2,0},{3,1},{4,6},{5,7},{6,4},{7,5},{8,10},{9,11},{10,... | collective-permute-start | bytes 1572872 | tf_op jit(solution)/shard_map/ppermute | solution.py:601
  24.3 9.5 %slice-start = ((s8[16777216]{0:T(1024)(128)(4,1)}), s8[4194304]{0:T(1024)(128)(4,1)S(1)}, s32[]{:S(2)}) async-start(s8[16777216]{0:T(1024)(128)(4,1)} %bitcast.14), calls=%async_computation | async-start | bytes 8388608
  24.3 9.5 %slice-start.1 = ((s8[16777216]{0:T(1024)(128)(4,1)}), s8[4194304]{0:T(1024)(128)(4,1)S(1)}, s32[]{:S(2)}) async-start(s8[16777216]{0:T(1024)(128)(4,1)} %bitcast.14), calls=%async_computation.1 | async-start | bytes 8388608
  24.3 9.5 %slice-start.2 = ((s8[16777216]{0:T(1024)(128)(4,1)}), s8[4194304]{0:T(1024)(128)(4,1)S(1)}, s32[]{:S(2)}) async-start(s8[16777216]{0:T(1024)(128)(4,1)} %bitcast.14), calls=%async_computation.2 | async-start | bytes 8388608
  24.3 9.5 %slice-start.3 = ((s8[16777216]{0:T(1024)(128)(4,1)}), s8[4194304]{0:T(1024)(128)(4,1)S(1)}, s32[]{:S(2)}) async-start(s8[16777216]{0:T(1024)(128)(4,1)} %bitcast.14), calls=%async_computation.3 | async-start | bytes 8388608
  25.0 5.7 %collective-permute-start.10 = (f32[32,128]{1,0:T(8,128)S(1)}, f32[32,128]{1,0:T(8,128)S(1)}, u32[]{:S(2)}, u32[]{:S(2)}) collective-permute-start(f32[32,128]{1,0:T(8,128)S(1)} %get-tuple-element.49), channel_id=1, source_target_pairs={{0,4},{8,12},{16,20},{24,28},{4,0},{12,8},{20,16},{28,24},{1,5},{9... | collective-permute-start | bytes 49160 | tf_op jit(solution)/shard_map/ppermute | solution.py:550
  25.6 6.9 %collective-permute-start.11 = (f32[32,128]{1,0:T(8,128)S(1)}, f32[32,128]{1,0:T(8,128)S(1)}, u32[]{:S(2)}, u32[]{:S(2)}) collective-permute-start(f32[32,128]{1,0:T(8,128)S(1)} %get-tuple-element.50), channel_id=1, source_target_pairs={{4,8},{12,16},{20,24},{8,4},{16,12},{24,20},{5,9},{13,17},{21,25},... | collective-permute-start | bytes 49160 | tf_op jit(solution)/shard_map/ppermute | solution.py:550
  36.1 9.2 %collective-permute-start.12 = (f32[32,128]{1,0:T(8,128)S(1)}, f32[32,128]{1,0:T(8,128)S(1)}, u32[]{:S(2)}, u32[]{:S(2)}) collective-permute-start(f32[32,128]{1,0:T(8,128)S(1)} %get-tuple-element.56), channel_id=1, source_target_pairs={{0,4},{8,12},{16,20},{24,28},{4,0},{12,8},{20,16},{28,24},{1,5},{9... | collective-permute-start | bytes 49160 | tf_op jit(solution)/shard_map/ppermute | solution.py:550
  36.7 8.6 %collective-permute-start.13 = (f32[32,128]{1,0:T(8,128)S(1)}, f32[32,128]{1,0:T(8,128)S(1)}, u32[]{:S(2)}, u32[]{:S(2)}) collective-permute-start(f32[32,128]{1,0:T(8,128)S(1)} %get-tuple-element.57), channel_id=1, source_target_pairs={{4,8},{12,16},{20,24},{8,4},{16,12},{24,20},{5,9},{13,17},{21,25},... | collective-permute-start | bytes 49160 | tf_op jit(solution)/shard_map/ppermute | solution.py:550
